TPU v7x, 128 devices: a whole 4x4x4 slice. The times are simulated.
128 devices in a mesh: gx: 8 (over x, z_hi), gy: 16 (over z_lo, y, core).
Axes of the slice: x: 4, y: 4, z: 4 (z_hi: 2, z_lo: 2; z = z_hi * 2 + z_lo), core: 2. Of those that a mesh axis runs over, the one named last changes fastest.
Arguments:
- hidden: bfloat16 [8192, 5376], P('gy', 'gx'), may hold values from -6 to 6
- start: int32 [1], replicated, may hold values from 1024 to 8191
- w_query: bfloat16 [5376, 4096], P('gx', 'gy'), may hold values from -0.078125 to 0.078125
- w_key_value: bfloat16 [5376, 2, 2048], P('gx', None, 'gy'), may hold values from -0.078125 to 0.078125
- w_out: bfloat16 [4096, 5376], P('gy', 'gx'), may hold values from -4 to 4
- cache: bfloat16 [1024, 2, 2048], P(None, None, 'gy'), may hold values from -6 to 6
Outputs:
- attn_branch: bfloat16 [8192, 5376], P('gy', 'gx')
All inputs are finite; a program needn't handle non-finite values.
Results may differ from a plain program's by a relative error of at most 0.035.
Values may be sent and summed in bfloat16 or wider, within the bound.
No kernel may reach another device: no remote copies, remote signals or barrier semaphores. Data moves between devices by JAX's collectives and lax.ppermute only.
A program may use at most 192 MiB of HBM per device.

v0:
```python
import functools

import jax
import jax.numpy as jnp
import numpy as np
from jax import lax
from jax.experimental import pallas as pl
from jax.experimental.pallas import tpu as pltpu
from jax.sharding import PartitionSpec as P

HD = 128
AXES = ("gx", "gy")
MIB = 1024 * 1024

query_scale = 168.0 ** (-0.5)
norm_eps = 1e-06


def place(index):
    gx, gy = divmod(index, 16)
    x, zh = divmod(gx, 2)
    zl, rest = divmod(gy, 8)
    y, core = divmod(rest, 2)
    return x, zh, zl, y, core


def number(x, zh, zl, y, core):
    return ((x % 4) * 2 + zh) * 16 + zl * 8 + (y % 4) * 2 + core


def move(value, to):
    return lax.ppermute(value, AXES, [(i, number(*to(*place(i)))) for i in range(128)])


def shift_x(value, by):
    return move(value, lambda x, zh, zl, y, c: (x + by, zh, zl, y, c))


def shift_y(value, by):
    return move(value, lambda x, zh, zl, y, c: (x, zh, zl, y + by, c))


def swap_zh(value):
    return move(value, lambda x, zh, zl, y, c: (x, 1 - zh, zl, y, c))


def swap_zl(value):
    return move(value, lambda x, zh, zl, y, c: (x, zh, 1 - zl, y, c))


def swap_core(value):
    return move(value, lambda x, zh, zl, y, c: (x, zh, zl, y, 1 - c))


def shear_y(value):
    return move(value, lambda x, zh, zl, y, c: (x, zh, zl, y + x, c))


def turn_x(value):
    return move(value, lambda x, zh, zl, y, c: (y - x, zl, zh, y, c))


def together(*values):
    return lax.optimization_barrier(values)


OFFSETS = ((0, 0), (0, 1), (3, 0), (1, 0), (3, 1), (1, 1), (2, 0), (2, 1))


def index_of(ring, pair):
    ring, pair = lax.rem(ring + 8, 4), lax.rem(pair, 2)
    base = jnp.where(ring == 0, 0, jnp.where(ring == 3, 2, jnp.where(ring == 1, 3, 6)))
    step = jnp.where((ring == 0) | (ring == 2), 1, 2)
    return base + step * pair


def coordinates():
    gx, gy = lax.axis_index("gx"), lax.axis_index("gy")
    zl, rest = lax.div(gy, 8), lax.rem(gy, 8)
    return lax.div(gx, 2), lax.rem(gx, 2), zl, lax.div(rest, 2), lax.rem(rest, 2)


def out_slots():
    x, zh, zl, y, core = coordinates()
    return [index_of(y + d - x, zl + e + zh) for d, e in OFFSETS]


def hidden_slots():
    x, zh, zl, y, core = coordinates()
    return [index_of(2 * x + d - y, zh + e + zl) for d, e in OFFSETS]


def project_most_kernel(*refs):
    own, other, weights = refs[0:8], refs[8:16], refs[16:23]
    total, left, held_w, staged, sems = refs[23:]
    width, rows = own[0].shape
    slots = hidden_slots()
    copies = [
        pltpu.make_async_copy(block, staged.at[i], sems.at[i]) for i, block in enumerate(weights)
    ]
    for copy in copies:
        copy.start()
    total[...] = jnp.zeros_like(total)
    for i, copy in enumerate(copies):
        copy.wait()
        held_w[i] = staged[i].T
    for j in range(8):

        @pl.when(slots[j] < 7)
        def _():
            weight = held_w[slots[j]]
            for half, blocks in enumerate((own, other)):
                at = slice(half * rows, (half + 1) * rows)
                total[:, at] += jnp.dot(
                    weight, blocks[j][...], preferred_element_type=jnp.float32
                )

        @pl.when(slots[j] == 7)
        def _():
            left[:, 0:rows] = own[j][...]
            left[:, rows : 2 * rows] = other[j][...]


def turned(v, cos, sin):
    v = v * lax.rsqrt(jnp.mean(v * v, axis=0, keepdims=True) + norm_eps)
    swapped = jnp.concatenate([v[HD // 2 :], v[: HD // 2]], axis=0)
    return v * cos + swapped * sin


def places(rows):
    core = lax.rem(lax.axis_index("gy"), 2)
    for half in range(2):
        begin = pl.multiple_of((core if half == 0 else 1 - core) * rows, rows)
        yield slice(half * rows, (half + 1) * rows), pl.ds(begin, rows)


def finish(left, weight, before):
    return before + jnp.dot(weight[...].T, left[...], preferred_element_type=jnp.float32)


def project_kv_kernel(weight, q_weight, left, before, cosine, sine, kv_out):
    total = finish(left, weight, before[0 : 2 * HD, :])
    for here, at in places(left.shape[1] // 2):
        values = total[:, here].astype(jnp.bfloat16)
        key = turned(values[0:HD].astype(jnp.float32), cosine[:, at], sine[:, at])
        kv_out[0:HD, at] = key.astype(jnp.bfloat16)
        kv_out[HD : 2 * HD, at] = values[HD : 2 * HD]


def project_q_kernel(weight, kv, left, before, cosine, sine, q_out):
    total = finish(left, weight, before[2 * HD : 4 * HD, :])
    for here, at in places(left.shape[1] // 2):
        values = total[:, here].astype(jnp.bfloat16).astype(jnp.float32)
        for h in range(2):
            part = slice(h * HD, (h + 1) * HD)
            query = turned(values[part], cosine[:, at], sine[:, at]) * query_scale
            q_out[part, at] = query.astype(jnp.bfloat16)


LIGHT = pl.CostEstimate(flops=1024, bytes_accessed=1024, transcendentals=0)
ANY_SPEC = pl.BlockSpec(memory_space=pl.ANY)
VMEM_SPEC = pl.BlockSpec(memory_space=pltpu.VMEM)


def project_most(own, other, weights):
    width, rows = own[0].shape
    columns = weights[0].shape[1]
    return pl.pallas_call(
        project_most_kernel,
        out_shape=(
            jax.ShapeDtypeStruct((columns, 2 * rows), jnp.float32),
            jax.ShapeDtypeStruct((width, 2 * rows), jnp.bfloat16),
        ),
        in_specs=[VMEM_SPEC] * 16 + [ANY_SPEC] * 7,
        out_specs=(VMEM_SPEC, VMEM_SPEC),
        scratch_shapes=[
            pltpu.VMEM((7, columns, width), jnp.bfloat16),
            pltpu.VMEM((7, width, columns), jnp.bfloat16),
            pltpu.SemaphoreType.DMA((7,)),
        ],
        compiler_params=pltpu.CompilerParams(vmem_limit_bytes=26 * MIB),
        cost_estimate=pl.CostEstimate(
            flops=28 * rows * width * columns, bytes_accessed=30 * MIB, transcendentals=0
        ),
        name="project_most",
    )(*own, *other, *weights)


def project_rest(kernel, weight, after, left, total, cosine, sine):
    return pl.pallas_call(
        kernel,
        out_shape=jax.ShapeDtypeStruct((weight.shape[1], left.shape[1]), jnp.bfloat16),
        in_specs=[VMEM_SPEC, ANY_SPEC] + [VMEM_SPEC] * 4,
        out_specs=VMEM_SPEC,
        compiler_params=pltpu.CompilerParams(vmem_limit_bytes=20 * MIB),
        cost_estimate=LIGHT,
        name="project_rest",
    )(weight, after, left, total, cosine, sine)


def small_call(kernel, out_shape, *args, in_specs=None):
    return pl.pallas_call(
        kernel,
        out_shape=out_shape,
        in_specs=in_specs or [VMEM_SPEC] * len(args),
        out_specs=jax.tree.map(lambda _: VMEM_SPEC, out_shape),
        compiler_params=pltpu.CompilerParams(vmem_limit_bytes=8 * MIB),
        cost_estimate=LIGHT,
        name="small",
    )(*args)


def angles_kernel(start, frequency, cosine, sine):
    rows = cosine.shape[1]
    chip = lax.div(lax.axis_index("gy"), 2)
    column = lax.broadcasted_iota(jnp.int32, (HD // 2, rows), 1)
    positions = (start[0] + chip * rows + column).astype(jnp.float32)
    angles = positions * frequency[...]
    cos, sin = jnp.cos(angles), jnp.sin(angles)
    cosine[0 : HD // 2, :] = cos
    cosine[HD // 2 : HD, :] = cos
    sine[0 : HD // 2, :] = -sin
    sine[HD // 2 : HD, :] = sin


def angles_of(start, rows):
    frequency = 10000.0 ** (-2.0 * np.arange(HD // 2) / HD)
    frequency = jnp.asarray(np.repeat(frequency[:, None], rows, axis=1), jnp.float32)
    shape = jax.ShapeDtypeStruct((HD, rows), jnp.float32)
    specs = [pl.BlockSpec(memory_space=pltpu.SMEM), VMEM_SPEC]
    return small_call(angles_kernel, (shape, shape), start, frequency, in_specs=specs)


def beside_kernel(left, right, out):
    columns = left.shape[1]
    out[:, 0:columns] = left[...]
    out[:, columns : 2 * columns] = right[...]


def beside(left, right):
    rows, columns = left.shape
    shape = jax.ShapeDtypeStruct((rows, 2 * columns), left.dtype)
    return small_call(beside_kernel, shape, left, right)


def halves_kernel(first, second, low, high):
    columns = low.shape[1]
    low[...] = first[:, 0:columns]
    high[...] = second[:, columns : 2 * columns]


def halves(first, second):
    rows, columns = first.shape
    shape = jax.ShapeDtypeStruct((rows, columns // 2), first.dtype)
    return small_call(halves_kernel, (shape, shape), first, second)


QB = 256


def window(q_ref, kv_ref, keys, i, low):
    count = q_ref.shape[1] // QB
    first, last = (0, i + 1) if low else (i, count)
    at = pl.ds(i * QB, QB)
    query = jnp.concatenate([q_ref[0:HD, at], q_ref[HD : 2 * HD, at]], axis=1)
    total, weight = None, None
    for j in range(first, last):
        here = slice(j * QB, (j + 1) * QB)
        e = jnp.exp(jnp.dot(keys[here], query, preferred_element_type=jnp.float32))
        if j == i:
            key = lax.broadcasted_iota(jnp.int32, (QB, QB), 0)
            column = lax.broadcasted_iota(jnp.int32, (QB, QB), 1)
            keep = key <= column if low else key > column
            e = jnp.where(jnp.concatenate([keep, keep], axis=1), e, 0.0)
        w = jnp.sum(e, axis=0, keepdims=True)
        t = jnp.dot(
            kv_ref[HD : 2 * HD, here], e.astype(jnp.bfloat16), preferred_element_type=jnp.float32
        )
        total = t if total is None else total + t
        weight = w if weight is None else weight + w
    return total, weight


def own_kernel(q_ref, kv_ref, total_ref, weight_ref, keys):
    keys[...] = kv_ref[0:HD, :].T
    for i in range(q_ref.shape[1] // QB):
        total, weight = window(q_ref, kv_ref, keys, i, True)
        for h in range(2):
            part = slice(h * QB, (h + 1) * QB)
            at = pl.ds(i * QB, QB)
            total_ref[h * HD : (h + 1) * HD, at] = total[:, part]
            weight_ref[h : h + 1, at] = weight[:, part]


def before_kernel(q_ref, sent_ref, cached_ref, total_ref, weight_ref, mixed_ref, kv_ref, keys):
    chip = lax.div(lax.axis_index("gy"), 2)

    @pl.when(chip == 0)
    def _():
        kv_ref[...] = cached_ref[...]

    @pl.when(chip > 0)
    def _():
        kv_ref[...] = sent_ref[...]

    keys[...] = kv_ref[0:HD, :].T
    for i in range(q_ref.shape[1] // QB):
        total, weight = window(q_ref, kv_ref, keys, i, False)
        for h in range(2):
            part = slice(h * QB, (h + 1) * QB)
            at = pl.ds(i * QB, QB)
            row = slice(h * HD, (h + 1) * HD)
            top = total[:, part] + total_ref[row, at]
            low = weight[:, part] + weight_ref[h : h + 1, at]
            mixed_ref[row, at] = (top / low).astype(jnp.bfloat16)


def attend_own(q, kv):
    rows = q.shape[1]
    return pl.pallas_call(
        own_kernel,
        out_shape=(
            jax.ShapeDtypeStruct(q.shape, jnp.float32),
            jax.ShapeDtypeStruct((2, rows), jnp.float32),
        ),
        scratch_shapes=[pltpu.VMEM((rows, HD), jnp.bfloat16)],
        compiler_params=pltpu.CompilerParams(vmem_limit_bytes=20 * MIB),
        cost_estimate=LIGHT,
        name="attend_own",
    )(q, kv)


def attend_before(q, sent, cached, total, weight):
    rows = q.shape[1]
    return pl.pallas_call(
        before_kernel,
        out_shape=jax.ShapeDtypeStruct(q.shape, jnp.bfloat16),
        scratch_shapes=[
            pltpu.VMEM(sent.shape, jnp.bfloat16),
            pltpu.VMEM((rows, HD), jnp.bfloat16),
        ],
        compiler_params=pltpu.CompilerParams(vmem_limit_bytes=20 * MIB),
        cost_estimate=LIGHT,
        name="attend_before",
    )(q, sent, cached, total, weight)


def out_most_kernel(*refs):
    mixed, weights = refs[0:7], refs[7:15]
    total, left, held_m, held_w, sems = refs[15:]
    depth = mixed[0].shape[0]
    slots = out_slots()
    copies = []
    for i in range(8):
        to = held_w.at[:, pl.ds(pl.multiple_of(slots[i] * depth, depth), depth)]
        copies.append(pltpu.make_async_copy(weights[i], to, sems.at[8 + i]))
    for i in range(7):
        here = held_m.at[pl.ds(i * depth, depth), :]
        copies.append(pltpu.make_async_copy(mixed[i], here, sems.at[i]))
    for copy in copies:
        copy.start()
    for copy in copies:
        copy.wait()
    rows = total.shape[2]
    left[...] = held_w[:, 7 * depth : 8 * depth]
    for half in range(2):
        here = held_m[:, half * rows : (half + 1) * rows]
        total[half] = jnp.dot(
            held_w[:, 0 : 7 * depth], here, preferred_element_type=jnp.float32
        )


def out_rest_kernel(flip, left, low, high, total, out):
    core = lax.rem(lax.axis_index("gy"), 2)
    half = 1 - core if flip else core
    for side, mixed in enumerate((low, high)):

        @pl.when(half == side)
        def _():
            product = jnp.dot(left[...], mixed[...], preferred_element_type=jnp.float32)
            out[...] = (total[side] + product).astype(out.dtype)


def out_most(mixed, weights):
    width, depth = weights[0].shape
    rows = mixed[0].shape[1] // 2
    return pl.pallas_call(
        out_most_kernel,
        out_shape=(
            jax.ShapeDtypeStruct((2, width, rows), jnp.float32),
            jax.ShapeDtypeStruct((width, depth), jnp.bfloat16),
        ),
        in_specs=[ANY_SPEC] * 15,
        out_specs=(VMEM_SPEC, VMEM_SPEC),
        scratch_shapes=[
            pltpu.VMEM((7 * depth, 2 * rows), jnp.bfloat16),
            pltpu.VMEM((width, 8 * depth), jnp.bfloat16),
            pltpu.SemaphoreType.DMA((16,)),
        ],
        compiler_params=pltpu.CompilerParams(vmem_limit_bytes=20 * MIB),
        cost_estimate=LIGHT,
        name="out_most",
    )(*mixed, *weights)


def out_rest(left, low, high, total, kind, flip):
    return pl.pallas_call(
        functools.partial(out_rest_kernel, flip),
        out_shape=jax.ShapeDtypeStruct(total.shape[1:], kind),
        in_specs=[VMEM_SPEC] * 4,
        out_specs=VMEM_SPEC,
        compiler_params=pltpu.CompilerParams(vmem_limit_bytes=20 * MIB),
        cost_estimate=LIGHT,
        name="out_rest",
    )(left, low, high, total)


def shards(hidden, start, w_query, w_key_value, w_out, cache):
    rows, width = hidden.shape
    kv_weight = w_key_value.reshape(width, 2 * HD)
    kv_weight, hidden = together(kv_weight, hidden)
    block = hidden.T
    out_block = w_out.T

    moved_q, moved_kv = shear_y(w_query), shear_y(kv_weight)
    block_z = swap_zh(block)
    block_r, block_l = shift_x(block, 1), shift_x(block, -1)
    moved_q, moved_kv, block_z, block_r, block_l, out_block, cache = together(
        moved_q, moved_kv, block_z, block_r, block_l, out_block, cache
    )
    moved = beside(turn_x(moved_kv), turn_x(moved_q))
    out_z, out_r, out_l = swap_zl(out_block), shift_y(out_block, 1), shift_y(out_block, -1)
    other = [swap_core(block), swap_core(block_z)]
    cosine, sine = angles_of(start, 2 * rows)
    moved, block_z, out_z, out_r, out_l, cosine, sine, *other = together(
        moved, block_z, out_z, out_r, out_l, cosine, sine, *other
    )
    moved_z = swap_zl(moved)
    moved_r, moved_l = shift_y(moved, 1), shift_y(moved, -1)
    block_zr, block_zl = shift_x(block_z, 1), shift_x(block_z, -1)
    other += [swap_core(block_r), swap_core(block_l)]
    moved_z, moved_r, moved_l, block_zr, block_zl, block_r, *other = together(
        moved_z, moved_r, moved_l, block_zr, block_zl, block_r, *other
    )
    moved_f, moved_zl, moved_zr = shift_y(moved_r, 1), shift_y(moved_z, -1), swap_zl(moved_r)
    block_f, block_zf = shift_x(block_r, 1), shift_x(block_zl, -1)
    other += [swap_core(block_zr), swap_core(block_zl)]
    moved_f, moved_zr, moved_zl, block_f, block_zf, out_z, out_l, cache, *other = together(
        moved_f, moved_zr, moved_zl, block_f, block_zf, out_z, out_l, cache, *other
    )
    half_zl, half_zr = halves(moved_zl, moved_zr)
    last_kv, last_q = shift_y(half_zl, -1), shift_y(half_zr, 1)
    own = [block, block_z, block_r, block_l, block_zr, block_zl, block_f, block_zf]
    other += [swap_core(block_f), swap_core(block_zf)]
    pairs = []
    for gx in range(8):
        head = 8 * (gx % 2) + 2 * (gx // 2)
        pairs += [(gx * 16 + head + c, gx * 16 + c) for c in range(2)]
    cached = lax.ppermute(cache, AXES, pairs)
    total, left = project_most(own, other, [moved, moved_z, moved_r, moved_l, moved_zr, moved_zl, moved_f])
    kv = project_rest(project_kv_kernel, last_kv, last_q, left, total, cosine, sine)
    before = lax.ppermute(kv, "gy", [(i, i + 2) for i in range(14)])
    q = project_rest(project_q_kernel, last_q, kv, left, total, cosine, sine)

    kv, q, out_z, out_r, cached = together(kv, q, out_z, out_r, cached)
    cached = cached.reshape(2 * rows, 2 * HD).T
    out_zr, out_zl = shift_y(out_z, 1), shift_y(out_z, -1)
    total, weight_sum = attend_own(q, kv)
    mixed = attend_before(q, before, cached, total, weight_sum)

    mixed, out_r, out_zr, out_zl = together(mixed, out_r, out_zr, out_zl)
    mixed_z = swap_zh(mixed)
    mixed_r, mixed_l = shift_x(mixed, 1), shift_x(mixed, -1)
    out_f, out_zf = shift_y(out_r, 1), shift_y(out_zl, -1)
    mixed_z, mixed_r, mixed_l = together(mixed_z, mixed_r, mixed_l)
    mixed_f, mixed_zl, mixed_zr = shift_x(mixed_r, 1), shift_x(mixed_z, -1), swap_zh(mixed_r)
    mixed_f, mixed_zr, mixed_zl = together(mixed_f, mixed_zr, mixed_zl)
    low, high = halves(mixed_zr, mixed_zl)
    low, high = shift_x(low, 1), shift_x(high, -1)
    outs = [out_block, out_z, out_r, out_l, out_zr, out_zl, out_f, out_zf]
    gathered = [mixed, mixed_z, mixed_r, mixed_l, mixed_zr, mixed_zl, mixed_f]
    total, left = out_most(gathered, outs)
    sent = swap_core(out_rest(left, low, high, total, jnp.bfloat16, True))
    kept = out_rest(left, low, high, total, jnp.float32, False)
    return (kept + sent.astype(jnp.float32)).astype(jnp.bfloat16).T


def solution(mesh):
    return jax.shard_map(
        shards,
        mesh=mesh,
        in_specs=(
            P("gy", "gx"),
            P(),
            P("gx", "gy"),
            P("gx", None, "gy"),
            P("gy", "gx"),
            P(None, None, "gy"),
        ),
        out_specs=P("gy", "gx"),
        check_vma=False,
    )
```

profile of v0, /device:TPU:1, one launch (start us, length us, event | category | flops | bytes accessed | tf_op | source)
XLA Modules:
  0.0 181.0 jit_solution(6629180316186598830)
XLA Ops:
  1.0 4.5 %collective-permute-start.2 = (bf16[672,512]{1,0:T(8,128)(2,1)}, bf16[672,512]{1,0:T(8,128)(2,1)S(1)}, u32[]{:S(2)}, u32[]{:S(2)}) collective-permute-start(bf16[672,512]{1,0:T(8,128)(2,1)} %bitcast.16), channel_id=1, source_target_pairs={{0,16},{1,17},{2,18},{3,19},{4,20},{5,21},{6,22},{7,23},{8,24},{9,... | collective-permute-start | bytes 2064392 | tf_op jit(solution)/shard_map/ppermute | solution.py:32
  12.1 8.9 %collective-permute-done.2.refs_1_ = bf16[672,512]{1,0:T(8,128)(2,1)S(1)} collective-permute-done((bf16[672,512]{1,0:T(8,128)(2,1)}, bf16[672,512]{1,0:T(8,128)(2,1)S(1)}, u32[]{:S(2)}, u32[]{:S(2)}) %collective-permute-start.2) | collective-permute-done | bytes 688160 | tf_op jit(solution)/shard_map/ppermute | solution.py:32
  24.3 4.7 %collective-permute-start.7 = (bf16[672,256]{1,0:T(8,128)(2,1)}, bf16[672,256]{1,0:T(8,128)(2,1)S(1)}, u32[]{:S(2)}, u32[]{:S(2)}) collective-permute-start(bf16[672,256]{1,0:T(8,128)(2,1)} %bitcast.12), channel_id=1, source_target_pairs={{0,8},{1,9},{2,10},{3,11},{4,12},{5,13},{6,14},{7,15},{8,0},{9,1},... | collective-permute-start | bytes 1032200 | tf_op jit(solution)/shard_map/ppermute | solution.py:32
  29.1 2.7 %collective-permute-start.11 = (bf16[672,512]{1,0:T(8,128)(2,1)S(1)}, bf16[672,512]{1,0:T(8,128)(2,1)S(1)}, u32[]{:S(2)}, u32[]{:S(2)}) collective-permute-start(bf16[672,512]{1,0:T(8,128)(2,1)S(1)} %collective-permute-done.2.refs_1_), channel_id=1, source_target_pairs={{0,1},{1,0},{2,3},{3,2},{4,5},{5,4},{6,7},{7,6},{8,9},{9,8},{10,11... | collective-permute-start | bytes 2064392 | tf_op jit(solution)/shard_map/ppermute | solution.py:32
  32.3 9.7 %collective-permute-start.8 = (bf16[672,256]{1,0:T(8,128)(2,1)}, bf16[672,256]{1,0:T(8,128)(2,1)S(1)}, u32[]{:S(2)}, u32[]{:S(2)}) collective-permute-start(bf16[672,256]{1,0:T(8,128)(2,1)} %bitcast.13), channel_id=1, source_target_pairs={{0,2},{1,3},{2,4},{3,5},{4,6},{5,7},{6,0},{7,1},{8,10},{9,11},{10,... | collective-permute-start | bytes 1032200 | tf_op jit(solution)/shard_map/ppermute | solution.py:32
  42.0 3.9 %collective-permute-start.9 = (bf16[672,256]{1,0:T(8,128)(2,1)}, bf16[672,256]{1,0:T(8,128)(2,1)S(1)}, u32[]{:S(2)}, u32[]{:S(2)}) collective-permute-start(bf16[672,256]{1,0:T(8,128)(2,1)} %bitcast.14), channel_id=1, source_target_pairs={{0,6},{1,7},{2,0},{3,1},{4,2},{5,3},{6,4},{7,5},{8,14},{9,15},{10,... | collective-permute-start | bytes 1032200 | tf_op jit(solution)/shard_map/ppermute | solution.py:32
  48.6 2.8 %collective-permute-done.8.refs_9_ = bf16[672,256]{1,0:T(8,128)(2,1)S(1)} collective-permute-done((bf16[672,256]{1,0:T(8,128)(2,1)}, bf16[672,256]{1,0:T(8,128)(2,1)S(1)}, u32[]{:S(2)}, u32[]{:S(2)}) %collective-permute-start.8) | collective-permute-done | bytes 344096 | tf_op jit(solution)/shard_map/ppermute | solution.py:32
  59.0 6.5 %collective-permute-done.12.refs_17_ = bf16[672,512]{1,0:T(8,128)(2,1)S(1)} collective-permute-done((bf16[672,512]{1,0:T(8,128)(2,1)S(1)}, bf16[672,512]{1,0:T(8,128)(2,1)S(1)}, u32[]{:S(2)}, u32[]{:S(2)}) %collective-permute-start.12) | collective-permute-done | bytes 688160 | tf_op jit(solution)/shard_map/ppermute | solution.py:32
  65.6 3.1 %collective-permute-done.13.refs_18_ = bf16[672,512]{1,0:T(8,128)(2,1)S(1)} collective-permute-done((bf16[672,512]{1,0:T(8,128)(2,1)S(1)}, bf16[672,512]{1,0:T(8,128)(2,1)S(1)}, u32[]{:S(2)}, u32[]{:S(2)}) %collective-permute-start.13) | collective-permute-done | bytes 688160 | tf_op jit(solution)/shard_map/ppermute | solution.py:32
  70.8 2.7 %collective-permute-start.21 = (bf16[672,512]{1,0:T(8,128)(2,1)S(1)}, bf16[672,512]{1,0:T(8,128)(2,1)S(1)}, u32[]{:S(2)}, u32[]{:S(2)}) collective-permute-start(bf16[672,512]{1,0:T(8,128)(2,1)S(1)} %collective-permute-done.12.refs_17_), channel_id=1, source_target_pairs={{0,6},{1,7},{2,0},{3,1},{4,2},{5,3},{6,4},{7,5},{8,14},{9,15},{10,... | collective-permute-start | bytes 2064392 | tf_op jit(solution)/shard_map/ppermute | solution.py:32
  73.5 2.7 %collective-permute-start.23 = (bf16[672,512]{1,0:T(8,128)(2,1)S(1)}, bf16[672,512]{1,0:T(8,128)(2,1)S(1)}, u32[]{:S(2)}, u32[]{:S(2)}) collective-permute-start(bf16[672,512]{1,0:T(8,128)(2,1)S(1)} %collective-permute-done.16.refs_5_), channel_id=1, source_target_pairs={{0,96},{1,97},{2,98},{3,99},{4,100},{5,101},{6,102},{7,103},{8,104... | collective-permute-start | bytes 2064392 | tf_op jit(solution)/shard_map/ppermute | solution.py:32
  76.2 8.2 %collective-permute-done.19.refs_22_ = bf16[672,512]{1,0:T(8,128)(2,1)S(1)} collective-permute-done((bf16[672,512]{1,0:T(8,128)(2,1)S(1)}, bf16[672,512]{1,0:T(8,128)(2,1)S(1)}, u32[]{:S(2)}, u32[]{:S(2)}) %collective-permute-start.19) | collective-permute-done | bytes 688160 | tf_op jit(solution)/shard_map/ppermute | solution.py:32
  84.3 5.5 %collective-permute-start.24 = (bf16[672,512]{1,0:T(8,128)(2,1)S(1)}, bf16[672,512]{1,0:T(8,128)(2,1)S(1)}, u32[]{:S(2)}, u32[]{:S(2)}) collective-permute-start(bf16[672,512]{1,0:T(8,128)(2,1)S(1)} %collective-permute-done.15.refs_4_), channel_id=1, source_target_pairs={{0,1},{1,0},{2,3},{3,2},{4,5},{5,4},{6,7},{7,6},{8,9},{9,8},{10,11... | collective-permute-start | bytes 2064392 | tf_op jit(solution)/shard_map/ppermute | solution.py:32
  96.2 11.0 %project_most.1 = (f32[512,1024]{1,0:T(8,128)S(1)}, bf16[672,1024]{1,0:T(8,128)(2,1)S(1)}) custom-call(bf16[672,512]{1,0:T(8,128)(2,1)S(1)} %bitcast.20, bf16[672,512]{1,0:T(8,128)(2,1)S(1)} %collective-permute-done.2.refs_1_, bf16[672,512]{1,0:T(8,128)(2,1)S(1)} %collective-permute-done.3.refs_2_, bf16[672,512]{1,0:T(8,128)(2,1)S(1)} %collective-permute-done.4.refs_3_, ...), custom_call_target="tpu_custom_call" | custom-call | flops 4932501504 | bytes 31457280 | tf_op jit(solution)/shard_map/project_most/pallas_call | solution.py:168
  110.9 3.5 %collective-permute-start.33 = (bf16[672,256]{1,0:T(8,128)(2,1)S(1)}, bf16[672,256]{1,0:T(8,128)(2,1)}, u32[]{:S(2)}, u32[]{:S(2)}) collective-permute-start(bf16[672,256]{1,0:T(8,128)(2,1)S(1)} %collective-permute-done.7.refs_8_), channel_id=1, source_target_pairs={{0,6},{1,7},{2,0},{3,1},{4,2},{5,3},{6,4},{7,5},{8,14},{9,15},{10,... | collective-permute-start | bytes 1032200 | tf_op jit(solution)/shard_map/ppermute | solution.py:32
  122.7 9.0 %collective-permute-done.32.refs_11_ = bf16[672,256]{1,0:T(8,128)(2,1)} collective-permute-done((bf16[672,256]{1,0:T(8,128)(2,1)S(1)}, bf16[672,256]{1,0:T(8,128)(2,1)}, u32[]{:S(2)}, u32[]{:S(2)}) %collective-permute-start.32) | collective-permute-done | bytes 344096 | tf_op jit(solution)/shard_map/ppermute | solution.py:32
  131.8 4.6 %collective-permute-start.34 = (bf16[256,1024]{1,0:T(8,128)(2,1)S(1)}, bf16[256,1024]{1,0:T(8,128)(2,1)S(1)}, u32[]{:S(2)}, u32[]{:S(2)}) collective-permute-start(bf16[256,1024]{1,0:T(8,128)(2,1)S(1)} %attend_before.1.refs_0_), channel_id=1, source_target_pairs={{0,16},{1,17},{2,18},{3,19},{4,20},{5,21},{6,22},{7,23},{8,24},{9,... | collective-permute-start | bytes 1572872 | tf_op jit(solution)/shard_map/ppermute | solution.py:32
  136.3 2.7 %collective-permute-start.36 = (bf16[256,1024]{1,0:T(8,128)(2,1)S(1)}, bf16[256,1024]{1,0:T(8,128)(2,1)S(1)}, u32[]{:S(2)}, u32[]{:S(2)}) collective-permute-start(bf16[256,1024]{1,0:T(8,128)(2,1)S(1)} %attend_before.1.refs_0_), channel_id=1, source_target_pairs={{0,96},{1,97},{2,98},{3,99},{4,100},{5,101},{6,102},{7,103},{8,104... | collective-permute-start | bytes 1572872 | tf_op jit(solution)/shard_map/ppermute | solution.py:32
  139.0 7.4 %collective-permute-done.34.refs_1_ = bf16[256,1024]{1,0:T(8,128)(2,1)S(1)} collective-permute-done((bf16[256,1024]{1,0:T(8,128)(2,1)S(1)}, bf16[256,1024]{1,0:T(8,128)(2,1)S(1)}, u32[]{:S(2)}, u32[]{:S(2)}) %collective-permute-start.34) | collective-permute-done | bytes 524320 | tf_op jit(solution)/shard_map/ppermute | solution.py:32
  148.5 4.0 %collective-permute-done.36.refs_3_ = bf16[256,1024]{1,0:T(8,128)(2,1)S(1)} collective-permute-done((bf16[256,1024]{1,0:T(8,128)(2,1)S(1)}, bf16[256,1024]{1,0:T(8,128)(2,1)S(1)}, u32[]{:S(2)}, u32[]{:S(2)}) %collective-permute-start.36) | collective-permute-done | bytes 524320 | tf_op jit(solution)/shard_map/ppermute | solution.py:32
  155.4 2.7 %collective-permute-start.41 = (bf16[672,256]{1,0:T(8,128)(2,1)}, bf16[672,256]{1,0:T(8,128)(2,1)S(1)}, u32[]{:S(2)}, u32[]{:S(2)}) collective-permute-start(bf16[672,256]{1,0:T(8,128)(2,1)} %collective-permute-done.33.refs_12_), channel_id=1, source_target_pairs={{0,6},{1,7},{2,0},{3,1},{4,2},{5,3},{6,4},{7,5},{8,14},{9,15},{10,... | collective-permute-start | bytes 1032200 | tf_op jit(solution)/shard_map/ppermute | solution.py:32
  158.1 5.4 %collective-permute-done.37.refs_6_ = bf16[256,1024]{1,0:T(8,128)(2,1)S(1)} collective-permute-done((bf16[256,1024]{1,0:T(8,128)(2,1)S(1)}, bf16[256,1024]{1,0:T(8,128)(2,1)S(1)}, u32[]{:S(2)}, u32[]{:S(2)}) %collective-permute-start.37) | collective-permute-done | bytes 524320 | tf_op jit(solution)/shard_map/ppermute | solution.py:32
  167.2 4.2 %out_most.1 = (f32[2,672,512]{2,1,0:T(8,128)S(1)}, bf16[672,256]{1,0:T(8,128)(2,1)S(1)}) custom-call(bf16[256,1024]{1,0:T(8,128)(2,1)S(1)} %attend_before.1.refs_0_, bf16[256,1024]{1,0:T(8,128)(2,1)S(1)} %collective-permute-done.34.refs_1_, bf16[256,1024]{1,0:T(8,128)(2,1)S(1)} %collective-permute-done.35.refs_2_, ...), custom_call_target="tpu_custom_call" | custom-call | flops 1024 | bytes 1024 | tf_op jit(solution)/shard_map/out_most/pallas_call | solution.py:387
  171.7 6.5 %collective-permute-start.44 = (bf16[672,512]{1,0:T(8,128)(2,1)S(1)}, bf16[672,512]{1,0:T(8,128)(2,1)S(1)}, u32[]{:S(2)}, u32[]{:S(2)}) collective-permute-start(bf16[672,512]{1,0:T(8,128)(2,1)S(1)} %out_rest.3), channel_id=1, source_target_pairs={{0,1},{1,0},{2,3},{3,2},{4,5},{5,4},{6,7},{7,6},{8,9},{9,8},{10,11... | collective-permute-start | bytes 2064392 | tf_op jit(solution)/shard_map/ppermute | solution.py:32
  (97 shorter events, 53.4 us)
Async XLA Ops:
  1.0 19.9 %collective-permute-start.2 = (bf16[672,512]{1,0:T(8,128)(2,1)}, bf16[672,512]{1,0:T(8,128)(2,1)S(1)}, u32[]{:S(2)}, u32[]{:S(2)}) collective-permute-start(bf16[672,512]{1,0:T(8,128)(2,1)} %bitcast.16), channel_id=1, source_target_pairs={{0,16},{1,17},{2,18},{3,19},{4,20},{5,21},{6,22},{7,23},{8,24},{9,... | collective-permute-start | bytes 2064392 | tf_op jit(solution)/shard_map/ppermute | solution.py:32
  5.5 17.4 %collective-permute-start.3 = (bf16[672,512]{1,0:T(8,128)(2,1)}, bf16[672,512]{1,0:T(8,128)(2,1)S(1)}, u32[]{:S(2)}, u32[]{:S(2)}) collective-permute-start(bf16[672,512]{1,0:T(8,128)(2,1)} %bitcast.17), channel_id=1, source_target_pairs={{0,32},{1,33},{2,34},{3,35},{4,36},{5,37},{6,38},{7,39},{8,40},{9,... | collective-permute-start | bytes 2064392 | tf_op jit(solution)/shard_map/ppermute | solution.py:32
  6.7 16.2 %collective-permute-start.4 = (bf16[672,512]{1,0:T(8,128)(2,1)}, bf16[672,512]{1,0:T(8,128)(2,1)S(1)}, u32[]{:S(2)}, u32[]{:S(2)}) collective-permute-start(bf16[672,512]{1,0:T(8,128)(2,1)} %bitcast.18), channel_id=1, source_target_pairs={{0,96},{1,97},{2,98},{3,99},{4,100},{5,101},{6,102},{7,103},{8,104... | collective-permute-start | bytes 2064392 | tf_op jit(solution)/shard_map/ppermute | solution.py:32
  10.5 21.2 %collective-permute-start.10 = (bf16[672,512]{1,0:T(8,128)(2,1)}, bf16[672,512]{1,0:T(8,128)(2,1)S(1)}, u32[]{:S(2)}, u32[]{:S(2)}) collective-permute-start(bf16[672,512]{1,0:T(8,128)(2,1)} %bitcast.19), channel_id=1, source_target_pairs={{0,1},{1,0},{2,3},{3,2},{4,5},{5,4},{6,7},{7,6},{8,9},{9,8},{10,11... | collective-permute-start | bytes 2064392 | tf_op jit(solution)/shard_map/ppermute | solution.py:32
  24.3 17.7 %collective-permute-start.7 = (bf16[672,256]{1,0:T(8,128)(2,1)}, bf16[672,256]{1,0:T(8,128)(2,1)S(1)}, u32[]{:S(2)}, u32[]{:S(2)}) collective-permute-start(bf16[672,256]{1,0:T(8,128)(2,1)} %bitcast.12), channel_id=1, source_target_pairs={{0,8},{1,9},{2,10},{3,11},{4,12},{5,13},{6,14},{7,15},{8,0},{9,1},... | collective-permute-start | bytes 1032200 | tf_op jit(solution)/shard_map/ppermute | solution.py:32
  29.1 23.1 %collective-permute-start.11 = (bf16[672,512]{1,0:T(8,128)(2,1)S(1)}, bf16[672,512]{1,0:T(8,128)(2,1)S(1)}, u32[]{:S(2)}, u32[]{:S(2)}) collective-permute-start(bf16[672,512]{1,0:T(8,128)(2,1)S(1)} %collective-permute-done.2.refs_1_), channel_id=1, source_target_pairs={{0,1},{1,0},{2,3},{3,2},{4,5},{5,4},{6,7},{7,6},{8,9},{9,8},{10,11... | collective-permute-start | bytes 2064392 | tf_op jit(solution)/shard_map/ppermute | solution.py:32
  31.8 24.6 %collective-permute-start.17 = (bf16[672,512]{1,0:T(8,128)(2,1)S(1)}, bf16[672,512]{1,0:T(8,128)(2,1)S(1)}, u32[]{:S(2)}, u32[]{:S(2)}) collective-permute-start(bf16[672,512]{1,0:T(8,128)(2,1)S(1)} %collective-permute-done.3.refs_2_), channel_id=1, source_target_pairs={{0,1},{1,0},{2,3},{3,2},{4,5},{5,4},{6,7},{7,6},{8,9},{9,8},{10,11... | collective-permute-start | bytes 2064392 | tf_op jit(solution)/shard_map/ppermute | solution.py:32
  31.8 25.0 %collective-permute-start.18 = (bf16[672,512]{1,0:T(8,128)(2,1)S(1)}, bf16[672,512]{1,0:T(8,128)(2,1)S(1)}, u32[]{:S(2)}, u32[]{:S(2)}) collective-permute-start(bf16[672,512]{1,0:T(8,128)(2,1)S(1)} %collective-permute-done.4.refs_3_), channel_id=1, source_target_pairs={{0,1},{1,0},{2,3},{3,2},{4,5},{5,4},{6,7},{7,6},{8,9},{9,8},{10,11... | collective-permute-start | bytes 2064392 | tf_op jit(solution)/shard_map/ppermute | solution.py:32
  32.3 19.2 %collective-permute-start.8 = (bf16[672,256]{1,0:T(8,128)(2,1)}, bf16[672,256]{1,0:T(8,128)(2,1)S(1)}, u32[]{:S(2)}, u32[]{:S(2)}) collective-permute-start(bf16[672,256]{1,0:T(8,128)(2,1)} %bitcast.13), channel_id=1, source_target_pairs={{0,2},{1,3},{2,4},{3,5},{4,6},{5,7},{6,0},{7,1},{8,10},{9,11},{10,... | collective-permute-start | bytes 1032200 | tf_op jit(solution)/shard_map/ppermute | solution.py:32
  53.7 15.0 %collective-permute-start.13 = (bf16[672,512]{1,0:T(8,128)(2,1)S(1)}, bf16[672,512]{1,0:T(8,128)(2,1)S(1)}, u32[]{:S(2)}, u32[]{:S(2)}) collective-permute-start(bf16[672,512]{1,0:T(8,128)(2,1)S(1)} %small.4.refs_16_), channel_id=1, source_target_pairs={{0,2},{1,3},{2,4},{3,5},{4,6},{5,7},{6,0},{7,1},{8,10},{9,11},{10,... | collective-permute-start | bytes 2064392 | tf_op jit(solution)/shard_map/ppermute | solution.py:32
  54.8 13.9 %collective-permute-start.14 = (bf16[672,512]{1,0:T(8,128)(2,1)S(1)}, bf16[672,512]{1,0:T(8,128)(2,1)S(1)}, u32[]{:S(2)}, u32[]{:S(2)}) collective-permute-start(bf16[672,512]{1,0:T(8,128)(2,1)S(1)} %small.4.refs_16_), channel_id=1, source_target_pairs={{0,6},{1,7},{2,0},{3,1},{4,2},{5,3},{6,4},{7,5},{8,14},{9,15},{10,... | collective-permute-start | bytes 2064392 | tf_op jit(solution)/shard_map/ppermute | solution.py:32
  56.4 14.4 %collective-permute-start.15 = (bf16[672,512]{1,0:T(8,128)(2,1)S(1)}, bf16[672,512]{1,0:T(8,128)(2,1)S(1)}, u32[]{:S(2)}, u32[]{:S(2)}) collective-permute-start(bf16[672,512]{1,0:T(8,128)(2,1)S(1)} %collective-permute-done.2.refs_1_), channel_id=1, source_target_pairs={{0,32},{1,33},{2,34},{3,35},{4,36},{5,37},{6,38},{7,39},{8,40},{9,... | collective-permute-start | bytes 2064392 | tf_op jit(solution)/shard_map/ppermute | solution.py:32
  56.8 14.0 %collective-permute-start.16 = (bf16[672,512]{1,0:T(8,128)(2,1)S(1)}, bf16[672,512]{1,0:T(8,128)(2,1)S(1)}, u32[]{:S(2)}, u32[]{:S(2)}) collective-permute-start(bf16[672,512]{1,0:T(8,128)(2,1)S(1)} %collective-permute-done.2.refs_1_), channel_id=1, source_target_pairs={{0,96},{1,97},{2,98},{3,99},{4,100},{5,101},{6,102},{7,103},{8,104... | collective-permute-start | bytes 2064392 | tf_op jit(solution)/shard_map/ppermute | solution.py:32
  70.8 13.5 %collective-permute-start.19 = (bf16[672,512]{1,0:T(8,128)(2,1)S(1)}, bf16[672,512]{1,0:T(8,128)(2,1)S(1)}, u32[]{:S(2)}, u32[]{:S(2)}) collective-permute-start(bf16[672,512]{1,0:T(8,128)(2,1)S(1)} %collective-permute-done.13.refs_18_), channel_id=1, source_target_pairs={{0,2},{1,3},{2,4},{3,5},{4,6},{5,7},{6,0},{7,1},{8,10},{9,11},{10,... | collective-permute-start | bytes 2064392 | tf_op jit(solution)/shard_map/ppermute | solution.py:32
  70.8 19.1 %collective-permute-start.20 = (bf16[672,512]{1,0:T(8,128)(2,1)S(1)}, bf16[672,512]{1,0:T(8,128)(2,1)S(1)}, u32[]{:S(2)}, u32[]{:S(2)}) collective-permute-start(bf16[672,512]{1,0:T(8,128)(2,1)S(1)} %collective-permute-done.13.refs_18_), channel_id=1, source_target_pairs={{0,8},{1,9},{2,10},{3,11},{4,12},{5,13},{6,14},{7,15},{8,0},{9,1},... | collective-permute-start | bytes 2064392 | tf_op jit(solution)/shard_map/ppermute | solution.py:32
  70.8 19.1 %collective-permute-start.21 = (bf16[672,512]{1,0:T(8,128)(2,1)S(1)}, bf16[672,512]{1,0:T(8,128)(2,1)S(1)}, u32[]{:S(2)}, u32[]{:S(2)}) collective-permute-start(bf16[672,512]{1,0:T(8,128)(2,1)S(1)} %collective-permute-done.12.refs_17_), channel_id=1, source_target_pairs={{0,6},{1,7},{2,0},{3,1},{4,2},{5,3},{6,4},{7,5},{8,14},{9,15},{10,... | collective-permute-start | bytes 2064392 | tf_op jit(solution)/shard_map/ppermute | solution.py:32
  73.5 16.4 %collective-permute-start.22 = (bf16[672,512]{1,0:T(8,128)(2,1)S(1)}, bf16[672,512]{1,0:T(8,128)(2,1)S(1)}, u32[]{:S(2)}, u32[]{:S(2)}) collective-permute-start(bf16[672,512]{1,0:T(8,128)(2,1)S(1)} %collective-permute-done.3.refs_2_), channel_id=1, source_target_pairs={{0,32},{1,33},{2,34},{3,35},{4,36},{5,37},{6,38},{7,39},{8,40},{9,... | collective-permute-start | bytes 2064392 | tf_op jit(solution)/shard_map/ppermute | solution.py:32
  73.5 16.4 %collective-permute-start.23 = (bf16[672,512]{1,0:T(8,128)(2,1)S(1)}, bf16[672,512]{1,0:T(8,128)(2,1)S(1)}, u32[]{:S(2)}, u32[]{:S(2)}) collective-permute-start(bf16[672,512]{1,0:T(8,128)(2,1)S(1)} %collective-permute-done.16.refs_5_), channel_id=1, source_target_pairs={{0,96},{1,97},{2,98},{3,99},{4,100},{5,101},{6,102},{7,103},{8,104... | collective-permute-start | bytes 2064392 | tf_op jit(solution)/shard_map/ppermute | solution.py:32
  93.2 14.0 %collective-permute-start.26 = (bf16[672,256]{1,0:T(8,128)(2,1)S(1)}, bf16[672,256]{1,0:T(8,128)(2,1)S(1)}, u32[]{:S(2)}, u32[]{:S(2)}) collective-permute-start(bf16[672,256]{1,0:T(8,128)(2,1)S(1)} %get-tuple-element.102), channel_id=1, source_target_pairs={{0,6},{1,7},{2,0},{3,1},{4,2},{5,3},{6,4},{7,5},{8,14},{9,15},{10,... | collective-permute-start | bytes 1032200 | tf_op jit(solution)/shard_map/ppermute | solution.py:32
  94.7 16.1 %collective-permute-start.30 = (bf16[1024,2,128]{2,1,0:T(2,128)(2,1)S(1)}, bf16[1024,2,128]{2,1,0:T(2,128)(2,1)}, u32[]{:S(2)}, u32[]{:S(2)}) collective-permute-start(bf16[1024,2,128]{2,1,0:T(2,128)(2,1)S(1)} %copy-done.7), channel_id=1, source_target_pairs={{0,0},{1,1},{24,16},{25,17},{34,32},{35,33},{58,48},{59,49},{68,64... | collective-permute-start | bytes 1572872 | tf_op jit(solution)/shard_map/ppermute | solution.py:459
  110.8 21.0 %collective-permute-start.32 = (bf16[672,256]{1,0:T(8,128)(2,1)S(1)}, bf16[672,256]{1,0:T(8,128)(2,1)}, u32[]{:S(2)}, u32[]{:S(2)}) collective-permute-start(bf16[672,256]{1,0:T(8,128)(2,1)S(1)} %collective-permute-done.7.refs_8_), channel_id=1, source_target_pairs={{0,2},{1,3},{2,4},{3,5},{4,6},{5,7},{6,0},{7,1},{8,10},{9,11},{10,... | collective-permute-start | bytes 1032200 | tf_op jit(solution)/shard_map/ppermute | solution.py:32
  110.9 20.9 %collective-permute-start.33 = (bf16[672,256]{1,0:T(8,128)(2,1)S(1)}, bf16[672,256]{1,0:T(8,128)(2,1)}, u32[]{:S(2)}, u32[]{:S(2)}) collective-permute-start(bf16[672,256]{1,0:T(8,128)(2,1)S(1)} %collective-permute-done.7.refs_8_), channel_id=1, source_target_pairs={{0,6},{1,7},{2,0},{3,1},{4,2},{5,3},{6,4},{7,5},{8,14},{9,15},{10,... | collective-permute-start | bytes 1032200 | tf_op jit(solution)/shard_map/ppermute | solution.py:32
  131.8 14.6 %collective-permute-start.34 = (bf16[256,1024]{1,0:T(8,128)(2,1)S(1)}, bf16[256,1024]{1,0:T(8,128)(2,1)S(1)}, u32[]{:S(2)}, u32[]{:S(2)}) collective-permute-start(bf16[256,1024]{1,0:T(8,128)(2,1)S(1)} %attend_before.1.refs_0_), channel_id=1, source_target_pairs={{0,16},{1,17},{2,18},{3,19},{4,20},{5,21},{6,22},{7,23},{8,24},{9,... | collective-permute-start | bytes 1572872 | tf_op jit(solution)/shard_map/ppermute | solution.py:32
  136.3 16.1 %collective-permute-start.36 = (bf16[256,1024]{1,0:T(8,128)(2,1)S(1)}, bf16[256,1024]{1,0:T(8,128)(2,1)S(1)}, u32[]{:S(2)}, u32[]{:S(2)}) collective-permute-start(bf16[256,1024]{1,0:T(8,128)(2,1)S(1)} %attend_before.1.refs_0_), channel_id=1, source_target_pairs={{0,96},{1,97},{2,98},{3,99},{4,100},{5,101},{6,102},{7,103},{8,104... | collective-permute-start | bytes 1572872 | tf_op jit(solution)/shard_map/ppermute | solution.py:32
  (29 other events, 512.3 us)
where the time goes:
time: 181 us
  starting transfers between devices  82.9 us (46%)
  waiting for transfers between devices  69.8 us (39%)
  Pallas kernels  23 us (13%)
  local copies, waits for them, and re-layouts  3.32 us (2%)
    ppermute x43, starting transfers between devices, move(): lax.ppermute(value, AXES, [(i, number(*to(*place(i)))) for i in range(128)])  79.5 us
    ppermute x43, waiting for transfers between devices, move(): lax.ppermute(value, AXES, [(i, number(*to(*place(i)))) for i in range(128)])  67.3 us
    pallas_call x1, Pallas kernels, project_most(): pl.pallas_call(project_most_kernel, out_shape=(jax.ShapeDtypeStruct((colu...  11 us
    pallas_call x1, Pallas kernels, out_most(): pl.pallas_call(out_most_kernel, out_shape=(jax.ShapeDtypeStruct((2, width...  4.16 us
  transfers between devices with their start and end apart: 45, of which 18 were waited for; matrix products, arithmetic and copies ran while one was open for 1% of the time, Pallas kernels for 13%

commit v1 on v0

--- a/solution.py
+++ b/solution.py
@@ -90,35 +90,37 @@
     return [index_of(2 * x + d - y, zh + e + zl) for d, e in OFFSETS]
 
 
+def turn_kernel(*refs):
+    blocks, out = refs[:-1], refs[-1]
+    for i, block in enumerate(blocks):
+        out[i] = block[...].T
+
+
+def turn(blocks):
+    width, columns = blocks[0].shape
+    shape = jax.ShapeDtypeStruct((len(blocks), columns, width), blocks[0].dtype)
+    return small_call(turn_kernel, shape, *blocks)
+
+
 def project_most_kernel(*refs):
-    own, other, weights = refs[0:8], refs[8:16], refs[16:23]
-    total, left, held_w, staged, sems = refs[23:]
-    width, rows = own[0].shape
+    blocks, early, late, total, left = refs[0:8], refs[8], refs[9], refs[10], refs[11]
     slots = hidden_slots()
-    copies = [
-        pltpu.make_async_copy(block, staged.at[i], sems.at[i]) for i, block in enumerate(weights)
-    ]
-    for copy in copies:
-        copy.start()
     total[...] = jnp.zeros_like(total)
-    for i, copy in enumerate(copies):
-        copy.wait()
-        held_w[i] = staged[i].T
     for j in range(8):
 
-        @pl.when(slots[j] < 7)
+        @pl.when(slots[j] < 4)
         def _():
-            weight = held_w[slots[j]]
-            for half, blocks in enumerate((own, other)):
-                at = slice(half * rows, (half + 1) * rows)
-                total[:, at] += jnp.dot(
-                    weight, blocks[j][...], preferred_element_type=jnp.float32
-                )
+            weight = early[jnp.minimum(slots[j], 3)]
+            total[...] += jnp.dot(weight, blocks[j][...], preferred_element_type=jnp.float32)
+
+        @pl.when((slots[j] >= 4) & (slots[j] < 7))
+        def _():
+            weight = late[jnp.clip(slots[j] - 4, 0, 2)]
+            total[...] += jnp.dot(weight, blocks[j][...], preferred_element_type=jnp.float32)
 
         @pl.when(slots[j] == 7)
         def _():
-            left[:, 0:rows] = own[j][...]
-            left[:, rows : 2 * rows] = other[j][...]
+            left[...] = blocks[j][...]
 
 
 def turned(v, cos, sin):
@@ -129,28 +131,29 @@
 
 def places(rows):
     core = lax.rem(lax.axis_index("gy"), 2)
-    for half in range(2):
-        begin = pl.multiple_of((core if half == 0 else 1 - core) * rows, rows)
-        yield slice(half * rows, (half + 1) * rows), pl.ds(begin, rows)
-
-
-def finish(left, weight, before):
-    return before + jnp.dot(weight[...].T, left[...], preferred_element_type=jnp.float32)
-
-
-def project_kv_kernel(weight, q_weight, left, before, cosine, sine, kv_out):
-    total = finish(left, weight, before[0 : 2 * HD, :])
-    for here, at in places(left.shape[1] // 2):
-        values = total[:, here].astype(jnp.bfloat16)
+    for half in (core, 1 - core):
+        yield pl.ds(pl.multiple_of(half * rows, rows), rows)
+
+
+def project_kv_kernel(weight, q_weight, *refs):
+    (left, before), (left_other, before_other), (cosine, sine, kv_out) = refs[0:2], refs[2:4], refs[4:]
+    turned_weight = weight[...].T
+    halves = ((left, before), (left_other, before_other))
+    for (block, total), at in zip(halves, places(left.shape[1])):
+        product = jnp.dot(turned_weight, block[...], preferred_element_type=jnp.float32)
+        values = (total[0 : 2 * HD, :] + product).astype(jnp.bfloat16)
         key = turned(values[0:HD].astype(jnp.float32), cosine[:, at], sine[:, at])
         kv_out[0:HD, at] = key.astype(jnp.bfloat16)
         kv_out[HD : 2 * HD, at] = values[HD : 2 * HD]
 
 
-def project_q_kernel(weight, kv, left, before, cosine, sine, q_out):
-    total = finish(left, weight, before[2 * HD : 4 * HD, :])
-    for here, at in places(left.shape[1] // 2):
-        values = total[:, here].astype(jnp.bfloat16).astype(jnp.float32)
+def project_q_kernel(weight, kv, *refs):
+    (left, before), (left_other, before_other), (cosine, sine, q_out) = refs[0:2], refs[2:4], refs[4:]
+    turned_weight = weight[...].T
+    halves = ((left, before), (left_other, before_other))
+    for (block, total), at in zip(halves, places(left.shape[1])):
+        product = jnp.dot(turned_weight, block[...], preferred_element_type=jnp.float32)
+        values = (total[2 * HD : 4 * HD, :] + product).astype(jnp.bfloat16).astype(jnp.float32)
         for h in range(2):
             part = slice(h * HD, (h + 1) * HD)
             query = turned(values[part], cosine[:, at], sine[:, at]) * query_scale
@@ -162,40 +165,36 @@
 VMEM_SPEC = pl.BlockSpec(memory_space=pltpu.VMEM)
 
 
-def project_most(own, other, weights):
-    width, rows = own[0].shape
-    columns = weights[0].shape[1]
+def project_most(blocks, early, late):
+    width, rows = blocks[0].shape
+    columns = early.shape[1]
     return pl.pallas_call(
         project_most_kernel,
         out_shape=(
-            jax.ShapeDtypeStruct((columns, 2 * rows), jnp.float32),
-            jax.ShapeDtypeStruct((width, 2 * rows), jnp.bfloat16),
+            jax.ShapeDtypeStruct((columns, rows), jnp.float32),
+            jax.ShapeDtypeStruct((width, rows), jnp.bfloat16),
         ),
-        in_specs=[VMEM_SPEC] * 16 + [ANY_SPEC] * 7,
+        in_specs=[VMEM_SPEC] * 10,
         out_specs=(VMEM_SPEC, VMEM_SPEC),
-        scratch_shapes=[
-            pltpu.VMEM((7, columns, width), jnp.bfloat16),
-            pltpu.VMEM((7, width, columns), jnp.bfloat16),
-            pltpu.SemaphoreType.DMA((7,)),
-        ],
-        compiler_params=pltpu.CompilerParams(vmem_limit_bytes=26 * MIB),
+        compiler_params=pltpu.CompilerParams(vmem_limit_bytes=20 * MIB),
         cost_estimate=pl.CostEstimate(
-            flops=28 * rows * width * columns, bytes_accessed=30 * MIB, transcendentals=0
+            flops=14 * rows * width * columns, bytes_accessed=15 * MIB, transcendentals=0
         ),
         name="project_most",
-    )(*own, *other, *weights)
-
-
-def project_rest(kernel, weight, after, left, total, cosine, sine):
+    )(*blocks, early, late)
+
+
+def project_rest(kernel, weight, after, most, most_other, cosine, sine):
+    (total, left), (total_other, left_other) = most, most_other
     return pl.pallas_call(
         kernel,
-        out_shape=jax.ShapeDtypeStruct((weight.shape[1], left.shape[1]), jnp.bfloat16),
-        in_specs=[VMEM_SPEC, ANY_SPEC] + [VMEM_SPEC] * 4,
+        out_shape=jax.ShapeDtypeStruct((weight.shape[1], 2 * left.shape[1]), jnp.bfloat16),
+        in_specs=[VMEM_SPEC, ANY_SPEC] + [VMEM_SPEC] * 6,
         out_specs=VMEM_SPEC,
-        compiler_params=pltpu.CompilerParams(vmem_limit_bytes=20 * MIB),
+        compiler_params=pltpu.CompilerParams(vmem_limit_bytes=16 * MIB),
         cost_estimate=LIGHT,
         name="project_rest",
-    )(weight, after, left, total, cosine, sine)
+    )(weight, after, left, total, left_other, total_other, cosine, sine)
 
 
 def small_call(kernel, out_shape, *args, in_specs=None):
@@ -428,53 +427,54 @@
     moved_q, moved_kv, block_z, block_r, block_l, out_block, cache = together(
         moved_q, moved_kv, block_z, block_r, block_l, out_block, cache
     )
-    moved = beside(turn_x(moved_kv), turn_x(moved_q))
-    out_z, out_r, out_l = swap_zl(out_block), shift_y(out_block, 1), shift_y(out_block, -1)
-    other = [swap_core(block), swap_core(block_z)]
+    moved = turn_x(beside(moved_kv, moved_q))
+    out_r, out_l = shift_y(out_block, 1), shift_y(out_block, -1)
+    other = [swap_core(block), swap_core(block_z), swap_core(block_r)]
     cosine, sine = angles_of(start, 2 * rows)
-    moved, block_z, out_z, out_r, out_l, cosine, sine, *other = together(
-        moved, block_z, out_z, out_r, out_l, cosine, sine, *other
+    moved, block_z, block_r, block_l, out_r, out_l, cosine, sine, *other = together(
+        moved, block_z, block_r, block_l, out_r, out_l, cosine, sine, *other
     )
     moved_z = swap_zl(moved)
     moved_r, moved_l = shift_y(moved, 1), shift_y(moved, -1)
     block_zr, block_zl = shift_x(block_z, 1), shift_x(block_z, -1)
-    other += [swap_core(block_r), swap_core(block_l)]
-    moved_z, moved_r, moved_l, block_zr, block_zl, block_r, *other = together(
-        moved_z, moved_r, moved_l, block_zr, block_zl, block_r, *other
+    moved_z, moved_r, moved_l, block_zr, block_zl, block_r, block_l = together(
+        moved_z, moved_r, moved_l, block_zr, block_zl, block_r, block_l
     )
     moved_f, moved_zl, moved_zr = shift_y(moved_r, 1), shift_y(moved_z, -1), swap_zl(moved_r)
     block_f, block_zf = shift_x(block_r, 1), shift_x(block_zl, -1)
-    other += [swap_core(block_zr), swap_core(block_zl)]
-    moved_f, moved_zr, moved_zl, block_f, block_zf, out_z, out_l, cache, *other = together(
-        moved_f, moved_zr, moved_zl, block_f, block_zf, out_z, out_l, cache, *other
+    early = turn([moved, moved_z, moved_r, moved_l])
+    moved_f, moved_zr, moved_zl, block_f, block_zf, cache, early = together(
+        moved_f, moved_zr, moved_zl, block_f, block_zf, cache, early
     )
     half_zl, half_zr = halves(moved_zl, moved_zr)
     last_kv, last_q = shift_y(half_zl, -1), shift_y(half_zr, 1)
+    late = turn([moved_zr, moved_zl, moved_f])
     own = [block, block_z, block_r, block_l, block_zr, block_zl, block_f, block_zf]
-    other += [swap_core(block_f), swap_core(block_zf)]
+    other += [swap_core(b) for b in (block_l, block_zr, block_zl, block_f, block_zf)]
     pairs = []
     for gx in range(8):
         head = 8 * (gx % 2) + 2 * (gx // 2)
         pairs += [(gx * 16 + head + c, gx * 16 + c) for c in range(2)]
     cached = lax.ppermute(cache, AXES, pairs)
-    total, left = project_most(own, other, [moved, moved_z, moved_r, moved_l, moved_zr, moved_zl, moved_f])
-    kv = project_rest(project_kv_kernel, last_kv, last_q, left, total, cosine, sine)
+    most = project_most(own, early, late)
+    most_other = project_most(other, early, late)
+    kv = project_rest(project_kv_kernel, last_kv, last_q, most, most_other, cosine, sine)
     before = lax.ppermute(kv, "gy", [(i, i + 2) for i in range(14)])
-    q = project_rest(project_q_kernel, last_q, kv, left, total, cosine, sine)
-
-    kv, q, out_z, out_r, cached = together(kv, q, out_z, out_r, cached)
+    q = project_rest(project_q_kernel, last_q, kv, most, most_other, cosine, sine)
+
+    kv, q, out_block, out_r, out_l, cached = together(kv, q, out_block, out_r, out_l, cached)
     cached = cached.reshape(2 * rows, 2 * HD).T
-    out_zr, out_zl = shift_y(out_z, 1), shift_y(out_z, -1)
+    out_z, out_f = swap_zl(out_block), shift_y(out_l, -1)
     total, weight_sum = attend_own(q, kv)
     mixed = attend_before(q, before, cached, total, weight_sum)
 
-    mixed, out_r, out_zr, out_zl = together(mixed, out_r, out_zr, out_zl)
     mixed_z = swap_zh(mixed)
     mixed_r, mixed_l = shift_x(mixed, 1), shift_x(mixed, -1)
-    out_f, out_zf = shift_y(out_r, 1), shift_y(out_zl, -1)
-    mixed_z, mixed_r, mixed_l = together(mixed_z, mixed_r, mixed_l)
+    out_zr, out_zl = shift_y(out_z, 1), shift_y(out_z, -1)
+    mixed_z, mixed_r, mixed_l, out_zr, out_zl = together(mixed_z, mixed_r, mixed_l, out_zr, out_zl)
     mixed_f, mixed_zl, mixed_zr = shift_x(mixed_r, 1), shift_x(mixed_z, -1), swap_zh(mixed_r)
-    mixed_f, mixed_zr, mixed_zl = together(mixed_f, mixed_zr, mixed_zl)
+    out_zf = shift_y(out_zl, -1)
+    mixed_f, mixed_zr, mixed_zl, out_zf = together(mixed_f, mixed_zr, mixed_zl, out_zf)
     low, high = halves(mixed_zr, mixed_zl)
     low, high = shift_x(low, 1), shift_x(high, -1)
     outs = [out_block, out_z, out_r, out_l, out_zr, out_zl, out_f, out_zf]

time: 181 us -> 168 us (0.928)
  the two profiles are of different devices: /device:TPU:1 before, /device:TPU:39 now
where the time goes in v1:
time: 168 us; the launch traced here: 165 us
  waiting for transfers between devices  69.7 us (41%)
  starting transfers between devices  69.2 us (41%)
  Pallas kernels  21.7 us (13%)
  local copies, waits for them, and re-layouts  2.44 us (1%)
    ppermute x42, starting transfers between devices, move(): lax.ppermute(value, AXES, [(i, number(*to(*place(i)))) for i in range(128)])  66.6 us
    ppermute x42, waiting for transfers between devices, move(): lax.ppermute(value, AXES, [(i, number(*to(*place(i)))) for i in range(128)])  62.3 us
    pallas_call x2, Pallas kernels, project_most(): pl.pallas_call(project_most_kernel, out_shape=(jax.ShapeDtypeStruct((colu...  8.54 us
    ppermute x1, waiting for transfers between devices, shards(): before = lax.ppermute(kv, 'gy', [(i, i + 2) for i in range(14)])  7.44 us
    pallas_call x1, Pallas kernels, out_most(): pl.pallas_call(out_most_kernel, out_shape=(jax.ShapeDtypeStruct((2, width...  3.87 us
  transfers between devices with their start and end apart: 44, of which 19 were waited for; matrix products, arithmetic and copies ran while one was open for 1% of the time, Pallas kernels for 13%

profile of v1, /device:TPU:39, one launch (start us, length us, event | category | flops | bytes accessed | tf_op | source)
XLA Modules:
  0.0 165.2 jit_solution(10531394783072334041)
XLA Ops:
  1.1 2.8 %collective-permute-start.2 = (bf16[672,512]{1,0:T(8,128)(2,1)}, bf16[672,512]{1,0:T(8,128)(2,1)S(1)}, u32[]{:S(2)}, u32[]{:S(2)}) collective-permute-start(bf16[672,512]{1,0:T(8,128)(2,1)} %bitcast.12), channel_id=1, source_target_pairs={{0,16},{1,17},{2,18},{3,19},{4,20},{5,21},{6,22},{7,23},{8,24},{9,... | collective-permute-start | bytes 2064392 | tf_op jit(solution)/shard_map/ppermute | solution.py:32
  5.3 4.6 %collective-permute-start = (bf16[672,256]{1,0:T(8,128)(2,1)}, bf16[672,256]{1,0:T(8,128)(2,1)S(1)}, u32[]{:S(2)}, u32[]{:S(2)}) collective-permute-start(bf16[672,256]{1,0:T(8,128)(2,1)} %param.9), channel_id=1, source_target_pairs={{0,0},{1,1},{2,2},{3,3},{4,4},{5,5},{6,6},{7,7},{8,8},{9,9},{10,10... | collective-permute-start | bytes 1032200 | tf_op jit(solution)/shard_map/ppermute | solution.py:32
  12.4 3.7 %collective-permute-done.right = bf16[672,256]{1,0:T(8,128)(2,1)S(1)} collective-permute-done((bf16[672,256]{1,0:T(8,128)(2,1)}, bf16[672,256]{1,0:T(8,128)(2,1)S(1)}, u32[]{:S(2)}, u32[]{:S(2)}) %collective-permute-start) | collective-permute-done | bytes 344096 | tf_op jit(solution)/shard_map/ppermute | solution.py:32
  16.1 4.5 %collective-permute-start.8 = (bf16[672,512]{1,0:T(8,128)(2,1)}, bf16[672,512]{1,0:T(8,128)(2,1)S(1)}, u32[]{:S(2)}, u32[]{:S(2)}) collective-permute-start(bf16[672,512]{1,0:T(8,128)(2,1)} %bitcast.15), channel_id=1, source_target_pairs={{0,1},{1,0},{2,3},{3,2},{4,5},{5,4},{6,7},{7,6},{8,9},{9,8},{10,11... | collective-permute-start | bytes 2064392 | tf_op jit(solution)/shard_map/ppermute | solution.py:32
  20.6 2.8 %collective-permute-done.1.left = bf16[672,256]{1,0:T(8,128)(2,1)S(1)} collective-permute-done((bf16[672,256]{1,0:T(8,128)(2,1)S(1)}, bf16[672,256]{1,0:T(8,128)(2,1)S(1)}, u32[]{:S(2)}, u32[]{:S(2)}) %collective-permute-start.1) | collective-permute-done | bytes 344096 | tf_op jit(solution)/shard_map/ppermute | solution.py:32
  23.4 2.9 %collective-permute-start.5 = (bf16[672,512]{1,0:T(8,128)(2,1)S(1)}, bf16[672,512]{1,0:T(8,128)(2,1)S(1)}, u32[]{:S(2)}, u32[]{:S(2)}) collective-permute-start(bf16[672,512]{1,0:T(8,128)(2,1)S(1)} %small.6), channel_id=1, source_target_pairs={{0,0},{1,1},{2,34},{3,35},{4,68},{5,69},{6,102},{7,103},{8,16},{9,... | collective-permute-start | bytes 2064392 | tf_op jit(solution)/shard_map/ppermute | solution.py:32
  33.2 6.1 %collective-permute-done.6.refs_9_ = bf16[672,256]{1,0:T(8,128)(2,1)S(1)} collective-permute-done((bf16[672,256]{1,0:T(8,128)(2,1)S(1)}, bf16[672,256]{1,0:T(8,128)(2,1)S(1)}, u32[]{:S(2)}, u32[]{:S(2)}) %collective-permute-start.6) | collective-permute-done | bytes 344096 | tf_op jit(solution)/shard_map/ppermute | solution.py:32
  39.3 2.9 %collective-permute-done.5.refs_0_ = bf16[672,512]{1,0:T(8,128)(2,1)S(1)} collective-permute-done((bf16[672,512]{1,0:T(8,128)(2,1)S(1)}, bf16[672,512]{1,0:T(8,128)(2,1)S(1)}, u32[]{:S(2)}, u32[]{:S(2)}) %collective-permute-start.5) | collective-permute-done | bytes 688160 | tf_op jit(solution)/shard_map/ppermute | solution.py:32
  42.3 3.2 %collective-permute-start.13 = (bf16[672,512]{1,0:T(8,128)(2,1)S(1)}, bf16[672,512]{1,0:T(8,128)(2,1)S(1)}, u32[]{:S(2)}, u32[]{:S(2)}) collective-permute-start(bf16[672,512]{1,0:T(8,128)(2,1)S(1)} %collective-permute-done.5.refs_0_), channel_id=1, source_target_pairs={{0,6},{1,7},{2,0},{3,1},{4,2},{5,3},{6,4},{7,5},{8,14},{9,15},{10,... | collective-permute-start | bytes 2064392 | tf_op jit(solution)/shard_map/ppermute | solution.py:32
  47.0 8.8 %collective-permute-done.11.refs_1_ = bf16[672,512]{1,0:T(8,128)(2,1)S(1)} collective-permute-done((bf16[672,512]{1,0:T(8,128)(2,1)S(1)}, bf16[672,512]{1,0:T(8,128)(2,1)S(1)}, u32[]{:S(2)}, u32[]{:S(2)}) %collective-permute-start.11) | collective-permute-done | bytes 688160 | tf_op jit(solution)/shard_map/ppermute | solution.py:32
  61.1 2.7 %collective-permute-start.18 = (bf16[672,512]{1,0:T(8,128)(2,1)S(1)}, bf16[672,512]{1,0:T(8,128)(2,1)S(1)}, u32[]{:S(2)}, u32[]{:S(2)}) collective-permute-start(bf16[672,512]{1,0:T(8,128)(2,1)S(1)} %collective-permute-done.11.refs_1_), channel_id=1, source_target_pairs={{0,6},{1,7},{2,0},{3,1},{4,2},{5,3},{6,4},{7,5},{8,14},{9,15},{10,... | collective-permute-start | bytes 2064392 | tf_op jit(solution)/shard_map/ppermute | solution.py:32
  65.2 9.5 %collective-permute-done.16.refs_2_ = bf16[672,512]{1,0:T(8,128)(2,1)S(1)} collective-permute-done((bf16[672,512]{1,0:T(8,128)(2,1)S(1)}, bf16[672,512]{1,0:T(8,128)(2,1)S(1)}, u32[]{:S(2)}, u32[]{:S(2)}) %collective-permute-start.16) | collective-permute-done | bytes 688160 | tf_op jit(solution)/shard_map/ppermute | solution.py:32
  74.7 5.2 %collective-permute-start.23 = (bf16[672,512]{1,0:T(8,128)(2,1)S(1)}, bf16[672,512]{1,0:T(8,128)(2,1)S(1)}, u32[]{:S(2)}, u32[]{:S(2)}) collective-permute-start(bf16[672,512]{1,0:T(8,128)(2,1)S(1)} %collective-permute-done.4.refs_3_), channel_id=1, source_target_pairs={{0,1},{1,0},{2,3},{3,2},{4,5},{5,4},{6,7},{7,6},{8,9},{9,8},{10,11... | collective-permute-start | bytes 2064392 | tf_op jit(solution)/shard_map/ppermute | solution.py:32
  85.4 4.4 %project_most.2 = (f32[512,512]{1,0:T(8,128)S(1)}, bf16[672,512]{1,0:T(8,128)(2,1)S(1)}) custom-call(bf16[672,512]{1,0:T(8,128)(2,1)S(1)} %bitcast.16, bf16[672,512]{1,0:T(8,128)(2,1)S(1)} %collective-permute-done.2.refs_1_, bf16[672,512]{1,0:T(8,128)(2,1)S(1)} %collective-permute-done.3.refs_2_, bf16[672,512]{1,0:T(8,128)(2,1)S(1)} %collective-permute-done.4.refs_3_, ...), custom_call_target="tpu_custom_call" | custom-call | flops 2466250752 | bytes 15728640 | tf_op jit(solution)/shard_map/project_most/pallas_call | solution.py:171
  90.5 4.2 %project_most.3 = (f32[512,512]{1,0:T(8,128)S(1)}, bf16[672,512]{1,0:T(8,128)(2,1)S(1)}) custom-call(bf16[672,512]{1,0:T(8,128)(2,1)S(1)} %collective-permute-done.8.refs_0_, bf16[672,512]{1,0:T(8,128)(2,1)S(1)} %collective-permute-done.9.refs_1_, bf16[672,512]{1,0:T(8,128)(2,1)S(1)} %collective-permute-done.10.refs_2_, ...), custom_call_target="tpu_custom_call" | custom-call | flops 2466250752 | bytes 15728640 | tf_op jit(solution)/shard_map/project_most/pallas_call | solution.py:171
  98.2 8.2 %collective-permute-start.33 = (bf16[672,256]{1,0:T(8,128)(2,1)S(1)}, bf16[672,256]{1,0:T(8,128)(2,1)}, u32[]{:S(2)}, u32[]{:S(2)}) collective-permute-start(bf16[672,256]{1,0:T(8,128)(2,1)S(1)} %bitcast.19), channel_id=1, source_target_pairs={{0,8},{1,9},{2,10},{3,11},{4,12},{5,13},{6,14},{7,15},{8,0},{9,1},... | collective-permute-start | bytes 1032200 | tf_op jit(solution)/shard_map/ppermute | solution.py:32
  110.0 7.4 %collective-permute-done.29.sent_ref = bf16[256,1024]{1,0:T(8,128)(2,1)S(1)} collective-permute-done((bf16[256,1024]{1,0:T(8,128)(2,1)S(1)}, bf16[256,1024]{1,0:T(8,128)(2,1)S(1)}, u32[]{:S(2)}, u32[]{:S(2)}) %collective-permute-start.29) | collective-permute-done | bytes 524320 | tf_op jit(solution)/shard_map/ppermute | solution.py:462
  121.7 3.0 %collective-permute-done.33.refs_8_ = bf16[672,256]{1,0:T(8,128)(2,1)} collective-permute-done((bf16[672,256]{1,0:T(8,128)(2,1)S(1)}, bf16[672,256]{1,0:T(8,128)(2,1)}, u32[]{:S(2)}, u32[]{:S(2)}) %collective-permute-start.33) | collective-permute-done | bytes 344096 | tf_op jit(solution)/shard_map/ppermute | solution.py:32
  124.6 2.7 %collective-permute-start.35 = (bf16[672,256]{1,0:T(8,128)(2,1)}, bf16[672,256]{1,0:T(8,128)(2,1)S(1)}, u32[]{:S(2)}, u32[]{:S(2)}) collective-permute-start(bf16[672,256]{1,0:T(8,128)(2,1)} %collective-permute-done.33.refs_8_), channel_id=1, source_target_pairs={{0,6},{1,7},{2,0},{3,1},{4,2},{5,3},{6,4},{7,5},{8,14},{9,15},{10,... | collective-permute-start | bytes 1032200 | tf_op jit(solution)/shard_map/ppermute | solution.py:32
  127.3 5.9 %collective-permute-done.34.refs_11_ = bf16[672,256]{1,0:T(8,128)(2,1)S(1)} collective-permute-done((bf16[672,256]{1,0:T(8,128)(2,1)}, bf16[672,256]{1,0:T(8,128)(2,1)S(1)}, u32[]{:S(2)}, u32[]{:S(2)}) %collective-permute-start.34) | collective-permute-done | bytes 344096 | tf_op jit(solution)/shard_map/ppermute | solution.py:32
  138.1 6.2 %collective-permute-done.39.refs_14_ = bf16[672,256]{1,0:T(8,128)(2,1)S(1)} collective-permute-done((bf16[672,256]{1,0:T(8,128)(2,1)S(1)}, bf16[672,256]{1,0:T(8,128)(2,1)S(1)}, u32[]{:S(2)}, u32[]{:S(2)}) %collective-permute-start.39) | collective-permute-done | bytes 344096 | tf_op jit(solution)/shard_map/ppermute | solution.py:32
  145.8 2.6 %collective-permute-done.37.refs_4_.first = bf16[256,1024]{1,0:T(8,128)(2,1)S(1)} collective-permute-done((bf16[256,1024]{1,0:T(8,128)(2,1)S(1)}, bf16[256,1024]{1,0:T(8,128)(2,1)S(1)}, u32[]{:S(2)}, u32[]{:S(2)}) %collective-permute-start.37) | collective-permute-done | bytes 524320 | tf_op jit(solution)/shard_map/ppermute | solution.py:32
  151.7 3.9 %out_most.1 = (f32[2,672,512]{2,1,0:T(8,128)S(1)}, bf16[672,256]{1,0:T(8,128)(2,1)S(1)}) custom-call(bf16[256,1024]{1,0:T(8,128)(2,1)S(1)} %attend_before.1.refs_0_, bf16[256,1024]{1,0:T(8,128)(2,1)S(1)} %collective-permute-done.30.refs_1_, bf16[256,1024]{1,0:T(8,128)(2,1)S(1)} %collective-permute-done.31.refs_2_, ...), custom_call_target="tpu_custom_call" | custom-call | flops 1024 | bytes 1024 | tf_op jit(solution)/shard_map/out_most/pallas_call | solution.py:386
  157.0 5.3 %collective-permute-start.43 = (bf16[672,512]{1,0:T(8,128)(2,1)S(1)}, bf16[672,512]{1,0:T(8,128)(2,1)S(1)}, u32[]{:S(2)}, u32[]{:S(2)}) collective-permute-start(bf16[672,512]{1,0:T(8,128)(2,1)S(1)} %out_rest.3), channel_id=1, source_target_pairs={{0,1},{1,0},{2,3},{3,2},{4,5},{5,4},{6,7},{7,6},{8,9},{9,8},{10,11... | collective-permute-start | bytes 2064392 | tf_op jit(solution)/shard_map/ppermute | solution.py:32
  (100 shorter events, 50.7 us)
Async XLA Ops:
  1.1 22.3 %collective-permute-start.2 = (bf16[672,512]{1,0:T(8,128)(2,1)}, bf16[672,512]{1,0:T(8,128)(2,1)S(1)}, u32[]{:S(2)}, u32[]{:S(2)}) collective-permute-start(bf16[672,512]{1,0:T(8,128)(2,1)} %bitcast.12), channel_id=1, source_target_pairs={{0,16},{1,17},{2,18},{3,19},{4,20},{5,21},{6,22},{7,23},{8,24},{9,... | collective-permute-start | bytes 2064392 | tf_op jit(solution)/shard_map/ppermute | solution.py:32
  3.9 19.5 %collective-permute-start.3 = (bf16[672,512]{1,0:T(8,128)(2,1)}, bf16[672,512]{1,0:T(8,128)(2,1)S(1)}, u32[]{:S(2)}, u32[]{:S(2)}) collective-permute-start(bf16[672,512]{1,0:T(8,128)(2,1)} %bitcast.13), channel_id=1, source_target_pairs={{0,32},{1,33},{2,34},{3,35},{4,36},{5,37},{6,38},{7,39},{8,40},{9,... | collective-permute-start | bytes 2064392 | tf_op jit(solution)/shard_map/ppermute | solution.py:32
  4.1 19.3 %collective-permute-start.4 = (bf16[672,512]{1,0:T(8,128)(2,1)}, bf16[672,512]{1,0:T(8,128)(2,1)S(1)}, u32[]{:S(2)}, u32[]{:S(2)}) collective-permute-start(bf16[672,512]{1,0:T(8,128)(2,1)} %bitcast.14), channel_id=1, source_target_pairs={{0,96},{1,97},{2,98},{3,99},{4,100},{5,101},{6,102},{7,103},{8,104... | collective-permute-start | bytes 2064392 | tf_op jit(solution)/shard_map/ppermute | solution.py:32
  10.0 13.4 %collective-permute-start.1 = (bf16[672,256]{1,0:T(8,128)(2,1)S(1)}, bf16[672,256]{1,0:T(8,128)(2,1)S(1)}, u32[]{:S(2)}, u32[]{:S(2)}) collective-permute-start(bf16[672,256]{1,0:T(8,128)(2,1)S(1)} %bitcast.22), channel_id=1, source_target_pairs={{0,0},{1,1},{2,2},{3,3},{4,4},{5,5},{6,6},{7,7},{8,8},{9,9},{10,10... | collective-permute-start | bytes 1032200 | tf_op jit(solution)/shard_map/ppermute | solution.py:32
  16.1 13.7 %collective-permute-start.8 = (bf16[672,512]{1,0:T(8,128)(2,1)}, bf16[672,512]{1,0:T(8,128)(2,1)S(1)}, u32[]{:S(2)}, u32[]{:S(2)}) collective-permute-start(bf16[672,512]{1,0:T(8,128)(2,1)} %bitcast.15), channel_id=1, source_target_pairs={{0,1},{1,0},{2,3},{3,2},{4,5},{5,4},{6,7},{7,6},{8,9},{9,8},{10,11... | collective-permute-start | bytes 2064392 | tf_op jit(solution)/shard_map/ppermute | solution.py:32
  23.4 18.8 %collective-permute-start.5 = (bf16[672,512]{1,0:T(8,128)(2,1)S(1)}, bf16[672,512]{1,0:T(8,128)(2,1)S(1)}, u32[]{:S(2)}, u32[]{:S(2)}) collective-permute-start(bf16[672,512]{1,0:T(8,128)(2,1)S(1)} %small.6), channel_id=1, source_target_pairs={{0,0},{1,1},{2,34},{3,35},{4,68},{5,69},{6,102},{7,103},{8,16},{9,... | collective-permute-start | bytes 2064392 | tf_op jit(solution)/shard_map/ppermute | solution.py:32
  26.3 15.9 %collective-permute-start.9 = (bf16[672,512]{1,0:T(8,128)(2,1)S(1)}, bf16[672,512]{1,0:T(8,128)(2,1)S(1)}, u32[]{:S(2)}, u32[]{:S(2)}) collective-permute-start(bf16[672,512]{1,0:T(8,128)(2,1)S(1)} %collective-permute-done.2.refs_1_), channel_id=1, source_target_pairs={{0,1},{1,0},{2,3},{3,2},{4,5},{5,4},{6,7},{7,6},{8,9},{9,8},{10,11... | collective-permute-start | bytes 2064392 | tf_op jit(solution)/shard_map/ppermute | solution.py:32
  28.8 13.5 %collective-permute-start.10 = (bf16[672,512]{1,0:T(8,128)(2,1)S(1)}, bf16[672,512]{1,0:T(8,128)(2,1)S(1)}, u32[]{:S(2)}, u32[]{:S(2)}) collective-permute-start(bf16[672,512]{1,0:T(8,128)(2,1)S(1)} %collective-permute-done.3.refs_2_), channel_id=1, source_target_pairs={{0,1},{1,0},{2,3},{3,2},{4,5},{5,4},{6,7},{7,6},{8,9},{9,8},{10,11... | collective-permute-start | bytes 2064392 | tf_op jit(solution)/shard_map/ppermute | solution.py:32
  42.2 13.6 %collective-permute-start.11 = (bf16[672,512]{1,0:T(8,128)(2,1)S(1)}, bf16[672,512]{1,0:T(8,128)(2,1)S(1)}, u32[]{:S(2)}, u32[]{:S(2)}) collective-permute-start(bf16[672,512]{1,0:T(8,128)(2,1)S(1)} %collective-permute-done.5.refs_0_), channel_id=1, source_target_pairs={{0,8},{1,9},{2,10},{3,11},{4,12},{5,13},{6,14},{7,15},{8,0},{9,1},... | collective-permute-start | bytes 2064392 | tf_op jit(solution)/shard_map/ppermute | solution.py:32
  42.2 15.5 %collective-permute-start.12 = (bf16[672,512]{1,0:T(8,128)(2,1)S(1)}, bf16[672,512]{1,0:T(8,128)(2,1)S(1)}, u32[]{:S(2)}, u32[]{:S(2)}) collective-permute-start(bf16[672,512]{1,0:T(8,128)(2,1)S(1)} %collective-permute-done.5.refs_0_), channel_id=1, source_target_pairs={{0,2},{1,3},{2,4},{3,5},{4,6},{5,7},{6,0},{7,1},{8,10},{9,11},{10,... | collective-permute-start | bytes 2064392 | tf_op jit(solution)/shard_map/ppermute | solution.py:32
  42.3 15.4 %collective-permute-start.13 = (bf16[672,512]{1,0:T(8,128)(2,1)S(1)}, bf16[672,512]{1,0:T(8,128)(2,1)S(1)}, u32[]{:S(2)}, u32[]{:S(2)}) collective-permute-start(bf16[672,512]{1,0:T(8,128)(2,1)S(1)} %collective-permute-done.5.refs_0_), channel_id=1, source_target_pairs={{0,6},{1,7},{2,0},{3,1},{4,2},{5,3},{6,4},{7,5},{8,14},{9,15},{10,... | collective-permute-start | bytes 2064392 | tf_op jit(solution)/shard_map/ppermute | solution.py:32
  45.5 13.3 %collective-permute-start.14 = (bf16[672,512]{1,0:T(8,128)(2,1)S(1)}, bf16[672,512]{1,0:T(8,128)(2,1)S(1)}, u32[]{:S(2)}, u32[]{:S(2)}) collective-permute-start(bf16[672,512]{1,0:T(8,128)(2,1)S(1)} %collective-permute-done.2.refs_1_), channel_id=1, source_target_pairs={{0,32},{1,33},{2,34},{3,35},{4,36},{5,37},{6,38},{7,39},{8,40},{9,... | collective-permute-start | bytes 2064392 | tf_op jit(solution)/shard_map/ppermute | solution.py:32
  46.0 14.8 %collective-permute-start.15 = (bf16[672,512]{1,0:T(8,128)(2,1)S(1)}, bf16[672,512]{1,0:T(8,128)(2,1)S(1)}, u32[]{:S(2)}, u32[]{:S(2)}) collective-permute-start(bf16[672,512]{1,0:T(8,128)(2,1)S(1)} %collective-permute-done.2.refs_1_), channel_id=1, source_target_pairs={{0,96},{1,97},{2,98},{3,99},{4,100},{5,101},{6,102},{7,103},{8,104... | collective-permute-start | bytes 2064392 | tf_op jit(solution)/shard_map/ppermute | solution.py:32
  60.8 13.8 %collective-permute-start.16 = (bf16[672,512]{1,0:T(8,128)(2,1)S(1)}, bf16[672,512]{1,0:T(8,128)(2,1)S(1)}, u32[]{:S(2)}, u32[]{:S(2)}) collective-permute-start(bf16[672,512]{1,0:T(8,128)(2,1)S(1)} %collective-permute-done.12.refs_2_), channel_id=1, source_target_pairs={{0,2},{1,3},{2,4},{3,5},{4,6},{5,7},{6,0},{7,1},{8,10},{9,11},{10,... | collective-permute-start | bytes 2064392 | tf_op jit(solution)/shard_map/ppermute | solution.py:32
  60.8 19.1 %collective-permute-start.17 = (bf16[672,512]{1,0:T(8,128)(2,1)S(1)}, bf16[672,512]{1,0:T(8,128)(2,1)S(1)}, u32[]{:S(2)}, u32[]{:S(2)}) collective-permute-start(bf16[672,512]{1,0:T(8,128)(2,1)S(1)} %collective-permute-done.12.refs_2_), channel_id=1, source_target_pairs={{0,8},{1,9},{2,10},{3,11},{4,12},{5,13},{6,14},{7,15},{8,0},{9,1},... | collective-permute-start | bytes 2064392 | tf_op jit(solution)/shard_map/ppermute | solution.py:32
  61.1 19.7 %collective-permute-start.18 = (bf16[672,512]{1,0:T(8,128)(2,1)S(1)}, bf16[672,512]{1,0:T(8,128)(2,1)S(1)}, u32[]{:S(2)}, u32[]{:S(2)}) collective-permute-start(bf16[672,512]{1,0:T(8,128)(2,1)S(1)} %collective-permute-done.11.refs_1_), channel_id=1, source_target_pairs={{0,6},{1,7},{2,0},{3,1},{4,2},{5,3},{6,4},{7,5},{8,14},{9,15},{10,... | collective-permute-start | bytes 2064392 | tf_op jit(solution)/shard_map/ppermute | solution.py:32
  63.7 17.6 %collective-permute-start.19 = (bf16[672,512]{1,0:T(8,128)(2,1)S(1)}, bf16[672,512]{1,0:T(8,128)(2,1)S(1)}, u32[]{:S(2)}, u32[]{:S(2)}) collective-permute-start(bf16[672,512]{1,0:T(8,128)(2,1)S(1)} %collective-permute-done.3.refs_2_), channel_id=1, source_target_pairs={{0,32},{1,33},{2,34},{3,35},{4,36},{5,37},{6,38},{7,39},{8,40},{9,... | collective-permute-start | bytes 2064392 | tf_op jit(solution)/shard_map/ppermute | solution.py:32
  64.0 17.4 %collective-permute-start.20 = (bf16[672,512]{1,0:T(8,128)(2,1)S(1)}, bf16[672,512]{1,0:T(8,128)(2,1)S(1)}, u32[]{:S(2)}, u32[]{:S(2)}) collective-permute-start(bf16[672,512]{1,0:T(8,128)(2,1)S(1)} %collective-permute-done.15.refs_5_), channel_id=1, source_target_pairs={{0,96},{1,97},{2,98},{3,99},{4,100},{5,101},{6,102},{7,103},{8,104... | collective-permute-start | bytes 2064392 | tf_op jit(solution)/shard_map/ppermute | solution.py:32
  95.4 22.0 %collective-permute-start.29 = (bf16[256,1024]{1,0:T(8,128)(2,1)S(1)}, bf16[256,1024]{1,0:T(8,128)(2,1)S(1)}, u32[]{:S(2)}, u32[]{:S(2)}) collective-permute-start(bf16[256,1024]{1,0:T(8,128)(2,1)S(1)} %project_rest.2.kv.kv_ref), channel_id=1, source_target_pairs={{0,2},{1,3},{2,4},{3,5},{4,6},{5,7},{6,8},{7,9},{8,10},{9,11},{10,... | collective-permute-start | bytes 1572872 | tf_op jit(solution)/shard_map/ppermute | solution.py:462
  98.2 26.4 %collective-permute-start.33 = (bf16[672,256]{1,0:T(8,128)(2,1)S(1)}, bf16[672,256]{1,0:T(8,128)(2,1)}, u32[]{:S(2)}, u32[]{:S(2)}) collective-permute-start(bf16[672,256]{1,0:T(8,128)(2,1)S(1)} %bitcast.19), channel_id=1, source_target_pairs={{0,8},{1,9},{2,10},{3,11},{4,12},{5,13},{6,14},{7,15},{8,0},{9,1},... | collective-permute-start | bytes 1032200 | tf_op jit(solution)/shard_map/ppermute | solution.py:32
  119.7 13.5 %collective-permute-start.30 = (bf16[256,1024]{1,0:T(8,128)(2,1)S(1)}, bf16[256,1024]{1,0:T(8,128)(2,1)S(1)}, u32[]{:S(2)}, u32[]{:S(2)}) collective-permute-start(bf16[256,1024]{1,0:T(8,128)(2,1)S(1)} %attend_before.1.refs_0_), channel_id=1, source_target_pairs={{0,16},{1,17},{2,18},{3,19},{4,20},{5,21},{6,22},{7,23},{8,24},{9,... | collective-permute-start | bytes 1572872 | tf_op jit(solution)/shard_map/ppermute | solution.py:32
  119.8 13.5 %collective-permute-start.31 = (bf16[256,1024]{1,0:T(8,128)(2,1)S(1)}, bf16[256,1024]{1,0:T(8,128)(2,1)S(1)}, u32[]{:S(2)}, u32[]{:S(2)}) collective-permute-start(bf16[256,1024]{1,0:T(8,128)(2,1)S(1)} %attend_before.1.refs_0_), channel_id=1, source_target_pairs={{0,32},{1,33},{2,34},{3,35},{4,36},{5,37},{6,38},{7,39},{8,40},{9,... | collective-permute-start | bytes 1572872 | tf_op jit(solution)/shard_map/ppermute | solution.py:32
  119.9 13.4 %collective-permute-start.32 = (bf16[256,1024]{1,0:T(8,128)(2,1)S(1)}, bf16[256,1024]{1,0:T(8,128)(2,1)S(1)}, u32[]{:S(2)}, u32[]{:S(2)}) collective-permute-start(bf16[256,1024]{1,0:T(8,128)(2,1)S(1)} %attend_before.1.refs_0_), channel_id=1, source_target_pairs={{0,96},{1,97},{2,98},{3,99},{4,100},{5,101},{6,102},{7,103},{8,104... | collective-permute-start | bytes 1572872 | tf_op jit(solution)/shard_map/ppermute | solution.py:32
  138.1 13.6 %collective-permute-start.40 = (bf16[672,256]{1,0:T(8,128)(2,1)S(1)}, bf16[672,256]{1,0:T(8,128)(2,1)S(1)}, u32[]{:S(2)}, u32[]{:S(2)}) collective-permute-start(bf16[672,256]{1,0:T(8,128)(2,1)S(1)} %copy-done.5), channel_id=1, source_target_pairs={{0,6},{1,7},{2,0},{3,1},{4,2},{5,3},{6,4},{7,5},{8,14},{9,15},{10,... | collective-permute-start | bytes 1032200 | tf_op jit(solution)/shard_map/ppermute | solution.py:32
  (29 other events, 357.1 us)

commit v2 on v1

--- a/solution.py
+++ b/solution.py
@@ -462,10 +462,11 @@
     before = lax.ppermute(kv, "gy", [(i, i + 2) for i in range(14)])
     q = project_rest(project_q_kernel, last_q, kv, most, most_other, cosine, sine)
 
-    kv, q, out_block, out_r, out_l, cached = together(kv, q, out_block, out_r, out_l, cached)
-    cached = cached.reshape(2 * rows, 2 * HD).T
+    kv, q, out_block, out_r, out_l = together(kv, q, out_block, out_r, out_l)
     out_z, out_f = swap_zl(out_block), shift_y(out_l, -1)
     total, weight_sum = attend_own(q, kv)
+    total, weight_sum, cached = together(total, weight_sum, cached)
+    cached = cached.reshape(2 * rows, 2 * HD).T
     mixed = attend_before(q, before, cached, total, weight_sum)
 
     mixed_z = swap_zh(mixed)

time: 168 us -> 166 us (0.988); the launches traced: 165 us -> 165 us
  starting transfers between devices: 69.2 us -> 63.1 us
  waiting for transfers between devices: 69.7 us -> 75.1 us
    ppermute x42, starting transfers between devices: 66.6 us -> 60.5 us  [move(): lax.ppermute(value, AXES, [(i, number(*to(*place(i)))) for i in range(128)])]
    ppermute x1, waiting for transfers between devices: 7.44 us -> 13.4 us  [shards(): before = lax.ppermute(kv, 'gy', [(i, i + 2) for i in range(14)])]
where the time goes in v2:
time: 166 us; the launch traced here: 165 us
  waiting for transfers between devices  75.1 us (45%)
  starting transfers between devices  63.1 us (38%)
  Pallas kernels  21.7 us (13%)
  local copies, waits for them, and re-layouts  3.22 us (2%)
    ppermute x42, waiting for transfers between devices, move(): lax.ppermute(value, AXES, [(i, number(*to(*place(i)))) for i in range(128)])  61.7 us
    ppermute x42, starting transfers between devices, move(): lax.ppermute(value, AXES, [(i, number(*to(*place(i)))) for i in range(128)])  60.5 us
    ppermute x1, waiting for transfers between devices, shards(): before = lax.ppermute(kv, 'gy', [(i, i + 2) for i in range(14)])  13.4 us
    pallas_call x2, Pallas kernels, project_most(): pl.pallas_call(project_most_kernel, out_shape=(jax.ShapeDtypeStruct((colu...  8.54 us
    pallas_call x1, Pallas kernels, out_most(): pl.pallas_call(out_most_kernel, out_shape=(jax.ShapeDtypeStruct((2, width...  3.87 us
  transfers between devices with their start and end apart: 44, of which 19 were waited for; matrix products, arithmetic and copies ran while one was open for 1% of the time, Pallas kernels for 13%

profile of v2, /device:TPU:39, one launch (start us, length us, event | category | flops | bytes accessed | tf_op | source)
XLA Modules:
  0.0 165.2 jit_solution(14896929977535419864)
XLA Ops:
  1.1 2.8 %collective-permute-start.2 = (bf16[672,512]{1,0:T(8,128)(2,1)}, bf16[672,512]{1,0:T(8,128)(2,1)S(1)}, u32[]{:S(2)}, u32[]{:S(2)}) collective-permute-start(bf16[672,512]{1,0:T(8,128)(2,1)} %bitcast.12), channel_id=1, source_target_pairs={{0,16},{1,17},{2,18},{3,19},{4,20},{5,21},{6,22},{7,23},{8,24},{9,... | collective-permute-start | bytes 2064392 | tf_op jit(solution)/shard_map/ppermute | solution.py:32
  5.3 4.6 %collective-permute-start = (bf16[672,256]{1,0:T(8,128)(2,1)}, bf16[672,256]{1,0:T(8,128)(2,1)S(1)}, u32[]{:S(2)}, u32[]{:S(2)}) collective-permute-start(bf16[672,256]{1,0:T(8,128)(2,1)} %param.9), channel_id=1, source_target_pairs={{0,0},{1,1},{2,2},{3,3},{4,4},{5,5},{6,6},{7,7},{8,8},{9,9},{10,10... | collective-permute-start | bytes 1032200 | tf_op jit(solution)/shard_map/ppermute | solution.py:32
  12.4 3.7 %collective-permute-done.right = bf16[672,256]{1,0:T(8,128)(2,1)S(1)} collective-permute-done((bf16[672,256]{1,0:T(8,128)(2,1)}, bf16[672,256]{1,0:T(8,128)(2,1)S(1)}, u32[]{:S(2)}, u32[]{:S(2)}) %collective-permute-start) | collective-permute-done | bytes 344096 | tf_op jit(solution)/shard_map/ppermute | solution.py:32
  16.1 4.5 %collective-permute-start.8 = (bf16[672,512]{1,0:T(8,128)(2,1)}, bf16[672,512]{1,0:T(8,128)(2,1)S(1)}, u32[]{:S(2)}, u32[]{:S(2)}) collective-permute-start(bf16[672,512]{1,0:T(8,128)(2,1)} %bitcast.15), channel_id=1, source_target_pairs={{0,1},{1,0},{2,3},{3,2},{4,5},{5,4},{6,7},{7,6},{8,9},{9,8},{10,11... | collective-permute-start | bytes 2064392 | tf_op jit(solution)/shard_map/ppermute | solution.py:32
  20.6 2.8 %collective-permute-done.1.left = bf16[672,256]{1,0:T(8,128)(2,1)S(1)} collective-permute-done((bf16[672,256]{1,0:T(8,128)(2,1)S(1)}, bf16[672,256]{1,0:T(8,128)(2,1)S(1)}, u32[]{:S(2)}, u32[]{:S(2)}) %collective-permute-start.1) | collective-permute-done | bytes 344096 | tf_op jit(solution)/shard_map/ppermute | solution.py:32
  23.4 2.9 %collective-permute-start.5 = (bf16[672,512]{1,0:T(8,128)(2,1)S(1)}, bf16[672,512]{1,0:T(8,128)(2,1)S(1)}, u32[]{:S(2)}, u32[]{:S(2)}) collective-permute-start(bf16[672,512]{1,0:T(8,128)(2,1)S(1)} %small.6), channel_id=1, source_target_pairs={{0,0},{1,1},{2,34},{3,35},{4,68},{5,69},{6,102},{7,103},{8,16},{9,... | collective-permute-start | bytes 2064392 | tf_op jit(solution)/shard_map/ppermute | solution.py:32
  26.3 2.4 %collective-permute-start.9 = (bf16[672,512]{1,0:T(8,128)(2,1)S(1)}, bf16[672,512]{1,0:T(8,128)(2,1)S(1)}, u32[]{:S(2)}, u32[]{:S(2)}) collective-permute-start(bf16[672,512]{1,0:T(8,128)(2,1)S(1)} %collective-permute-done.2.refs_1_), channel_id=1, source_target_pairs={{0,1},{1,0},{2,3},{3,2},{4,5},{5,4},{6,7},{7,6},{8,9},{9,8},{10,11... | collective-permute-start | bytes 2064392 | tf_op jit(solution)/shard_map/ppermute | solution.py:32
  33.2 6.1 %collective-permute-done.6.refs_9_ = bf16[672,256]{1,0:T(8,128)(2,1)S(1)} collective-permute-done((bf16[672,256]{1,0:T(8,128)(2,1)S(1)}, bf16[672,256]{1,0:T(8,128)(2,1)S(1)}, u32[]{:S(2)}, u32[]{:S(2)}) %collective-permute-start.6) | collective-permute-done | bytes 344096 | tf_op jit(solution)/shard_map/ppermute | solution.py:32
  39.3 2.9 %collective-permute-done.5.refs_0_ = bf16[672,512]{1,0:T(8,128)(2,1)S(1)} collective-permute-done((bf16[672,512]{1,0:T(8,128)(2,1)S(1)}, bf16[672,512]{1,0:T(8,128)(2,1)S(1)}, u32[]{:S(2)}, u32[]{:S(2)}) %collective-permute-start.5) | collective-permute-done | bytes 688160 | tf_op jit(solution)/shard_map/ppermute | solution.py:32
  42.3 3.2 %collective-permute-start.13 = (bf16[672,512]{1,0:T(8,128)(2,1)S(1)}, bf16[672,512]{1,0:T(8,128)(2,1)S(1)}, u32[]{:S(2)}, u32[]{:S(2)}) collective-permute-start(bf16[672,512]{1,0:T(8,128)(2,1)S(1)} %collective-permute-done.5.refs_0_), channel_id=1, source_target_pairs={{0,6},{1,7},{2,0},{3,1},{4,2},{5,3},{6,4},{7,5},{8,14},{9,15},{10,... | collective-permute-start | bytes 2064392 | tf_op jit(solution)/shard_map/ppermute | solution.py:32
  47.0 8.8 %collective-permute-done.11.refs_1_ = bf16[672,512]{1,0:T(8,128)(2,1)S(1)} collective-permute-done((bf16[672,512]{1,0:T(8,128)(2,1)S(1)}, bf16[672,512]{1,0:T(8,128)(2,1)S(1)}, u32[]{:S(2)}, u32[]{:S(2)}) %collective-permute-start.11) | collective-permute-done | bytes 688160 | tf_op jit(solution)/shard_map/ppermute | solution.py:32
  61.1 2.7 %collective-permute-start.18 = (bf16[672,512]{1,0:T(8,128)(2,1)S(1)}, bf16[672,512]{1,0:T(8,128)(2,1)S(1)}, u32[]{:S(2)}, u32[]{:S(2)}) collective-permute-start(bf16[672,512]{1,0:T(8,128)(2,1)S(1)} %collective-permute-done.11.refs_1_), channel_id=1, source_target_pairs={{0,6},{1,7},{2,0},{3,1},{4,2},{5,3},{6,4},{7,5},{8,14},{9,15},{10,... | collective-permute-start | bytes 2064392 | tf_op jit(solution)/shard_map/ppermute | solution.py:32
  65.2 9.5 %collective-permute-done.16.refs_2_ = bf16[672,512]{1,0:T(8,128)(2,1)S(1)} collective-permute-done((bf16[672,512]{1,0:T(8,128)(2,1)S(1)}, bf16[672,512]{1,0:T(8,128)(2,1)S(1)}, u32[]{:S(2)}, u32[]{:S(2)}) %collective-permute-start.16) | collective-permute-done | bytes 688160 | tf_op jit(solution)/shard_map/ppermute | solution.py:32
  74.7 5.2 %collective-permute-start.23 = (bf16[672,512]{1,0:T(8,128)(2,1)S(1)}, bf16[672,512]{1,0:T(8,128)(2,1)S(1)}, u32[]{:S(2)}, u32[]{:S(2)}) collective-permute-start(bf16[672,512]{1,0:T(8,128)(2,1)S(1)} %collective-permute-done.4.refs_3_), channel_id=1, source_target_pairs={{0,1},{1,0},{2,3},{3,2},{4,5},{5,4},{6,7},{7,6},{8,9},{9,8},{10,11... | collective-permute-start | bytes 2064392 | tf_op jit(solution)/shard_map/ppermute | solution.py:32
  85.4 4.4 %project_most.2 = (f32[512,512]{1,0:T(8,128)S(1)}, bf16[672,512]{1,0:T(8,128)(2,1)S(1)}) custom-call(bf16[672,512]{1,0:T(8,128)(2,1)S(1)} %bitcast.16, bf16[672,512]{1,0:T(8,128)(2,1)S(1)} %collective-permute-done.2.refs_1_, bf16[672,512]{1,0:T(8,128)(2,1)S(1)} %collective-permute-done.3.refs_2_, bf16[672,512]{1,0:T(8,128)(2,1)S(1)} %collective-permute-done.4.refs_3_, ...), custom_call_target="tpu_custom_call" | custom-call | flops 2466250752 | bytes 15728640 | tf_op jit(solution)/shard_map/project_most/pallas_call | solution.py:171
  90.5 4.2 %project_most.3 = (f32[512,512]{1,0:T(8,128)S(1)}, bf16[672,512]{1,0:T(8,128)(2,1)S(1)}) custom-call(bf16[672,512]{1,0:T(8,128)(2,1)S(1)} %collective-permute-done.8.refs_0_, bf16[672,512]{1,0:T(8,128)(2,1)S(1)} %collective-permute-done.9.refs_1_, bf16[672,512]{1,0:T(8,128)(2,1)S(1)} %collective-permute-done.10.refs_2_, ...), custom_call_target="tpu_custom_call" | custom-call | flops 2466250752 | bytes 15728640 | tf_op jit(solution)/shard_map/project_most/pallas_call | solution.py:171
  104.1 13.4 %collective-permute-done.28.sent_ref = bf16[256,1024]{1,0:T(8,128)(2,1)S(1)} collective-permute-done((bf16[256,1024]{1,0:T(8,128)(2,1)S(1)}, bf16[256,1024]{1,0:T(8,128)(2,1)S(1)}, u32[]{:S(2)}, u32[]{:S(2)}) %collective-permute-start.28) | collective-permute-done | bytes 524320 | tf_op jit(solution)/shard_map/ppermute | solution.py:462
  121.7 2.7 %collective-permute-start.35 = (bf16[672,256]{1,0:T(8,128)(2,1)}, bf16[672,256]{1,0:T(8,128)(2,1)S(1)}, u32[]{:S(2)}, u32[]{:S(2)}) collective-permute-start(bf16[672,256]{1,0:T(8,128)(2,1)} %collective-permute-done.33.refs_8_), channel_id=1, source_target_pairs={{0,6},{1,7},{2,0},{3,1},{4,2},{5,3},{6,4},{7,5},{8,14},{9,15},{10,... | collective-permute-start | bytes 1032200 | tf_op jit(solution)/shard_map/ppermute | solution.py:32
  124.4 6.0 %collective-permute-done.34.refs_11_ = bf16[672,256]{1,0:T(8,128)(2,1)S(1)} collective-permute-done((bf16[672,256]{1,0:T(8,128)(2,1)}, bf16[672,256]{1,0:T(8,128)(2,1)S(1)}, u32[]{:S(2)}, u32[]{:S(2)}) %collective-permute-start.34) | collective-permute-done | bytes 344096 | tf_op jit(solution)/shard_map/ppermute | solution.py:32
  132.7 2.5 %collective-permute-start.36 = (bf16[256,1024]{1,0:T(8,128)(2,1)S(1)}, bf16[256,1024]{1,0:T(8,128)(2,1)S(1)}, u32[]{:S(2)}, u32[]{:S(2)}) collective-permute-start(bf16[256,1024]{1,0:T(8,128)(2,1)S(1)} %collective-permute-done.31.refs_2_), channel_id=1, source_target_pairs={{0,32},{1,33},{2,34},{3,35},{4,36},{5,37},{6,38},{7,39},{8,40},{9,... | collective-permute-start | bytes 1572872 | tf_op jit(solution)/shard_map/ppermute | solution.py:32
  135.1 2.6 %collective-permute-start.37 = (bf16[256,1024]{1,0:T(8,128)(2,1)S(1)}, bf16[256,1024]{1,0:T(8,128)(2,1)S(1)}, u32[]{:S(2)}, u32[]{:S(2)}) collective-permute-start(bf16[256,1024]{1,0:T(8,128)(2,1)S(1)} %collective-permute-done.31.refs_2_), channel_id=1, source_target_pairs={{0,16},{1,17},{2,18},{3,19},{4,20},{5,21},{6,22},{7,23},{8,24},{9,... | collective-permute-start | bytes 1572872 | tf_op jit(solution)/shard_map/ppermute | solution.py:32
  138.2 6.2 %collective-permute-done.39.refs_14_ = bf16[672,256]{1,0:T(8,128)(2,1)S(1)} collective-permute-done((bf16[672,256]{1,0:T(8,128)(2,1)S(1)}, bf16[672,256]{1,0:T(8,128)(2,1)S(1)}, u32[]{:S(2)}, u32[]{:S(2)}) %collective-permute-start.39) | collective-permute-done | bytes 344096 | tf_op jit(solution)/shard_map/ppermute | solution.py:32
  151.8 3.9 %out_most.1 = (f32[2,672,512]{2,1,0:T(8,128)S(1)}, bf16[672,256]{1,0:T(8,128)(2,1)S(1)}) custom-call(bf16[256,1024]{1,0:T(8,128)(2,1)S(1)} %attend_before.1.refs_0_, bf16[256,1024]{1,0:T(8,128)(2,1)S(1)} %collective-permute-done.30.refs_1_, bf16[256,1024]{1,0:T(8,128)(2,1)S(1)} %collective-permute-done.31.refs_2_, ...), custom_call_target="tpu_custom_call" | custom-call | flops 1024 | bytes 1024 | tf_op jit(solution)/shard_map/out_most/pallas_call | solution.py:386
  157.0 5.3 %collective-permute-start.43 = (bf16[672,512]{1,0:T(8,128)(2,1)S(1)}, bf16[672,512]{1,0:T(8,128)(2,1)S(1)}, u32[]{:S(2)}, u32[]{:S(2)}) collective-permute-start(bf16[672,512]{1,0:T(8,128)(2,1)S(1)} %out_rest.3), channel_id=1, source_target_pairs={{0,1},{1,0},{2,3},{3,2},{4,5},{5,4},{6,7},{7,6},{8,9},{9,8},{10,11... | collective-permute-start | bytes 2064392 | tf_op jit(solution)/shard_map/ppermute | solution.py:32
  (100 shorter events, 50.9 us)
Async XLA Ops:
  1.1 22.3 %collective-permute-start.2 = (bf16[672,512]{1,0:T(8,128)(2,1)}, bf16[672,512]{1,0:T(8,128)(2,1)S(1)}, u32[]{:S(2)}, u32[]{:S(2)}) collective-permute-start(bf16[672,512]{1,0:T(8,128)(2,1)} %bitcast.12), channel_id=1, source_target_pairs={{0,16},{1,17},{2,18},{3,19},{4,20},{5,21},{6,22},{7,23},{8,24},{9,... | collective-permute-start | bytes 2064392 | tf_op jit(solution)/shard_map/ppermute | solution.py:32
  3.9 19.5 %collective-permute-start.3 = (bf16[672,512]{1,0:T(8,128)(2,1)}, bf16[672,512]{1,0:T(8,128)(2,1)S(1)}, u32[]{:S(2)}, u32[]{:S(2)}) collective-permute-start(bf16[672,512]{1,0:T(8,128)(2,1)} %bitcast.13), channel_id=1, source_target_pairs={{0,32},{1,33},{2,34},{3,35},{4,36},{5,37},{6,38},{7,39},{8,40},{9,... | collective-permute-start | bytes 2064392 | tf_op jit(solution)/shard_map/ppermute | solution.py:32
  4.1 19.3 %collective-permute-start.4 = (bf16[672,512]{1,0:T(8,128)(2,1)}, bf16[672,512]{1,0:T(8,128)(2,1)S(1)}, u32[]{:S(2)}, u32[]{:S(2)}) collective-permute-start(bf16[672,512]{1,0:T(8,128)(2,1)} %bitcast.14), channel_id=1, source_target_pairs={{0,96},{1,97},{2,98},{3,99},{4,100},{5,101},{6,102},{7,103},{8,104... | collective-permute-start | bytes 2064392 | tf_op jit(solution)/shard_map/ppermute | solution.py:32
  10.0 13.4 %collective-permute-start.1 = (bf16[672,256]{1,0:T(8,128)(2,1)S(1)}, bf16[672,256]{1,0:T(8,128)(2,1)S(1)}, u32[]{:S(2)}, u32[]{:S(2)}) collective-permute-start(bf16[672,256]{1,0:T(8,128)(2,1)S(1)} %bitcast.22), channel_id=1, source_target_pairs={{0,0},{1,1},{2,2},{3,3},{4,4},{5,5},{6,6},{7,7},{8,8},{9,9},{10,10... | collective-permute-start | bytes 1032200 | tf_op jit(solution)/shard_map/ppermute | solution.py:32
  16.1 13.7 %collective-permute-start.8 = (bf16[672,512]{1,0:T(8,128)(2,1)}, bf16[672,512]{1,0:T(8,128)(2,1)S(1)}, u32[]{:S(2)}, u32[]{:S(2)}) collective-permute-start(bf16[672,512]{1,0:T(8,128)(2,1)} %bitcast.15), channel_id=1, source_target_pairs={{0,1},{1,0},{2,3},{3,2},{4,5},{5,4},{6,7},{7,6},{8,9},{9,8},{10,11... | collective-permute-start | bytes 2064392 | tf_op jit(solution)/shard_map/ppermute | solution.py:32
  23.4 18.8 %collective-permute-start.5 = (bf16[672,512]{1,0:T(8,128)(2,1)S(1)}, bf16[672,512]{1,0:T(8,128)(2,1)S(1)}, u32[]{:S(2)}, u32[]{:S(2)}) collective-permute-start(bf16[672,512]{1,0:T(8,128)(2,1)S(1)} %small.6), channel_id=1, source_target_pairs={{0,0},{1,1},{2,34},{3,35},{4,68},{5,69},{6,102},{7,103},{8,16},{9,... | collective-permute-start | bytes 2064392 | tf_op jit(solution)/shard_map/ppermute | solution.py:32
  26.3 15.9 %collective-permute-start.9 = (bf16[672,512]{1,0:T(8,128)(2,1)S(1)}, bf16[672,512]{1,0:T(8,128)(2,1)S(1)}, u32[]{:S(2)}, u32[]{:S(2)}) collective-permute-start(bf16[672,512]{1,0:T(8,128)(2,1)S(1)} %collective-permute-done.2.refs_1_), channel_id=1, source_target_pairs={{0,1},{1,0},{2,3},{3,2},{4,5},{5,4},{6,7},{7,6},{8,9},{9,8},{10,11... | collective-permute-start | bytes 2064392 | tf_op jit(solution)/shard_map/ppermute | solution.py:32
  28.8 13.5 %collective-permute-start.10 = (bf16[672,512]{1,0:T(8,128)(2,1)S(1)}, bf16[672,512]{1,0:T(8,128)(2,1)S(1)}, u32[]{:S(2)}, u32[]{:S(2)}) collective-permute-start(bf16[672,512]{1,0:T(8,128)(2,1)S(1)} %collective-permute-done.3.refs_2_), channel_id=1, source_target_pairs={{0,1},{1,0},{2,3},{3,2},{4,5},{5,4},{6,7},{7,6},{8,9},{9,8},{10,11... | collective-permute-start | bytes 2064392 | tf_op jit(solution)/shard_map/ppermute | solution.py:32
  42.2 13.6 %collective-permute-start.11 = (bf16[672,512]{1,0:T(8,128)(2,1)S(1)}, bf16[672,512]{1,0:T(8,128)(2,1)S(1)}, u32[]{:S(2)}, u32[]{:S(2)}) collective-permute-start(bf16[672,512]{1,0:T(8,128)(2,1)S(1)} %collective-permute-done.5.refs_0_), channel_id=1, source_target_pairs={{0,8},{1,9},{2,10},{3,11},{4,12},{5,13},{6,14},{7,15},{8,0},{9,1},... | collective-permute-start | bytes 2064392 | tf_op jit(solution)/shard_map/ppermute | solution.py:32
  42.2 15.5 %collective-permute-start.12 = (bf16[672,512]{1,0:T(8,128)(2,1)S(1)}, bf16[672,512]{1,0:T(8,128)(2,1)S(1)}, u32[]{:S(2)}, u32[]{:S(2)}) collective-permute-start(bf16[672,512]{1,0:T(8,128)(2,1)S(1)} %collective-permute-done.5.refs_0_), channel_id=1, source_target_pairs={{0,2},{1,3},{2,4},{3,5},{4,6},{5,7},{6,0},{7,1},{8,10},{9,11},{10,... | collective-permute-start | bytes 2064392 | tf_op jit(solution)/shard_map/ppermute | solution.py:32
  42.3 15.4 %collective-permute-start.13 = (bf16[672,512]{1,0:T(8,128)(2,1)S(1)}, bf16[672,512]{1,0:T(8,128)(2,1)S(1)}, u32[]{:S(2)}, u32[]{:S(2)}) collective-permute-start(bf16[672,512]{1,0:T(8,128)(2,1)S(1)} %collective-permute-done.5.refs_0_), channel_id=1, source_target_pairs={{0,6},{1,7},{2,0},{3,1},{4,2},{5,3},{6,4},{7,5},{8,14},{9,15},{10,... | collective-permute-start | bytes 2064392 | tf_op jit(solution)/shard_map/ppermute | solution.py:32
  45.5 13.3 %collective-permute-start.14 = (bf16[672,512]{1,0:T(8,128)(2,1)S(1)}, bf16[672,512]{1,0:T(8,128)(2,1)S(1)}, u32[]{:S(2)}, u32[]{:S(2)}) collective-permute-start(bf16[672,512]{1,0:T(8,128)(2,1)S(1)} %collective-permute-done.2.refs_1_), channel_id=1, source_target_pairs={{0,32},{1,33},{2,34},{3,35},{4,36},{5,37},{6,38},{7,39},{8,40},{9,... | collective-permute-start | bytes 2064392 | tf_op jit(solution)/shard_map/ppermute | solution.py:32
  46.0 14.8 %collective-permute-start.15 = (bf16[672,512]{1,0:T(8,128)(2,1)S(1)}, bf16[672,512]{1,0:T(8,128)(2,1)S(1)}, u32[]{:S(2)}, u32[]{:S(2)}) collective-permute-start(bf16[672,512]{1,0:T(8,128)(2,1)S(1)} %collective-permute-done.2.refs_1_), channel_id=1, source_target_pairs={{0,96},{1,97},{2,98},{3,99},{4,100},{5,101},{6,102},{7,103},{8,104... | collective-permute-start | bytes 2064392 | tf_op jit(solution)/shard_map/ppermute | solution.py:32
  60.8 13.8 %collective-permute-start.16 = (bf16[672,512]{1,0:T(8,128)(2,1)S(1)}, bf16[672,512]{1,0:T(8,128)(2,1)S(1)}, u32[]{:S(2)}, u32[]{:S(2)}) collective-permute-start(bf16[672,512]{1,0:T(8,128)(2,1)S(1)} %collective-permute-done.12.refs_2_), channel_id=1, source_target_pairs={{0,2},{1,3},{2,4},{3,5},{4,6},{5,7},{6,0},{7,1},{8,10},{9,11},{10,... | collective-permute-start | bytes 2064392 | tf_op jit(solution)/shard_map/ppermute | solution.py:32
  60.8 19.1 %collective-permute-start.17 = (bf16[672,512]{1,0:T(8,128)(2,1)S(1)}, bf16[672,512]{1,0:T(8,128)(2,1)S(1)}, u32[]{:S(2)}, u32[]{:S(2)}) collective-permute-start(bf16[672,512]{1,0:T(8,128)(2,1)S(1)} %collective-permute-done.12.refs_2_), channel_id=1, source_target_pairs={{0,8},{1,9},{2,10},{3,11},{4,12},{5,13},{6,14},{7,15},{8,0},{9,1},... | collective-permute-start | bytes 2064392 | tf_op jit(solution)/shard_map/ppermute | solution.py:32
  61.1 19.7 %collective-permute-start.18 = (bf16[672,512]{1,0:T(8,128)(2,1)S(1)}, bf16[672,512]{1,0:T(8,128)(2,1)S(1)}, u32[]{:S(2)}, u32[]{:S(2)}) collective-permute-start(bf16[672,512]{1,0:T(8,128)(2,1)S(1)} %collective-permute-done.11.refs_1_), channel_id=1, source_target_pairs={{0,6},{1,7},{2,0},{3,1},{4,2},{5,3},{6,4},{7,5},{8,14},{9,15},{10,... | collective-permute-start | bytes 2064392 | tf_op jit(solution)/shard_map/ppermute | solution.py:32
  63.7 17.6 %collective-permute-start.19 = (bf16[672,512]{1,0:T(8,128)(2,1)S(1)}, bf16[672,512]{1,0:T(8,128)(2,1)S(1)}, u32[]{:S(2)}, u32[]{:S(2)}) collective-permute-start(bf16[672,512]{1,0:T(8,128)(2,1)S(1)} %collective-permute-done.3.refs_2_), channel_id=1, source_target_pairs={{0,32},{1,33},{2,34},{3,35},{4,36},{5,37},{6,38},{7,39},{8,40},{9,... | collective-permute-start | bytes 2064392 | tf_op jit(solution)/shard_map/ppermute | solution.py:32
  64.0 17.4 %collective-permute-start.20 = (bf16[672,512]{1,0:T(8,128)(2,1)S(1)}, bf16[672,512]{1,0:T(8,128)(2,1)S(1)}, u32[]{:S(2)}, u32[]{:S(2)}) collective-permute-start(bf16[672,512]{1,0:T(8,128)(2,1)S(1)} %collective-permute-done.15.refs_5_), channel_id=1, source_target_pairs={{0,96},{1,97},{2,98},{3,99},{4,100},{5,101},{6,102},{7,103},{8,104... | collective-permute-start | bytes 2064392 | tf_op jit(solution)/shard_map/ppermute | solution.py:32
  95.4 22.0 %collective-permute-start.28 = (bf16[256,1024]{1,0:T(8,128)(2,1)S(1)}, bf16[256,1024]{1,0:T(8,128)(2,1)S(1)}, u32[]{:S(2)}, u32[]{:S(2)}) collective-permute-start(bf16[256,1024]{1,0:T(8,128)(2,1)S(1)} %project_rest.2.kv.kv_ref), channel_id=1, source_target_pairs={{0,2},{1,3},{2,4},{3,5},{4,6},{5,7},{6,8},{7,9},{8,10},{9,11},{10,... | collective-permute-start | bytes 1572872 | tf_op jit(solution)/shard_map/ppermute | solution.py:462
  98.2 23.5 %collective-permute-start.33 = (bf16[672,256]{1,0:T(8,128)(2,1)S(1)}, bf16[672,256]{1,0:T(8,128)(2,1)}, u32[]{:S(2)}, u32[]{:S(2)}) collective-permute-start(bf16[672,256]{1,0:T(8,128)(2,1)S(1)} %bitcast.19), channel_id=1, source_target_pairs={{0,8},{1,9},{2,10},{3,11},{4,12},{5,13},{6,14},{7,15},{8,0},{9,1},... | collective-permute-start | bytes 1032200 | tf_op jit(solution)/shard_map/ppermute | solution.py:32
  119.7 12.9 %collective-permute-start.30 = (bf16[256,1024]{1,0:T(8,128)(2,1)S(1)}, bf16[256,1024]{1,0:T(8,128)(2,1)S(1)}, u32[]{:S(2)}, u32[]{:S(2)}) collective-permute-start(bf16[256,1024]{1,0:T(8,128)(2,1)S(1)} %attend_before.1.refs_0_), channel_id=1, source_target_pairs={{0,16},{1,17},{2,18},{3,19},{4,20},{5,21},{6,22},{7,23},{8,24},{9,... | collective-permute-start | bytes 1572872 | tf_op jit(solution)/shard_map/ppermute | solution.py:32
  132.7 14.1 %collective-permute-start.36 = (bf16[256,1024]{1,0:T(8,128)(2,1)S(1)}, bf16[256,1024]{1,0:T(8,128)(2,1)S(1)}, u32[]{:S(2)}, u32[]{:S(2)}) collective-permute-start(bf16[256,1024]{1,0:T(8,128)(2,1)S(1)} %collective-permute-done.31.refs_2_), channel_id=1, source_target_pairs={{0,32},{1,33},{2,34},{3,35},{4,36},{5,37},{6,38},{7,39},{8,40},{9,... | collective-permute-start | bytes 1572872 | tf_op jit(solution)/shard_map/ppermute | solution.py:32
  135.1 13.2 %collective-permute-start.37 = (bf16[256,1024]{1,0:T(8,128)(2,1)S(1)}, bf16[256,1024]{1,0:T(8,128)(2,1)S(1)}, u32[]{:S(2)}, u32[]{:S(2)}) collective-permute-start(bf16[256,1024]{1,0:T(8,128)(2,1)S(1)} %collective-permute-done.31.refs_2_), channel_id=1, source_target_pairs={{0,16},{1,17},{2,18},{3,19},{4,20},{5,21},{6,22},{7,23},{8,24},{9,... | collective-permute-start | bytes 1572872 | tf_op jit(solution)/shard_map/ppermute | solution.py:32
  138.1 13.6 %collective-permute-start.40 = (bf16[672,256]{1,0:T(8,128)(2,1)S(1)}, bf16[672,256]{1,0:T(8,128)(2,1)S(1)}, u32[]{:S(2)}, u32[]{:S(2)}) collective-permute-start(bf16[672,256]{1,0:T(8,128)(2,1)S(1)} %copy-done.5), channel_id=1, source_target_pairs={{0,6},{1,7},{2,0},{3,1},{4,2},{5,3},{6,4},{7,5},{8,14},{9,15},{10,... | collective-permute-start | bytes 1032200 | tf_op jit(solution)/shard_map/ppermute | solution.py:32
  (29 other events, 353.5 us)

commit v3 on v2

--- a/solution.py
+++ b/solution.py
@@ -428,11 +428,11 @@
         moved_q, moved_kv, block_z, block_r, block_l, out_block, cache
     )
     moved = turn_x(beside(moved_kv, moved_q))
-    out_r, out_l = shift_y(out_block, 1), shift_y(out_block, -1)
-    other = [swap_core(block), swap_core(block_z), swap_core(block_r)]
+    out_z, out_r, out_l = swap_zl(out_block), shift_y(out_block, 1), shift_y(out_block, -1)
+    other = [swap_core(block), swap_core(block_z)]
     cosine, sine = angles_of(start, 2 * rows)
-    moved, block_z, block_r, block_l, out_r, out_l, cosine, sine, *other = together(
-        moved, block_z, block_r, block_l, out_r, out_l, cosine, sine, *other
+    moved, block_z, block_r, block_l, out_z, out_r, out_l, cosine, sine, *other = together(
+        moved, block_z, block_r, block_l, out_z, out_r, out_l, cosine, sine, *other
     )
     moved_z = swap_zl(moved)
     moved_r, moved_l = shift_y(moved, 1), shift_y(moved, -1)
@@ -450,7 +450,7 @@
     last_kv, last_q = shift_y(half_zl, -1), shift_y(half_zr, 1)
     late = turn([moved_zr, moved_zl, moved_f])
     own = [block, block_z, block_r, block_l, block_zr, block_zl, block_f, block_zf]
-    other += [swap_core(b) for b in (block_l, block_zr, block_zl, block_f, block_zf)]
+    other += [swap_core(b) for b in (block_r, block_l, block_zr, block_zl, block_f, block_zf)]
     pairs = []
     for gx in range(8):
         head = 8 * (gx % 2) + 2 * (gx // 2)
@@ -462,20 +462,20 @@
     before = lax.ppermute(kv, "gy", [(i, i + 2) for i in range(14)])
     q = project_rest(project_q_kernel, last_q, kv, most, most_other, cosine, sine)
 
-    kv, q, out_block, out_r, out_l = together(kv, q, out_block, out_r, out_l)
-    out_z, out_f = swap_zl(out_block), shift_y(out_l, -1)
+    kv, q, out_z, out_l = together(kv, q, out_z, out_l)
+    out_f, out_zl = shift_y(out_l, -1), shift_y(out_z, -1)
     total, weight_sum = attend_own(q, kv)
     total, weight_sum, cached = together(total, weight_sum, cached)
     cached = cached.reshape(2 * rows, 2 * HD).T
     mixed = attend_before(q, before, cached, total, weight_sum)
 
+    mixed, out_z, out_zl = together(mixed, out_z, out_zl)
     mixed_z = swap_zh(mixed)
     mixed_r, mixed_l = shift_x(mixed, 1), shift_x(mixed, -1)
-    out_zr, out_zl = shift_y(out_z, 1), shift_y(out_z, -1)
-    mixed_z, mixed_r, mixed_l, out_zr, out_zl = together(mixed_z, mixed_r, mixed_l, out_zr, out_zl)
+    out_zr, out_zf = shift_y(out_z, 1), shift_y(out_zl, -1)
+    mixed_z, mixed_r, mixed_l, out_zr, out_zf = together(mixed_z, mixed_r, mixed_l, out_zr, out_zf)
     mixed_f, mixed_zl, mixed_zr = shift_x(mixed_r, 1), shift_x(mixed_z, -1), swap_zh(mixed_r)
-    out_zf = shift_y(out_zl, -1)
-    mixed_f, mixed_zr, mixed_zl, out_zf = together(mixed_f, mixed_zr, mixed_zl, out_zf)
+    mixed_f, mixed_zr, mixed_zl = together(mixed_f, mixed_zr, mixed_zl)
     low, high = halves(mixed_zr, mixed_zl)
     low, high = shift_x(low, 1), shift_x(high, -1)
     outs = [out_block, out_z, out_r, out_l, out_zr, out_zl, out_f, out_zf]

time: 166 us -> 165 us (level)
    ppermute x42, waiting for transfers between devices: 61.7 us -> 60 us  [move(): lax.ppermute(value, AXES, [(i, number(*to(*place(i)))) for i in range(128)])]
where the time goes in v3:
time: 165 us
  waiting for transfers between devices  73.5 us (45%)
  starting transfers between devices  64.1 us (39%)
  Pallas kernels  21.9 us (13%)
  local copies, waits for them, and re-layouts  3.22 us (2%)
    ppermute x42, starting transfers between devices, move(): lax.ppermute(value, AXES, [(i, number(*to(*place(i)))) for i in range(128)])  61.5 us
    ppermute x42, waiting for transfers between devices, move(): lax.ppermute(value, AXES, [(i, number(*to(*place(i)))) for i in range(128)])  60 us
    ppermute x1, waiting for transfers between devices, shards(): before = lax.ppermute(kv, 'gy', [(i, i + 2) for i in range(14)])  13.5 us
    pallas_call x2, Pallas kernels, project_most(): pl.pallas_call(project_most_kernel, out_shape=(jax.ShapeDtypeStruct((colu...  8.54 us
    pallas_call x1, Pallas kernels, out_most(): pl.pallas_call(out_most_kernel, out_shape=(jax.ShapeDtypeStruct((2, width...  4.04 us
  transfers between devices with their start and end apart: 44, of which 19 were waited for; matrix products, arithmetic and copies ran while one was open for 1% of the time, Pallas kernels for 13%

profile of v3, /device:TPU:39, one launch (start us, length us, event | category | flops | bytes accessed | tf_op | source)
XLA Modules:
  0.0 164.7 jit_solution(4635505430168193361)
XLA Ops:
  1.1 2.8 %collective-permute-start.2 = (bf16[672,512]{1,0:T(8,128)(2,1)}, bf16[672,512]{1,0:T(8,128)(2,1)S(1)}, u32[]{:S(2)}, u32[]{:S(2)}) collective-permute-start(bf16[672,512]{1,0:T(8,128)(2,1)} %bitcast.12), channel_id=1, source_target_pairs={{0,16},{1,17},{2,18},{3,19},{4,20},{5,21},{6,22},{7,23},{8,24},{9,... | collective-permute-start | bytes 2064392 | tf_op jit(solution)/shard_map/ppermute | solution.py:32
  5.3 4.6 %collective-permute-start = (bf16[672,256]{1,0:T(8,128)(2,1)}, bf16[672,256]{1,0:T(8,128)(2,1)S(1)}, u32[]{:S(2)}, u32[]{:S(2)}) collective-permute-start(bf16[672,256]{1,0:T(8,128)(2,1)} %param.9), channel_id=1, source_target_pairs={{0,0},{1,1},{2,2},{3,3},{4,4},{5,5},{6,6},{7,7},{8,8},{9,9},{10,10... | collective-permute-start | bytes 1032200 | tf_op jit(solution)/shard_map/ppermute | solution.py:32
  10.0 2.4 %collective-permute-start.1 = (bf16[672,256]{1,0:T(8,128)(2,1)S(1)}, bf16[672,256]{1,0:T(8,128)(2,1)S(1)}, u32[]{:S(2)}, u32[]{:S(2)}) collective-permute-start(bf16[672,256]{1,0:T(8,128)(2,1)S(1)} %bitcast.22), channel_id=1, source_target_pairs={{0,0},{1,1},{2,2},{3,3},{4,4},{5,5},{6,6},{7,7},{8,8},{9,9},{10,10... | collective-permute-start | bytes 1032200 | tf_op jit(solution)/shard_map/ppermute | solution.py:32
  12.4 3.7 %collective-permute-done.right = bf16[672,256]{1,0:T(8,128)(2,1)S(1)} collective-permute-done((bf16[672,256]{1,0:T(8,128)(2,1)}, bf16[672,256]{1,0:T(8,128)(2,1)S(1)}, u32[]{:S(2)}, u32[]{:S(2)}) %collective-permute-start) | collective-permute-done | bytes 344096 | tf_op jit(solution)/shard_map/ppermute | solution.py:32
  16.1 4.5 %collective-permute-start.9 = (bf16[672,512]{1,0:T(8,128)(2,1)}, bf16[672,512]{1,0:T(8,128)(2,1)S(1)}, u32[]{:S(2)}, u32[]{:S(2)}) collective-permute-start(bf16[672,512]{1,0:T(8,128)(2,1)} %bitcast.15), channel_id=1, source_target_pairs={{0,1},{1,0},{2,3},{3,2},{4,5},{5,4},{6,7},{7,6},{8,9},{9,8},{10,11... | collective-permute-start | bytes 2064392 | tf_op jit(solution)/shard_map/ppermute | solution.py:32
  20.6 2.8 %collective-permute-done.1.left = bf16[672,256]{1,0:T(8,128)(2,1)S(1)} collective-permute-done((bf16[672,256]{1,0:T(8,128)(2,1)S(1)}, bf16[672,256]{1,0:T(8,128)(2,1)S(1)}, u32[]{:S(2)}, u32[]{:S(2)}) %collective-permute-start.1) | collective-permute-done | bytes 344096 | tf_op jit(solution)/shard_map/ppermute | solution.py:32
  23.4 2.9 %collective-permute-start.5 = (bf16[672,512]{1,0:T(8,128)(2,1)S(1)}, bf16[672,512]{1,0:T(8,128)(2,1)S(1)}, u32[]{:S(2)}, u32[]{:S(2)}) collective-permute-start(bf16[672,512]{1,0:T(8,128)(2,1)S(1)} %small.6), channel_id=1, source_target_pairs={{0,0},{1,1},{2,34},{3,35},{4,68},{5,69},{6,102},{7,103},{8,16},{9,... | collective-permute-start | bytes 2064392 | tf_op jit(solution)/shard_map/ppermute | solution.py:32
  26.3 2.4 %collective-permute-start.10 = (bf16[672,512]{1,0:T(8,128)(2,1)S(1)}, bf16[672,512]{1,0:T(8,128)(2,1)S(1)}, u32[]{:S(2)}, u32[]{:S(2)}) collective-permute-start(bf16[672,512]{1,0:T(8,128)(2,1)S(1)} %collective-permute-done.2.refs_1_), channel_id=1, source_target_pairs={{0,1},{1,0},{2,3},{3,2},{4,5},{5,4},{6,7},{7,6},{8,9},{9,8},{10,11... | collective-permute-start | bytes 2064392 | tf_op jit(solution)/shard_map/ppermute | solution.py:32
  35.1 4.1 %collective-permute-done.6.refs_8_ = bf16[672,256]{1,0:T(8,128)(2,1)} collective-permute-done((bf16[672,256]{1,0:T(8,128)(2,1)S(1)}, bf16[672,256]{1,0:T(8,128)(2,1)}, u32[]{:S(2)}, u32[]{:S(2)}) %collective-permute-start.6) | collective-permute-done | bytes 344096 | tf_op jit(solution)/shard_map/ppermute | solution.py:32
  42.3 3.2 %collective-permute-start.13 = (bf16[672,512]{1,0:T(8,128)(2,1)S(1)}, bf16[672,512]{1,0:T(8,128)(2,1)S(1)}, u32[]{:S(2)}, u32[]{:S(2)}) collective-permute-start(bf16[672,512]{1,0:T(8,128)(2,1)S(1)} %collective-permute-done.5.refs_0_), channel_id=1, source_target_pairs={{0,6},{1,7},{2,0},{3,1},{4,2},{5,3},{6,4},{7,5},{8,14},{9,15},{10,... | collective-permute-start | bytes 2064392 | tf_op jit(solution)/shard_map/ppermute | solution.py:32
  46.9 8.9 %collective-permute-done.11.refs_1_ = bf16[672,512]{1,0:T(8,128)(2,1)S(1)} collective-permute-done((bf16[672,512]{1,0:T(8,128)(2,1)S(1)}, bf16[672,512]{1,0:T(8,128)(2,1)S(1)}, u32[]{:S(2)}, u32[]{:S(2)}) %collective-permute-start.11) | collective-permute-done | bytes 688160 | tf_op jit(solution)/shard_map/ppermute | solution.py:32
  58.7 2.6 %collective-permute-done.15.refs_5_ = bf16[672,512]{1,0:T(8,128)(2,1)S(1)} collective-permute-done((bf16[672,512]{1,0:T(8,128)(2,1)S(1)}, bf16[672,512]{1,0:T(8,128)(2,1)S(1)}, u32[]{:S(2)}, u32[]{:S(2)}) %collective-permute-start.15) | collective-permute-done | bytes 688160 | tf_op jit(solution)/shard_map/ppermute | solution.py:32
  66.5 8.8 %collective-permute-done.16.refs_2_ = bf16[672,512]{1,0:T(8,128)(2,1)S(1)} collective-permute-done((bf16[672,512]{1,0:T(8,128)(2,1)S(1)}, bf16[672,512]{1,0:T(8,128)(2,1)S(1)}, u32[]{:S(2)}, u32[]{:S(2)}) %collective-permute-start.16) | collective-permute-done | bytes 688160 | tf_op jit(solution)/shard_map/ppermute | solution.py:32
  75.3 5.0 %collective-permute-start.23 = (bf16[672,512]{1,0:T(8,128)(2,1)S(1)}, bf16[672,512]{1,0:T(8,128)(2,1)S(1)}, u32[]{:S(2)}, u32[]{:S(2)}) collective-permute-start(bf16[672,512]{1,0:T(8,128)(2,1)S(1)} %collective-permute-done.3.refs_2_), channel_id=1, source_target_pairs={{0,1},{1,0},{2,3},{3,2},{4,5},{5,4},{6,7},{7,6},{8,9},{9,8},{10,11... | collective-permute-start | bytes 2064392 | tf_op jit(solution)/shard_map/ppermute | solution.py:32
  86.7 4.4 %project_most.2 = (f32[512,512]{1,0:T(8,128)S(1)}, bf16[672,512]{1,0:T(8,128)(2,1)S(1)}) custom-call(bf16[672,512]{1,0:T(8,128)(2,1)S(1)} %bitcast.16, bf16[672,512]{1,0:T(8,128)(2,1)S(1)} %collective-permute-done.2.refs_1_, bf16[672,512]{1,0:T(8,128)(2,1)S(1)} %collective-permute-done.3.refs_2_, bf16[672,512]{1,0:T(8,128)(2,1)S(1)} %collective-permute-done.4.refs_3_, ...), custom_call_target="tpu_custom_call" | custom-call | flops 2466250752 | bytes 15728640 | tf_op jit(solution)/shard_map/project_most/pallas_call | solution.py:171
  91.8 4.2 %project_most.3 = (f32[512,512]{1,0:T(8,128)S(1)}, bf16[672,512]{1,0:T(8,128)(2,1)S(1)}) custom-call(bf16[672,512]{1,0:T(8,128)(2,1)S(1)} %collective-permute-done.9.refs_0_, bf16[672,512]{1,0:T(8,128)(2,1)S(1)} %collective-permute-done.10.refs_1_, bf16[672,512]{1,0:T(8,128)(2,1)S(1)} %collective-permute-done.23.refs_2_, ...), custom_call_target="tpu_custom_call" | custom-call | flops 2466250752 | bytes 15728640 | tf_op jit(solution)/shard_map/project_most/pallas_call | solution.py:171
  106.0 13.5 %collective-permute-done.29.sent_ref = bf16[256,1024]{1,0:T(8,128)(2,1)S(1)} collective-permute-done((bf16[256,1024]{1,0:T(8,128)(2,1)S(1)}, bf16[256,1024]{1,0:T(8,128)(2,1)S(1)}, u32[]{:S(2)}, u32[]{:S(2)}) %collective-permute-start.29) | collective-permute-done | bytes 524320 | tf_op jit(solution)/shard_map/ppermute | solution.py:462
  123.4 2.7 %collective-permute-start.36 = (bf16[672,256]{1,0:T(8,128)(2,1)}, bf16[672,256]{1,0:T(8,128)(2,1)S(1)}, u32[]{:S(2)}, u32[]{:S(2)}) collective-permute-start(bf16[672,256]{1,0:T(8,128)(2,1)} %collective-permute-done.31.refs_12_), channel_id=1, source_target_pairs={{0,6},{1,7},{2,0},{3,1},{4,2},{5,3},{6,4},{7,5},{8,14},{9,15},{10,... | collective-permute-start | bytes 1032200 | tf_op jit(solution)/shard_map/ppermute | solution.py:32
  126.1 6.4 %collective-permute-done.35.refs_11_ = bf16[672,256]{1,0:T(8,128)(2,1)S(1)} collective-permute-done((bf16[672,256]{1,0:T(8,128)(2,1)}, bf16[672,256]{1,0:T(8,128)(2,1)S(1)}, u32[]{:S(2)}, u32[]{:S(2)}) %collective-permute-start.35) | collective-permute-done | bytes 344096 | tf_op jit(solution)/shard_map/ppermute | solution.py:32
  132.5 3.0 %collective-permute-done.32.refs_1_ = bf16[256,1024]{1,0:T(8,128)(2,1)S(1)} collective-permute-done((bf16[256,1024]{1,0:T(8,128)(2,1)S(1)}, bf16[256,1024]{1,0:T(8,128)(2,1)S(1)}, u32[]{:S(2)}, u32[]{:S(2)}) %collective-permute-start.32) | collective-permute-done | bytes 524320 | tf_op jit(solution)/shard_map/ppermute | solution.py:32
  135.6 2.6 %collective-permute-start.38 = (bf16[256,1024]{1,0:T(8,128)(2,1)S(1)}, bf16[256,1024]{1,0:T(8,128)(2,1)S(1)}, u32[]{:S(2)}, u32[]{:S(2)}) collective-permute-start(bf16[256,1024]{1,0:T(8,128)(2,1)S(1)} %collective-permute-done.33.refs_2_), channel_id=1, source_target_pairs={{0,16},{1,17},{2,18},{3,19},{4,20},{5,21},{6,22},{7,23},{8,24},{9,... | collective-permute-start | bytes 1572872 | tf_op jit(solution)/shard_map/ppermute | solution.py:32
  139.3 7.3 %collective-permute-done.37.refs_6_ = bf16[256,1024]{1,0:T(8,128)(2,1)S(1)} collective-permute-done((bf16[256,1024]{1,0:T(8,128)(2,1)S(1)}, bf16[256,1024]{1,0:T(8,128)(2,1)S(1)}, u32[]{:S(2)}, u32[]{:S(2)}) %collective-permute-start.37) | collective-permute-done | bytes 524320 | tf_op jit(solution)/shard_map/ppermute | solution.py:32
  151.5 4.0 %out_most.1 = (f32[2,672,512]{2,1,0:T(8,128)S(1)}, bf16[672,256]{1,0:T(8,128)(2,1)S(1)}) custom-call(bf16[256,1024]{1,0:T(8,128)(2,1)S(1)} %attend_before.1.refs_0_, bf16[256,1024]{1,0:T(8,128)(2,1)S(1)} %collective-permute-done.32.refs_1_, bf16[256,1024]{1,0:T(8,128)(2,1)S(1)} %collective-permute-done.33.refs_2_, ...), custom_call_target="tpu_custom_call" | custom-call | flops 1024 | bytes 1024 | tf_op jit(solution)/shard_map/out_most/pallas_call | solution.py:386
  156.9 5.0 %collective-permute-start.43 = (bf16[672,512]{1,0:T(8,128)(2,1)S(1)}, bf16[672,512]{1,0:T(8,128)(2,1)S(1)}, u32[]{:S(2)}, u32[]{:S(2)}) collective-permute-start(bf16[672,512]{1,0:T(8,128)(2,1)S(1)} %out_rest.3), channel_id=1, source_target_pairs={{0,1},{1,0},{2,3},{3,2},{4,5},{5,4},{6,7},{7,6},{8,9},{9,8},{10,11... | collective-permute-start | bytes 2064392 | tf_op jit(solution)/shard_map/ppermute | solution.py:32
  (100 shorter events, 52.1 us)
Async XLA Ops:
  1.1 22.3 %collective-permute-start.2 = (bf16[672,512]{1,0:T(8,128)(2,1)}, bf16[672,512]{1,0:T(8,128)(2,1)S(1)}, u32[]{:S(2)}, u32[]{:S(2)}) collective-permute-start(bf16[672,512]{1,0:T(8,128)(2,1)} %bitcast.12), channel_id=1, source_target_pairs={{0,16},{1,17},{2,18},{3,19},{4,20},{5,21},{6,22},{7,23},{8,24},{9,... | collective-permute-start | bytes 2064392 | tf_op jit(solution)/shard_map/ppermute | solution.py:32
  3.9 19.5 %collective-permute-start.3 = (bf16[672,512]{1,0:T(8,128)(2,1)}, bf16[672,512]{1,0:T(8,128)(2,1)S(1)}, u32[]{:S(2)}, u32[]{:S(2)}) collective-permute-start(bf16[672,512]{1,0:T(8,128)(2,1)} %bitcast.13), channel_id=1, source_target_pairs={{0,32},{1,33},{2,34},{3,35},{4,36},{5,37},{6,38},{7,39},{8,40},{9,... | collective-permute-start | bytes 2064392 | tf_op jit(solution)/shard_map/ppermute | solution.py:32
  4.1 19.3 %collective-permute-start.4 = (bf16[672,512]{1,0:T(8,128)(2,1)}, bf16[672,512]{1,0:T(8,128)(2,1)S(1)}, u32[]{:S(2)}, u32[]{:S(2)}) collective-permute-start(bf16[672,512]{1,0:T(8,128)(2,1)} %bitcast.14), channel_id=1, source_target_pairs={{0,96},{1,97},{2,98},{3,99},{4,100},{5,101},{6,102},{7,103},{8,104... | collective-permute-start | bytes 2064392 | tf_op jit(solution)/shard_map/ppermute | solution.py:32
  10.0 13.4 %collective-permute-start.1 = (bf16[672,256]{1,0:T(8,128)(2,1)S(1)}, bf16[672,256]{1,0:T(8,128)(2,1)S(1)}, u32[]{:S(2)}, u32[]{:S(2)}) collective-permute-start(bf16[672,256]{1,0:T(8,128)(2,1)S(1)} %bitcast.22), channel_id=1, source_target_pairs={{0,0},{1,1},{2,2},{3,3},{4,4},{5,5},{6,6},{7,7},{8,8},{9,9},{10,10... | collective-permute-start | bytes 1032200 | tf_op jit(solution)/shard_map/ppermute | solution.py:32
  16.1 15.6 %collective-permute-start.9 = (bf16[672,512]{1,0:T(8,128)(2,1)}, bf16[672,512]{1,0:T(8,128)(2,1)S(1)}, u32[]{:S(2)}, u32[]{:S(2)}) collective-permute-start(bf16[672,512]{1,0:T(8,128)(2,1)} %bitcast.15), channel_id=1, source_target_pairs={{0,1},{1,0},{2,3},{3,2},{4,5},{5,4},{6,7},{7,6},{8,9},{9,8},{10,11... | collective-permute-start | bytes 2064392 | tf_op jit(solution)/shard_map/ppermute | solution.py:32
  23.4 18.8 %collective-permute-start.5 = (bf16[672,512]{1,0:T(8,128)(2,1)S(1)}, bf16[672,512]{1,0:T(8,128)(2,1)S(1)}, u32[]{:S(2)}, u32[]{:S(2)}) collective-permute-start(bf16[672,512]{1,0:T(8,128)(2,1)S(1)} %small.6), channel_id=1, source_target_pairs={{0,0},{1,1},{2,34},{3,35},{4,68},{5,69},{6,102},{7,103},{8,16},{9,... | collective-permute-start | bytes 2064392 | tf_op jit(solution)/shard_map/ppermute | solution.py:32
  26.3 15.9 %collective-permute-start.10 = (bf16[672,512]{1,0:T(8,128)(2,1)S(1)}, bf16[672,512]{1,0:T(8,128)(2,1)S(1)}, u32[]{:S(2)}, u32[]{:S(2)}) collective-permute-start(bf16[672,512]{1,0:T(8,128)(2,1)S(1)} %collective-permute-done.2.refs_1_), channel_id=1, source_target_pairs={{0,1},{1,0},{2,3},{3,2},{4,5},{5,4},{6,7},{7,6},{8,9},{9,8},{10,11... | collective-permute-start | bytes 2064392 | tf_op jit(solution)/shard_map/ppermute | solution.py:32
  42.2 13.6 %collective-permute-start.11 = (bf16[672,512]{1,0:T(8,128)(2,1)S(1)}, bf16[672,512]{1,0:T(8,128)(2,1)S(1)}, u32[]{:S(2)}, u32[]{:S(2)}) collective-permute-start(bf16[672,512]{1,0:T(8,128)(2,1)S(1)} %collective-permute-done.5.refs_0_), channel_id=1, source_target_pairs={{0,8},{1,9},{2,10},{3,11},{4,12},{5,13},{6,14},{7,15},{8,0},{9,1},... | collective-permute-start | bytes 2064392 | tf_op jit(solution)/shard_map/ppermute | solution.py:32
  42.2 15.4 %collective-permute-start.12 = (bf16[672,512]{1,0:T(8,128)(2,1)S(1)}, bf16[672,512]{1,0:T(8,128)(2,1)S(1)}, u32[]{:S(2)}, u32[]{:S(2)}) collective-permute-start(bf16[672,512]{1,0:T(8,128)(2,1)S(1)} %collective-permute-done.5.refs_0_), channel_id=1, source_target_pairs={{0,2},{1,3},{2,4},{3,5},{4,6},{5,7},{6,0},{7,1},{8,10},{9,11},{10,... | collective-permute-start | bytes 2064392 | tf_op jit(solution)/shard_map/ppermute | solution.py:32
  42.3 15.4 %collective-permute-start.13 = (bf16[672,512]{1,0:T(8,128)(2,1)S(1)}, bf16[672,512]{1,0:T(8,128)(2,1)S(1)}, u32[]{:S(2)}, u32[]{:S(2)}) collective-permute-start(bf16[672,512]{1,0:T(8,128)(2,1)S(1)} %collective-permute-done.5.refs_0_), channel_id=1, source_target_pairs={{0,6},{1,7},{2,0},{3,1},{4,2},{5,3},{6,4},{7,5},{8,14},{9,15},{10,... | collective-permute-start | bytes 2064392 | tf_op jit(solution)/shard_map/ppermute | solution.py:32
  45.4 13.3 %collective-permute-start.14 = (bf16[672,512]{1,0:T(8,128)(2,1)S(1)}, bf16[672,512]{1,0:T(8,128)(2,1)S(1)}, u32[]{:S(2)}, u32[]{:S(2)}) collective-permute-start(bf16[672,512]{1,0:T(8,128)(2,1)S(1)} %collective-permute-done.2.refs_1_), channel_id=1, source_target_pairs={{0,32},{1,33},{2,34},{3,35},{4,36},{5,37},{6,38},{7,39},{8,40},{9,... | collective-permute-start | bytes 2064392 | tf_op jit(solution)/shard_map/ppermute | solution.py:32
  46.3 15.0 %collective-permute-start.15 = (bf16[672,512]{1,0:T(8,128)(2,1)S(1)}, bf16[672,512]{1,0:T(8,128)(2,1)S(1)}, u32[]{:S(2)}, u32[]{:S(2)}) collective-permute-start(bf16[672,512]{1,0:T(8,128)(2,1)S(1)} %collective-permute-done.2.refs_1_), channel_id=1, source_target_pairs={{0,96},{1,97},{2,98},{3,99},{4,100},{5,101},{6,102},{7,103},{8,104... | collective-permute-start | bytes 2064392 | tf_op jit(solution)/shard_map/ppermute | solution.py:32
  61.3 14.1 %collective-permute-start.16 = (bf16[672,512]{1,0:T(8,128)(2,1)S(1)}, bf16[672,512]{1,0:T(8,128)(2,1)S(1)}, u32[]{:S(2)}, u32[]{:S(2)}) collective-permute-start(bf16[672,512]{1,0:T(8,128)(2,1)S(1)} %collective-permute-done.12.refs_2_), channel_id=1, source_target_pairs={{0,2},{1,3},{2,4},{3,5},{4,6},{5,7},{6,0},{7,1},{8,10},{9,11},{10,... | collective-permute-start | bytes 2064392 | tf_op jit(solution)/shard_map/ppermute | solution.py:32
  61.3 19.1 %collective-permute-start.17 = (bf16[672,512]{1,0:T(8,128)(2,1)S(1)}, bf16[672,512]{1,0:T(8,128)(2,1)S(1)}, u32[]{:S(2)}, u32[]{:S(2)}) collective-permute-start(bf16[672,512]{1,0:T(8,128)(2,1)S(1)} %collective-permute-done.12.refs_2_), channel_id=1, source_target_pairs={{0,8},{1,9},{2,10},{3,11},{4,12},{5,13},{6,14},{7,15},{8,0},{9,1},... | collective-permute-start | bytes 2064392 | tf_op jit(solution)/shard_map/ppermute | solution.py:32
  62.9 17.4 %collective-permute-start.18 = (bf16[672,512]{1,0:T(8,128)(2,1)S(1)}, bf16[672,512]{1,0:T(8,128)(2,1)S(1)}, u32[]{:S(2)}, u32[]{:S(2)}) collective-permute-start(bf16[672,512]{1,0:T(8,128)(2,1)S(1)} %collective-permute-done.11.refs_1_), channel_id=1, source_target_pairs={{0,6},{1,7},{2,0},{3,1},{4,2},{5,3},{6,4},{7,5},{8,14},{9,15},{10,... | collective-permute-start | bytes 2064392 | tf_op jit(solution)/shard_map/ppermute | solution.py:32
  65.0 16.7 %collective-permute-start.19 = (bf16[672,512]{1,0:T(8,128)(2,1)S(1)}, bf16[672,512]{1,0:T(8,128)(2,1)S(1)}, u32[]{:S(2)}, u32[]{:S(2)}) collective-permute-start(bf16[672,512]{1,0:T(8,128)(2,1)S(1)} %collective-permute-done.3.refs_2_), channel_id=1, source_target_pairs={{0,32},{1,33},{2,34},{3,35},{4,36},{5,37},{6,38},{7,39},{8,40},{9,... | collective-permute-start | bytes 2064392 | tf_op jit(solution)/shard_map/ppermute | solution.py:32
  65.3 17.6 %collective-permute-start.20 = (bf16[672,512]{1,0:T(8,128)(2,1)S(1)}, bf16[672,512]{1,0:T(8,128)(2,1)S(1)}, u32[]{:S(2)}, u32[]{:S(2)}) collective-permute-start(bf16[672,512]{1,0:T(8,128)(2,1)S(1)} %collective-permute-done.15.refs_5_), channel_id=1, source_target_pairs={{0,96},{1,97},{2,98},{3,99},{4,100},{5,101},{6,102},{7,103},{8,104... | collective-permute-start | bytes 2064392 | tf_op jit(solution)/shard_map/ppermute | solution.py:32
  91.1 12.8 %collective-permute-start.30 = (bf16[1024,2,128]{2,1,0:T(2,128)(2,1)S(1)}, bf16[1024,2,128]{2,1,0:T(2,128)(2,1)S(1)}, u32[]{:S(2)}, u32[]{:S(2)}) collective-permute-start(bf16[1024,2,128]{2,1,0:T(2,128)(2,1)S(1)} %copy-done.8), channel_id=1, source_target_pairs={{0,0},{1,1},{24,16},{25,17},{34,32},{35,33},{58,48},{59,49},{68,64... | collective-permute-start | bytes 1572872 | tf_op jit(solution)/shard_map/ppermute | solution.py:458
  97.3 22.2 %collective-permute-start.29 = (bf16[256,1024]{1,0:T(8,128)(2,1)S(1)}, bf16[256,1024]{1,0:T(8,128)(2,1)S(1)}, u32[]{:S(2)}, u32[]{:S(2)}) collective-permute-start(bf16[256,1024]{1,0:T(8,128)(2,1)S(1)} %project_rest.2.kv.kv_ref), channel_id=1, source_target_pairs={{0,2},{1,3},{2,4},{3,5},{4,6},{5,7},{6,8},{7,9},{8,10},{9,11},{10,... | collective-permute-start | bytes 1572872 | tf_op jit(solution)/shard_map/ppermute | solution.py:462
  100.1 21.7 %collective-permute-start.31 = (bf16[672,256]{1,0:T(8,128)(2,1)}, bf16[672,256]{1,0:T(8,128)(2,1)}, u32[]{:S(2)}, u32[]{:S(2)}) collective-permute-start(bf16[672,256]{1,0:T(8,128)(2,1)} %collective-permute-done.6.refs_8_), channel_id=1, source_target_pairs={{0,6},{1,7},{2,0},{3,1},{4,2},{5,3},{6,4},{7,5},{8,14},{9,15},{10,... | collective-permute-start | bytes 1032200 | tf_op jit(solution)/shard_map/ppermute | solution.py:32
  121.8 13.7 %collective-permute-start.32 = (bf16[256,1024]{1,0:T(8,128)(2,1)S(1)}, bf16[256,1024]{1,0:T(8,128)(2,1)S(1)}, u32[]{:S(2)}, u32[]{:S(2)}) collective-permute-start(bf16[256,1024]{1,0:T(8,128)(2,1)S(1)} %attend_before.1.refs_0_), channel_id=1, source_target_pairs={{0,16},{1,17},{2,18},{3,19},{4,20},{5,21},{6,22},{7,23},{8,24},{9,... | collective-permute-start | bytes 1572872 | tf_op jit(solution)/shard_map/ppermute | solution.py:32
  121.9 13.6 %collective-permute-start.33 = (bf16[256,1024]{1,0:T(8,128)(2,1)S(1)}, bf16[256,1024]{1,0:T(8,128)(2,1)S(1)}, u32[]{:S(2)}, u32[]{:S(2)}) collective-permute-start(bf16[256,1024]{1,0:T(8,128)(2,1)S(1)} %attend_before.1.refs_0_), channel_id=1, source_target_pairs={{0,32},{1,33},{2,34},{3,35},{4,36},{5,37},{6,38},{7,39},{8,40},{9,... | collective-permute-start | bytes 1572872 | tf_op jit(solution)/shard_map/ppermute | solution.py:32
  122.0 13.5 %collective-permute-start.34 = (bf16[256,1024]{1,0:T(8,128)(2,1)S(1)}, bf16[256,1024]{1,0:T(8,128)(2,1)S(1)}, u32[]{:S(2)}, u32[]{:S(2)}) collective-permute-start(bf16[256,1024]{1,0:T(8,128)(2,1)S(1)} %attend_before.1.refs_0_), channel_id=1, source_target_pairs={{0,96},{1,97},{2,98},{3,99},{4,100},{5,101},{6,102},{7,103},{8,104... | collective-permute-start | bytes 1572872 | tf_op jit(solution)/shard_map/ppermute | solution.py:32
  135.6 12.7 %collective-permute-start.38 = (bf16[256,1024]{1,0:T(8,128)(2,1)S(1)}, bf16[256,1024]{1,0:T(8,128)(2,1)S(1)}, u32[]{:S(2)}, u32[]{:S(2)}) collective-permute-start(bf16[256,1024]{1,0:T(8,128)(2,1)S(1)} %collective-permute-done.33.refs_2_), channel_id=1, source_target_pairs={{0,16},{1,17},{2,18},{3,19},{4,20},{5,21},{6,22},{7,23},{8,24},{9,... | collective-permute-start | bytes 1572872 | tf_op jit(solution)/shard_map/ppermute | solution.py:32
  (29 other events, 343.7 us)

commit v4 on v3

--- a/solution.py
+++ b/solution.py
@@ -421,13 +421,13 @@
     block = hidden.T
     out_block = w_out.T
 
-    moved_q, moved_kv = shear_y(w_query), shear_y(kv_weight)
+    moved = shear_y(beside(kv_weight, w_query))
     block_z = swap_zh(block)
     block_r, block_l = shift_x(block, 1), shift_x(block, -1)
-    moved_q, moved_kv, block_z, block_r, block_l, out_block, cache = together(
-        moved_q, moved_kv, block_z, block_r, block_l, out_block, cache
+    moved, block_z, block_r, block_l, out_block, cache = together(
+        moved, block_z, block_r, block_l, out_block, cache
     )
-    moved = turn_x(beside(moved_kv, moved_q))
+    moved = turn_x(moved)
     out_z, out_r, out_l = swap_zl(out_block), shift_y(out_block, 1), shift_y(out_block, -1)
     other = [swap_core(block), swap_core(block_z)]
     cosine, sine = angles_of(start, 2 * rows)

time: 165 us -> 167 us (1.012)
  waiting for transfers between devices: 73.5 us -> 78.7 us
  starting transfers between devices: 64.1 us -> 60.2 us
    ppermute x42 -> x41, waiting for transfers between devices: 60 us -> 65.3 us  [move(): lax.ppermute(value, AXES, [(i, number(*to(*place(i)))) for i in range(128)])]
    ppermute x42 -> x41, starting transfers between devices: 61.5 us -> 56.8 us  [move(): lax.ppermute(value, AXES, [(i, number(*to(*place(i)))) for i in range(128)])]
  transfers between devices with their start and end apart: 44 -> 43, of which waited for: 19 -> 20; matrix products, arithmetic and copies ran while one was open for 1% -> 1% of each run, Pallas kernels for 13% -> 13%
where the time goes in v4:
time: 167 us; the launch traced here: 166 us
  waiting for transfers between devices  78.7 us (47%)
  starting transfers between devices  60.2 us (36%)
  Pallas kernels  21.9 us (13%)
  local copies, waits for them, and re-layouts  3.41 us (2%)
    ppermute x41, waiting for transfers between devices, move(): lax.ppermute(value, AXES, [(i, number(*to(*place(i)))) for i in range(128)])  65.3 us
    ppermute x41, starting transfers between devices, move(): lax.ppermute(value, AXES, [(i, number(*to(*place(i)))) for i in range(128)])  56.8 us
    ppermute x1, waiting for transfers between devices, shards(): before = lax.ppermute(kv, 'gy', [(i, i + 2) for i in range(14)])  13.4 us
    pallas_call x2, Pallas kernels, project_most(): pl.pallas_call(project_most_kernel, out_shape=(jax.ShapeDtypeStruct((colu...  8.53 us
    pallas_call x1, Pallas kernels, out_most(): pl.pallas_call(out_most_kernel, out_shape=(jax.ShapeDtypeStruct((2, width...  4.04 us
  transfers between devices with their start and end apart: 43, of which 20 were waited for; matrix products, arithmetic and copies ran while one was open for 1% of the time, Pallas kernels for 13%

profile of v4, /device:TPU:39, one launch (start us, length us, event | category | flops | bytes accessed | tf_op | source)
XLA Modules:
  0.0 166.2 jit_solution(16938791645484932752)
XLA Ops:
  2.1 4.8 %collective-permute-start = (bf16[672,512]{1,0:T(8,128)(2,1)S(1)}, bf16[672,512]{1,0:T(8,128)(2,1)S(1)}, u32[]{:S(2)}, u32[]{:S(2)}) collective-permute-start(bf16[672,512]{1,0:T(8,128)(2,1)S(1)} %small.6), channel_id=1, source_target_pairs={{0,0},{1,1},{2,2},{3,3},{4,4},{5,5},{6,6},{7,7},{8,8},{9,9},{10,10... | collective-permute-start | bytes 2064392 | tf_op jit(solution)/shard_map/ppermute | solution.py:32
  6.9 2.8 %collective-permute-start.1 = (bf16[672,512]{1,0:T(8,128)(2,1)S(1)}, bf16[672,512]{1,0:T(8,128)(2,1)S(1)}, u32[]{:S(2)}, u32[]{:S(2)}) collective-permute-start(bf16[672,512]{1,0:T(8,128)(2,1)S(1)} %bitcast.13), channel_id=1, source_target_pairs={{0,16},{1,17},{2,18},{3,19},{4,20},{5,21},{6,22},{7,23},{8,24},{9,... | collective-permute-start | bytes 2064392 | tf_op jit(solution)/shard_map/ppermute | solution.py:32
  13.0 8.0 %collective-permute-done = bf16[672,512]{1,0:T(8,128)(2,1)S(1)} collective-permute-done((bf16[672,512]{1,0:T(8,128)(2,1)S(1)}, bf16[672,512]{1,0:T(8,128)(2,1)S(1)}, u32[]{:S(2)}, u32[]{:S(2)}) %collective-permute-start) | collective-permute-done | bytes 688160 | tf_op jit(solution)/shard_map/ppermute | solution.py:32
  21.0 3.5 %collective-permute-done.1.refs_1_ = bf16[672,512]{1,0:T(8,128)(2,1)S(1)} collective-permute-done((bf16[672,512]{1,0:T(8,128)(2,1)S(1)}, bf16[672,512]{1,0:T(8,128)(2,1)S(1)}, u32[]{:S(2)}, u32[]{:S(2)}) %collective-permute-start.1) | collective-permute-done | bytes 688160 | tf_op jit(solution)/shard_map/ppermute | solution.py:32
  28.6 2.5 %collective-permute-start.9 = (bf16[672,512]{1,0:T(8,128)(2,1)S(1)}, bf16[672,512]{1,0:T(8,128)(2,1)S(1)}, u32[]{:S(2)}, u32[]{:S(2)}) collective-permute-start(bf16[672,512]{1,0:T(8,128)(2,1)S(1)} %collective-permute-done.1.refs_1_), channel_id=1, source_target_pairs={{0,1},{1,0},{2,3},{3,2},{4,5},{5,4},{6,7},{7,6},{8,9},{9,8},{10,11... | collective-permute-start | bytes 2064392 | tf_op jit(solution)/shard_map/ppermute | solution.py:32
  33.1 2.7 %collective-permute-start.7 = (bf16[672,256]{1,0:T(8,128)(2,1)S(1)}, bf16[672,256]{1,0:T(8,128)(2,1)S(1)}, u32[]{:S(2)}, u32[]{:S(2)}) collective-permute-start(bf16[672,256]{1,0:T(8,128)(2,1)S(1)} %bitcast.20), channel_id=1, source_target_pairs={{0,6},{1,7},{2,0},{3,1},{4,2},{5,3},{6,4},{7,5},{8,14},{9,15},{10,... | collective-permute-start | bytes 1032200 | tf_op jit(solution)/shard_map/ppermute | solution.py:32
  37.4 4.1 %collective-permute-done.5.refs_8_ = bf16[672,256]{1,0:T(8,128)(2,1)} collective-permute-done((bf16[672,256]{1,0:T(8,128)(2,1)S(1)}, bf16[672,256]{1,0:T(8,128)(2,1)}, u32[]{:S(2)}, u32[]{:S(2)}) %collective-permute-start.5) | collective-permute-done | bytes 344096 | tf_op jit(solution)/shard_map/ppermute | solution.py:32
  45.7 2.7 %collective-permute-start.12 = (bf16[672,512]{1,0:T(8,128)(2,1)S(1)}, bf16[672,512]{1,0:T(8,128)(2,1)S(1)}, u32[]{:S(2)}, u32[]{:S(2)}) collective-permute-start(bf16[672,512]{1,0:T(8,128)(2,1)S(1)} %collective-permute-done.4.refs_0_), channel_id=1, source_target_pairs={{0,6},{1,7},{2,0},{3,1},{4,2},{5,3},{6,4},{7,5},{8,14},{9,15},{10,... | collective-permute-start | bytes 2064392 | tf_op jit(solution)/shard_map/ppermute | solution.py:32
  49.8 9.7 %collective-permute-done.10.refs_1_ = bf16[672,512]{1,0:T(8,128)(2,1)S(1)} collective-permute-done((bf16[672,512]{1,0:T(8,128)(2,1)S(1)}, bf16[672,512]{1,0:T(8,128)(2,1)S(1)}, u32[]{:S(2)}, u32[]{:S(2)}) %collective-permute-start.10) | collective-permute-done | bytes 688160 | tf_op jit(solution)/shard_map/ppermute | solution.py:32
  64.0 2.7 %collective-permute-start.17 = (bf16[672,512]{1,0:T(8,128)(2,1)S(1)}, bf16[672,512]{1,0:T(8,128)(2,1)S(1)}, u32[]{:S(2)}, u32[]{:S(2)}) collective-permute-start(bf16[672,512]{1,0:T(8,128)(2,1)S(1)} %collective-permute-done.10.refs_1_), channel_id=1, source_target_pairs={{0,6},{1,7},{2,0},{3,1},{4,2},{5,3},{6,4},{7,5},{8,14},{9,15},{10,... | collective-permute-start | bytes 2064392 | tf_op jit(solution)/shard_map/ppermute | solution.py:32
  68.2 8.0 %collective-permute-done.15.refs_2_ = bf16[672,512]{1,0:T(8,128)(2,1)S(1)} collective-permute-done((bf16[672,512]{1,0:T(8,128)(2,1)S(1)}, bf16[672,512]{1,0:T(8,128)(2,1)S(1)}, u32[]{:S(2)}, u32[]{:S(2)}) %collective-permute-start.15) | collective-permute-done | bytes 688160 | tf_op jit(solution)/shard_map/ppermute | solution.py:32
  76.2 5.6 %collective-permute-start.22 = (bf16[672,512]{1,0:T(8,128)(2,1)S(1)}, bf16[672,512]{1,0:T(8,128)(2,1)S(1)}, u32[]{:S(2)}, u32[]{:S(2)}) collective-permute-start(bf16[672,512]{1,0:T(8,128)(2,1)S(1)} %collective-permute-done.2.refs_2_), channel_id=1, source_target_pairs={{0,1},{1,0},{2,3},{3,2},{4,5},{5,4},{6,7},{7,6},{8,9},{9,8},{10,11... | collective-permute-start | bytes 2064392 | tf_op jit(solution)/shard_map/ppermute | solution.py:32
  88.3 4.4 %project_most.2 = (f32[512,512]{1,0:T(8,128)S(1)}, bf16[672,512]{1,0:T(8,128)(2,1)S(1)}) custom-call(bf16[672,512]{1,0:T(8,128)(2,1)S(1)} %bitcast.17, bf16[672,512]{1,0:T(8,128)(2,1)S(1)} %collective-permute-done.1.refs_1_, bf16[672,512]{1,0:T(8,128)(2,1)S(1)} %collective-permute-done.2.refs_2_, bf16[672,512]{1,0:T(8,128)(2,1)S(1)} %collective-permute-done.3.refs_3_, ...), custom_call_target="tpu_custom_call" | custom-call | flops 2466250752 | bytes 15728640 | tf_op jit(solution)/shard_map/project_most/pallas_call | solution.py:171
  94.2 4.2 %project_most.3 = (f32[512,512]{1,0:T(8,128)S(1)}, bf16[672,512]{1,0:T(8,128)(2,1)S(1)}) custom-call(bf16[672,512]{1,0:T(8,128)(2,1)S(1)} %collective-permute-done.8.refs_0_, bf16[672,512]{1,0:T(8,128)(2,1)S(1)} %collective-permute-done.9.refs_1_, bf16[672,512]{1,0:T(8,128)(2,1)S(1)} %collective-permute-done.22.refs_2_, ...), custom_call_target="tpu_custom_call" | custom-call | flops 2466250752 | bytes 15728640 | tf_op jit(solution)/shard_map/project_most/pallas_call | solution.py:171
  104.1 2.2 %attend_own.1 = (f32[256,1024]{1,0:T(8,128)S(1)}, f32[2,1024]{1,0:T(2,128)S(1)}) custom-call(bf16[256,1024]{1,0:T(8,128)(2,1)S(1)} %project_rest.3.q_ref, bf16[256,1024]{1,0:T(8,128)(2,1)S(1)} %project_rest.2.kv.kv_ref), custom_call_target="tpu_custom_call" | custom-call | flops 1024 | bytes 1024 | tf_op jit(solution)/shard_map/attend_own/pallas_call | solution.py:319
  107.6 13.4 %collective-permute-done.28.sent_ref = bf16[256,1024]{1,0:T(8,128)(2,1)S(1)} collective-permute-done((bf16[256,1024]{1,0:T(8,128)(2,1)S(1)}, bf16[256,1024]{1,0:T(8,128)(2,1)S(1)}, u32[]{:S(2)}, u32[]{:S(2)}) %collective-permute-start.28) | collective-permute-done | bytes 524320 | tf_op jit(solution)/shard_map/ppermute | solution.py:462
  121.0 2.3 %attend_before.1.refs_0_ = bf16[256,1024]{1,0:T(8,128)(2,1)S(1)} custom-call(bf16[256,1024]{1,0:T(8,128)(2,1)S(1)} %project_rest.3.q_ref, bf16[256,1024]{1,0:T(8,128)(2,1)S(1)} %collective-permute-done.28.sent_ref, bf16[256,1024]{1,0:T(8,128)(2,1)S(1)} %bitcast.11, f32[256,1024]{1,0:T(8,128)S(1)} %get-tuple-element.115.total_ref, ...), custom_call_target="tpu_custom_call" | custom-call | flops 1024 | bytes 1024 | tf_op jit(solution)/shard_map/attend_before/pallas_call | solution.py:334
  124.9 2.7 %collective-permute-start.35 = (bf16[672,256]{1,0:T(8,128)(2,1)}, bf16[672,256]{1,0:T(8,128)(2,1)S(1)}, u32[]{:S(2)}, u32[]{:S(2)}) collective-permute-start(bf16[672,256]{1,0:T(8,128)(2,1)} %collective-permute-done.30.refs_12_), channel_id=1, source_target_pairs={{0,6},{1,7},{2,0},{3,1},{4,2},{5,3},{6,4},{7,5},{8,14},{9,15},{10,... | collective-permute-start | bytes 1032200 | tf_op jit(solution)/shard_map/ppermute | solution.py:32
  127.6 6.4 %collective-permute-done.34.refs_11_ = bf16[672,256]{1,0:T(8,128)(2,1)S(1)} collective-permute-done((bf16[672,256]{1,0:T(8,128)(2,1)}, bf16[672,256]{1,0:T(8,128)(2,1)S(1)}, u32[]{:S(2)}, u32[]{:S(2)}) %collective-permute-start.34) | collective-permute-done | bytes 344096 | tf_op jit(solution)/shard_map/ppermute | solution.py:32
  134.0 3.0 %collective-permute-done.31.refs_1_ = bf16[256,1024]{1,0:T(8,128)(2,1)S(1)} collective-permute-done((bf16[256,1024]{1,0:T(8,128)(2,1)S(1)}, bf16[256,1024]{1,0:T(8,128)(2,1)S(1)}, u32[]{:S(2)}, u32[]{:S(2)}) %collective-permute-start.31) | collective-permute-done | bytes 524320 | tf_op jit(solution)/shard_map/ppermute | solution.py:32
  137.1 2.6 %collective-permute-start.37 = (bf16[256,1024]{1,0:T(8,128)(2,1)S(1)}, bf16[256,1024]{1,0:T(8,128)(2,1)S(1)}, u32[]{:S(2)}, u32[]{:S(2)}) collective-permute-start(bf16[256,1024]{1,0:T(8,128)(2,1)S(1)} %collective-permute-done.32.refs_2_), channel_id=1, source_target_pairs={{0,16},{1,17},{2,18},{3,19},{4,20},{5,21},{6,22},{7,23},{8,24},{9,... | collective-permute-start | bytes 1572872 | tf_op jit(solution)/shard_map/ppermute | solution.py:32
  140.9 7.3 %collective-permute-done.36.refs_6_ = bf16[256,1024]{1,0:T(8,128)(2,1)S(1)} collective-permute-done((bf16[256,1024]{1,0:T(8,128)(2,1)S(1)}, bf16[256,1024]{1,0:T(8,128)(2,1)S(1)}, u32[]{:S(2)}, u32[]{:S(2)}) %collective-permute-start.36) | collective-permute-done | bytes 524320 | tf_op jit(solution)/shard_map/ppermute | solution.py:32
  153.1 4.0 %out_most.1 = (f32[2,672,512]{2,1,0:T(8,128)S(1)}, bf16[672,256]{1,0:T(8,128)(2,1)S(1)}) custom-call(bf16[256,1024]{1,0:T(8,128)(2,1)S(1)} %attend_before.1.refs_0_, bf16[256,1024]{1,0:T(8,128)(2,1)S(1)} %collective-permute-done.31.refs_1_, bf16[256,1024]{1,0:T(8,128)(2,1)S(1)} %collective-permute-done.32.refs_2_, ...), custom_call_target="tpu_custom_call" | custom-call | flops 1024 | bytes 1024 | tf_op jit(solution)/shard_map/out_most/pallas_call | solution.py:386
  158.5 4.9 %collective-permute-start.42 = (bf16[672,512]{1,0:T(8,128)(2,1)S(1)}, bf16[672,512]{1,0:T(8,128)(2,1)S(1)}, u32[]{:S(2)}, u32[]{:S(2)}) collective-permute-start(bf16[672,512]{1,0:T(8,128)(2,1)S(1)} %out_rest.3), channel_id=1, source_target_pairs={{0,1},{1,0},{2,3},{3,2},{4,5},{5,4},{6,7},{7,6},{8,9},{9,8},{10,11... | collective-permute-start | bytes 2064392 | tf_op jit(solution)/shard_map/ppermute | solution.py:32
  (98 shorter events, 50.9 us)
Async XLA Ops:
  2.1 18.9 %collective-permute-start = (bf16[672,512]{1,0:T(8,128)(2,1)S(1)}, bf16[672,512]{1,0:T(8,128)(2,1)S(1)}, u32[]{:S(2)}, u32[]{:S(2)}) collective-permute-start(bf16[672,512]{1,0:T(8,128)(2,1)S(1)} %small.6), channel_id=1, source_target_pairs={{0,0},{1,1},{2,2},{3,3},{4,4},{5,5},{6,6},{7,7},{8,8},{9,9},{10,10... | collective-permute-start | bytes 2064392 | tf_op jit(solution)/shard_map/ppermute | solution.py:32
  6.9 17.6 %collective-permute-start.1 = (bf16[672,512]{1,0:T(8,128)(2,1)S(1)}, bf16[672,512]{1,0:T(8,128)(2,1)S(1)}, u32[]{:S(2)}, u32[]{:S(2)}) collective-permute-start(bf16[672,512]{1,0:T(8,128)(2,1)S(1)} %bitcast.13), channel_id=1, source_target_pairs={{0,16},{1,17},{2,18},{3,19},{4,20},{5,21},{6,22},{7,23},{8,24},{9,... | collective-permute-start | bytes 2064392 | tf_op jit(solution)/shard_map/ppermute | solution.py:32
  9.7 15.7 %collective-permute-start.2 = (bf16[672,512]{1,0:T(8,128)(2,1)S(1)}, bf16[672,512]{1,0:T(8,128)(2,1)S(1)}, u32[]{:S(2)}, u32[]{:S(2)}) collective-permute-start(bf16[672,512]{1,0:T(8,128)(2,1)S(1)} %bitcast.14), channel_id=1, source_target_pairs={{0,32},{1,33},{2,34},{3,35},{4,36},{5,37},{6,38},{7,39},{8,40},{9,... | collective-permute-start | bytes 2064392 | tf_op jit(solution)/shard_map/ppermute | solution.py:32
  9.7 16.9 %collective-permute-start.3 = (bf16[672,512]{1,0:T(8,128)(2,1)S(1)}, bf16[672,512]{1,0:T(8,128)(2,1)S(1)}, u32[]{:S(2)}, u32[]{:S(2)}) collective-permute-start(bf16[672,512]{1,0:T(8,128)(2,1)S(1)} %bitcast.15), channel_id=1, source_target_pairs={{0,96},{1,97},{2,98},{3,99},{4,100},{5,101},{6,102},{7,103},{8,104... | collective-permute-start | bytes 2064392 | tf_op jit(solution)/shard_map/ppermute | solution.py:32
  11.2 21.9 %collective-permute-start.8 = (bf16[672,512]{1,0:T(8,128)(2,1)S(1)}, bf16[672,512]{1,0:T(8,128)(2,1)S(1)}, u32[]{:S(2)}, u32[]{:S(2)}) collective-permute-start(bf16[672,512]{1,0:T(8,128)(2,1)S(1)} %bitcast.16), channel_id=1, source_target_pairs={{0,1},{1,0},{2,3},{3,2},{4,5},{5,4},{6,7},{7,6},{8,9},{9,8},{10,11... | collective-permute-start | bytes 2064392 | tf_op jit(solution)/shard_map/ppermute | solution.py:32
  26.6 19.1 %collective-permute-start.4 = (bf16[672,512]{1,0:T(8,128)(2,1)S(1)}, bf16[672,512]{1,0:T(8,128)(2,1)S(1)}, u32[]{:S(2)}, u32[]{:S(2)}) collective-permute-start(bf16[672,512]{1,0:T(8,128)(2,1)S(1)} %collective-permute-done), channel_id=1, source_target_pairs={{0,0},{1,1},{2,34},{3,35},{4,68},{5,69},{6,102},{7,103},{8,16},{9,... | collective-permute-start | bytes 2064392 | tf_op jit(solution)/shard_map/ppermute | solution.py:32
  28.6 17.1 %collective-permute-start.9 = (bf16[672,512]{1,0:T(8,128)(2,1)S(1)}, bf16[672,512]{1,0:T(8,128)(2,1)S(1)}, u32[]{:S(2)}, u32[]{:S(2)}) collective-permute-start(bf16[672,512]{1,0:T(8,128)(2,1)S(1)} %collective-permute-done.1.refs_1_), channel_id=1, source_target_pairs={{0,1},{1,0},{2,3},{3,2},{4,5},{5,4},{6,7},{7,6},{8,9},{9,8},{10,11... | collective-permute-start | bytes 2064392 | tf_op jit(solution)/shard_map/ppermute | solution.py:32
  45.7 13.8 %collective-permute-start.10 = (bf16[672,512]{1,0:T(8,128)(2,1)S(1)}, bf16[672,512]{1,0:T(8,128)(2,1)S(1)}, u32[]{:S(2)}, u32[]{:S(2)}) collective-permute-start(bf16[672,512]{1,0:T(8,128)(2,1)S(1)} %collective-permute-done.4.refs_0_), channel_id=1, source_target_pairs={{0,8},{1,9},{2,10},{3,11},{4,12},{5,13},{6,14},{7,15},{8,0},{9,1},... | collective-permute-start | bytes 2064392 | tf_op jit(solution)/shard_map/ppermute | solution.py:32
  45.7 14.9 %collective-permute-start.11 = (bf16[672,512]{1,0:T(8,128)(2,1)S(1)}, bf16[672,512]{1,0:T(8,128)(2,1)S(1)}, u32[]{:S(2)}, u32[]{:S(2)}) collective-permute-start(bf16[672,512]{1,0:T(8,128)(2,1)S(1)} %collective-permute-done.4.refs_0_), channel_id=1, source_target_pairs={{0,2},{1,3},{2,4},{3,5},{4,6},{5,7},{6,0},{7,1},{8,10},{9,11},{10,... | collective-permute-start | bytes 2064392 | tf_op jit(solution)/shard_map/ppermute | solution.py:32
  45.7 14.9 %collective-permute-start.12 = (bf16[672,512]{1,0:T(8,128)(2,1)S(1)}, bf16[672,512]{1,0:T(8,128)(2,1)S(1)}, u32[]{:S(2)}, u32[]{:S(2)}) collective-permute-start(bf16[672,512]{1,0:T(8,128)(2,1)S(1)} %collective-permute-done.4.refs_0_), channel_id=1, source_target_pairs={{0,6},{1,7},{2,0},{3,1},{4,2},{5,3},{6,4},{7,5},{8,14},{9,15},{10,... | collective-permute-start | bytes 2064392 | tf_op jit(solution)/shard_map/ppermute | solution.py:32
  48.4 13.2 %collective-permute-start.13 = (bf16[672,512]{1,0:T(8,128)(2,1)S(1)}, bf16[672,512]{1,0:T(8,128)(2,1)S(1)}, u32[]{:S(2)}, u32[]{:S(2)}) collective-permute-start(bf16[672,512]{1,0:T(8,128)(2,1)S(1)} %collective-permute-done.1.refs_1_), channel_id=1, source_target_pairs={{0,32},{1,33},{2,34},{3,35},{4,36},{5,37},{6,38},{7,39},{8,40},{9,... | collective-permute-start | bytes 2064392 | tf_op jit(solution)/shard_map/ppermute | solution.py:32
  48.4 14.4 %collective-permute-start.14 = (bf16[672,512]{1,0:T(8,128)(2,1)S(1)}, bf16[672,512]{1,0:T(8,128)(2,1)S(1)}, u32[]{:S(2)}, u32[]{:S(2)}) collective-permute-start(bf16[672,512]{1,0:T(8,128)(2,1)S(1)} %collective-permute-done.1.refs_1_), channel_id=1, source_target_pairs={{0,96},{1,97},{2,98},{3,99},{4,100},{5,101},{6,102},{7,103},{8,104... | collective-permute-start | bytes 2064392 | tf_op jit(solution)/shard_map/ppermute | solution.py:32
  62.7 13.5 %collective-permute-start.15 = (bf16[672,512]{1,0:T(8,128)(2,1)S(1)}, bf16[672,512]{1,0:T(8,128)(2,1)S(1)}, u32[]{:S(2)}, u32[]{:S(2)}) collective-permute-start(bf16[672,512]{1,0:T(8,128)(2,1)S(1)} %collective-permute-done.11.refs_2_), channel_id=1, source_target_pairs={{0,2},{1,3},{2,4},{3,5},{4,6},{5,7},{6,0},{7,1},{8,10},{9,11},{10,... | collective-permute-start | bytes 2064392 | tf_op jit(solution)/shard_map/ppermute | solution.py:32
  62.7 19.1 %collective-permute-start.16 = (bf16[672,512]{1,0:T(8,128)(2,1)S(1)}, bf16[672,512]{1,0:T(8,128)(2,1)S(1)}, u32[]{:S(2)}, u32[]{:S(2)}) collective-permute-start(bf16[672,512]{1,0:T(8,128)(2,1)S(1)} %collective-permute-done.11.refs_2_), channel_id=1, source_target_pairs={{0,8},{1,9},{2,10},{3,11},{4,12},{5,13},{6,14},{7,15},{8,0},{9,1},... | collective-permute-start | bytes 2064392 | tf_op jit(solution)/shard_map/ppermute | solution.py:32
  64.0 17.8 %collective-permute-start.17 = (bf16[672,512]{1,0:T(8,128)(2,1)S(1)}, bf16[672,512]{1,0:T(8,128)(2,1)S(1)}, u32[]{:S(2)}, u32[]{:S(2)}) collective-permute-start(bf16[672,512]{1,0:T(8,128)(2,1)S(1)} %collective-permute-done.10.refs_1_), channel_id=1, source_target_pairs={{0,6},{1,7},{2,0},{3,1},{4,2},{5,3},{6,4},{7,5},{8,14},{9,15},{10,... | collective-permute-start | bytes 2064392 | tf_op jit(solution)/shard_map/ppermute | solution.py:32
  66.7 16.5 %collective-permute-start.18 = (bf16[672,512]{1,0:T(8,128)(2,1)S(1)}, bf16[672,512]{1,0:T(8,128)(2,1)S(1)}, u32[]{:S(2)}, u32[]{:S(2)}) collective-permute-start(bf16[672,512]{1,0:T(8,128)(2,1)S(1)} %collective-permute-done.2.refs_2_), channel_id=1, source_target_pairs={{0,32},{1,33},{2,34},{3,35},{4,36},{5,37},{6,38},{7,39},{8,40},{9,... | collective-permute-start | bytes 2064392 | tf_op jit(solution)/shard_map/ppermute | solution.py:32
  67.0 17.6 %collective-permute-start.19 = (bf16[672,512]{1,0:T(8,128)(2,1)S(1)}, bf16[672,512]{1,0:T(8,128)(2,1)S(1)}, u32[]{:S(2)}, u32[]{:S(2)}) collective-permute-start(bf16[672,512]{1,0:T(8,128)(2,1)S(1)} %collective-permute-done.14.refs_5_), channel_id=1, source_target_pairs={{0,96},{1,97},{2,98},{3,99},{4,100},{5,101},{6,102},{7,103},{8,104... | collective-permute-start | bytes 2064392 | tf_op jit(solution)/shard_map/ppermute | solution.py:32
  92.7 13.6 %collective-permute-start.29 = (bf16[1024,2,128]{2,1,0:T(2,128)(2,1)S(1)}, bf16[1024,2,128]{2,1,0:T(2,128)(2,1)}, u32[]{:S(2)}, u32[]{:S(2)}) collective-permute-start(bf16[1024,2,128]{2,1,0:T(2,128)(2,1)S(1)} %copy-done.8), channel_id=1, source_target_pairs={{0,0},{1,1},{24,16},{25,17},{34,32},{35,33},{58,48},{59,49},{68,64... | collective-permute-start | bytes 1572872 | tf_op jit(solution)/shard_map/ppermute | solution.py:458
  99.1 21.9 %collective-permute-start.28 = (bf16[256,1024]{1,0:T(8,128)(2,1)S(1)}, bf16[256,1024]{1,0:T(8,128)(2,1)S(1)}, u32[]{:S(2)}, u32[]{:S(2)}) collective-permute-start(bf16[256,1024]{1,0:T(8,128)(2,1)S(1)} %project_rest.2.kv.kv_ref), channel_id=1, source_target_pairs={{0,2},{1,3},{2,4},{3,5},{4,6},{5,7},{6,8},{7,9},{8,10},{9,11},{10,... | collective-permute-start | bytes 1572872 | tf_op jit(solution)/shard_map/ppermute | solution.py:462
  101.9 21.4 %collective-permute-start.30 = (bf16[672,256]{1,0:T(8,128)(2,1)}, bf16[672,256]{1,0:T(8,128)(2,1)}, u32[]{:S(2)}, u32[]{:S(2)}) collective-permute-start(bf16[672,256]{1,0:T(8,128)(2,1)} %collective-permute-done.5.refs_8_), channel_id=1, source_target_pairs={{0,6},{1,7},{2,0},{3,1},{4,2},{5,3},{6,4},{7,5},{8,14},{9,15},{10,... | collective-permute-start | bytes 1032200 | tf_op jit(solution)/shard_map/ppermute | solution.py:32
  123.3 13.7 %collective-permute-start.31 = (bf16[256,1024]{1,0:T(8,128)(2,1)S(1)}, bf16[256,1024]{1,0:T(8,128)(2,1)S(1)}, u32[]{:S(2)}, u32[]{:S(2)}) collective-permute-start(bf16[256,1024]{1,0:T(8,128)(2,1)S(1)} %attend_before.1.refs_0_), channel_id=1, source_target_pairs={{0,16},{1,17},{2,18},{3,19},{4,20},{5,21},{6,22},{7,23},{8,24},{9,... | collective-permute-start | bytes 1572872 | tf_op jit(solution)/shard_map/ppermute | solution.py:32
  123.4 13.6 %collective-permute-start.32 = (bf16[256,1024]{1,0:T(8,128)(2,1)S(1)}, bf16[256,1024]{1,0:T(8,128)(2,1)S(1)}, u32[]{:S(2)}, u32[]{:S(2)}) collective-permute-start(bf16[256,1024]{1,0:T(8,128)(2,1)S(1)} %attend_before.1.refs_0_), channel_id=1, source_target_pairs={{0,32},{1,33},{2,34},{3,35},{4,36},{5,37},{6,38},{7,39},{8,40},{9,... | collective-permute-start | bytes 1572872 | tf_op jit(solution)/shard_map/ppermute | solution.py:32
  123.5 13.5 %collective-permute-start.33 = (bf16[256,1024]{1,0:T(8,128)(2,1)S(1)}, bf16[256,1024]{1,0:T(8,128)(2,1)S(1)}, u32[]{:S(2)}, u32[]{:S(2)}) collective-permute-start(bf16[256,1024]{1,0:T(8,128)(2,1)S(1)} %attend_before.1.refs_0_), channel_id=1, source_target_pairs={{0,96},{1,97},{2,98},{3,99},{4,100},{5,101},{6,102},{7,103},{8,104... | collective-permute-start | bytes 1572872 | tf_op jit(solution)/shard_map/ppermute | solution.py:32
  137.1 12.7 %collective-permute-start.37 = (bf16[256,1024]{1,0:T(8,128)(2,1)S(1)}, bf16[256,1024]{1,0:T(8,128)(2,1)S(1)}, u32[]{:S(2)}, u32[]{:S(2)}) collective-permute-start(bf16[256,1024]{1,0:T(8,128)(2,1)S(1)} %collective-permute-done.32.refs_2_), channel_id=1, source_target_pairs={{0,16},{1,17},{2,18},{3,19},{4,20},{5,21},{6,22},{7,23},{8,24},{9,... | collective-permute-start | bytes 1572872 | tf_op jit(solution)/shard_map/ppermute | solution.py:32
  (28 other events, 379.5 us)

commit v5 on v3

--- a/solution.py
+++ b/solution.py
@@ -429,7 +429,7 @@
     )
     moved = turn_x(beside(moved_kv, moved_q))
     out_z, out_r, out_l = swap_zl(out_block), shift_y(out_block, 1), shift_y(out_block, -1)
-    other = [swap_core(block), swap_core(block_z)]
+    other = [swap_core(block), swap_core(block_z), swap_core(block_r)]
     cosine, sine = angles_of(start, 2 * rows)
     moved, block_z, block_r, block_l, out_z, out_r, out_l, cosine, sine, *other = together(
         moved, block_z, block_r, block_l, out_z, out_r, out_l, cosine, sine, *other
@@ -450,7 +450,7 @@
     last_kv, last_q = shift_y(half_zl, -1), shift_y(half_zr, 1)
     late = turn([moved_zr, moved_zl, moved_f])
     own = [block, block_z, block_r, block_l, block_zr, block_zl, block_f, block_zf]
-    other += [swap_core(b) for b in (block_r, block_l, block_zr, block_zl, block_f, block_zf)]
+    other += [swap_core(b) for b in (block_l, block_zr, block_zl, block_f, block_zf)]
     pairs = []
     for gx in range(8):
         head = 8 * (gx % 2) + 2 * (gx // 2)

time: 165 us -> 164 us (level)
  waiting for transfers between devices: 73.5 us -> 68 us
  starting transfers between devices: 64.1 us -> 68.7 us
    ppermute x42, waiting for transfers between devices: 60 us -> 54.8 us  [move(): lax.ppermute(value, AXES, [(i, number(*to(*place(i)))) for i in range(128)])]
    ppermute x42, starting transfers between devices: 61.5 us -> 66 us  [move(): lax.ppermute(value, AXES, [(i, number(*to(*place(i)))) for i in range(128)])]
  transfers between devices with their start and end apart: 44 -> 44, of which waited for: 19 -> 18; matrix products, arithmetic and copies ran while one was open for 1% -> 1% of each run, Pallas kernels for 13% -> 13%
where the time goes in v5:
time: 164 us
  starting transfers between devices  68.7 us (42%)
  waiting for transfers between devices  68 us (41%)
  Pallas kernels  21.9 us (13%)
  local copies, waits for them, and re-layouts  3.22 us (2%)
    ppermute x42, starting transfers between devices, move(): lax.ppermute(value, AXES, [(i, number(*to(*place(i)))) for i in range(128)])  66 us
    ppermute x42, waiting for transfers between devices, move(): lax.ppermute(value, AXES, [(i, number(*to(*place(i)))) for i in range(128)])  54.8 us
    ppermute x1, waiting for transfers between devices, shards(): before = lax.ppermute(kv, 'gy', [(i, i + 2) for i in range(14)])  13.1 us
    pallas_call x2, Pallas kernels, project_most(): pl.pallas_call(project_most_kernel, out_shape=(jax.ShapeDtypeStruct((colu...  8.54 us
    pallas_call x1, Pallas kernels, out_most(): pl.pallas_call(out_most_kernel, out_shape=(jax.ShapeDtypeStruct((2, width...  4.04 us
  transfers between devices with their start and end apart: 44, of which 18 were waited for; matrix products, arithmetic and copies ran while one was open for 1% of the time, Pallas kernels for 13%

profile of v5, /device:TPU:39, one launch (start us, length us, event | category | flops | bytes accessed | tf_op | source)
XLA Modules:
  0.0 163.8 jit_solution(9104716670475473562)
XLA Ops:
  1.1 2.8 %collective-permute-start.2 = (bf16[672,512]{1,0:T(8,128)(2,1)}, bf16[672,512]{1,0:T(8,128)(2,1)S(1)}, u32[]{:S(2)}, u32[]{:S(2)}) collective-permute-start(bf16[672,512]{1,0:T(8,128)(2,1)} %bitcast.12), channel_id=1, source_target_pairs={{0,16},{1,17},{2,18},{3,19},{4,20},{5,21},{6,22},{7,23},{8,24},{9,... | collective-permute-start | bytes 2064392 | tf_op jit(solution)/shard_map/ppermute | solution.py:32
  5.3 4.6 %collective-permute-start = (bf16[672,256]{1,0:T(8,128)(2,1)}, bf16[672,256]{1,0:T(8,128)(2,1)S(1)}, u32[]{:S(2)}, u32[]{:S(2)}) collective-permute-start(bf16[672,256]{1,0:T(8,128)(2,1)} %param.9), channel_id=1, source_target_pairs={{0,0},{1,1},{2,2},{3,3},{4,4},{5,5},{6,6},{7,7},{8,8},{9,9},{10,10... | collective-permute-start | bytes 1032200 | tf_op jit(solution)/shard_map/ppermute | solution.py:32
  12.4 3.7 %collective-permute-done.right = bf16[672,256]{1,0:T(8,128)(2,1)S(1)} collective-permute-done((bf16[672,256]{1,0:T(8,128)(2,1)}, bf16[672,256]{1,0:T(8,128)(2,1)S(1)}, u32[]{:S(2)}, u32[]{:S(2)}) %collective-permute-start) | collective-permute-done | bytes 344096 | tf_op jit(solution)/shard_map/ppermute | solution.py:32
  16.1 4.5 %collective-permute-start.9 = (bf16[672,512]{1,0:T(8,128)(2,1)}, bf16[672,512]{1,0:T(8,128)(2,1)S(1)}, u32[]{:S(2)}, u32[]{:S(2)}) collective-permute-start(bf16[672,512]{1,0:T(8,128)(2,1)} %bitcast.15), channel_id=1, source_target_pairs={{0,1},{1,0},{2,3},{3,2},{4,5},{5,4},{6,7},{7,6},{8,9},{9,8},{10,11... | collective-permute-start | bytes 2064392 | tf_op jit(solution)/shard_map/ppermute | solution.py:32
  20.6 2.8 %collective-permute-done.1.left = bf16[672,256]{1,0:T(8,128)(2,1)S(1)} collective-permute-done((bf16[672,256]{1,0:T(8,128)(2,1)S(1)}, bf16[672,256]{1,0:T(8,128)(2,1)S(1)}, u32[]{:S(2)}, u32[]{:S(2)}) %collective-permute-start.1) | collective-permute-done | bytes 344096 | tf_op jit(solution)/shard_map/ppermute | solution.py:32
  23.4 2.9 %collective-permute-start.5 = (bf16[672,512]{1,0:T(8,128)(2,1)S(1)}, bf16[672,512]{1,0:T(8,128)(2,1)S(1)}, u32[]{:S(2)}, u32[]{:S(2)}) collective-permute-start(bf16[672,512]{1,0:T(8,128)(2,1)S(1)} %small.6), channel_id=1, source_target_pairs={{0,0},{1,1},{2,34},{3,35},{4,68},{5,69},{6,102},{7,103},{8,16},{9,... | collective-permute-start | bytes 2064392 | tf_op jit(solution)/shard_map/ppermute | solution.py:32
  28.1 2.9 %collective-permute-start.10 = (bf16[672,512]{1,0:T(8,128)(2,1)S(1)}, bf16[672,512]{1,0:T(8,128)(2,1)S(1)}, u32[]{:S(2)}, u32[]{:S(2)}) collective-permute-start(bf16[672,512]{1,0:T(8,128)(2,1)S(1)} %collective-permute-done.2.refs_1_), channel_id=1, source_target_pairs={{0,1},{1,0},{2,3},{3,2},{4,5},{5,4},{6,7},{7,6},{8,9},{9,8},{10,11... | collective-permute-start | bytes 2064392 | tf_op jit(solution)/shard_map/ppermute | solution.py:32
  37.7 3.7 %collective-permute-done.7.refs_9_ = bf16[672,256]{1,0:T(8,128)(2,1)S(1)} collective-permute-done((bf16[672,256]{1,0:T(8,128)(2,1)S(1)}, bf16[672,256]{1,0:T(8,128)(2,1)S(1)}, u32[]{:S(2)}, u32[]{:S(2)}) %collective-permute-start.7) | collective-permute-done | bytes 344096 | tf_op jit(solution)/shard_map/ppermute | solution.py:32
  42.4 3.1 %collective-permute-start.14 = (bf16[672,512]{1,0:T(8,128)(2,1)S(1)}, bf16[672,512]{1,0:T(8,128)(2,1)S(1)}, u32[]{:S(2)}, u32[]{:S(2)}) collective-permute-start(bf16[672,512]{1,0:T(8,128)(2,1)S(1)} %collective-permute-done.5.refs_0_), channel_id=1, source_target_pairs={{0,6},{1,7},{2,0},{3,1},{4,2},{5,3},{6,4},{7,5},{8,14},{9,15},{10,... | collective-permute-start | bytes 2064392 | tf_op jit(solution)/shard_map/ppermute | solution.py:32
  47.0 8.8 %collective-permute-done.12.refs_1_ = bf16[672,512]{1,0:T(8,128)(2,1)S(1)} collective-permute-done((bf16[672,512]{1,0:T(8,128)(2,1)S(1)}, bf16[672,512]{1,0:T(8,128)(2,1)S(1)}, u32[]{:S(2)}, u32[]{:S(2)}) %collective-permute-start.12) | collective-permute-done | bytes 688160 | tf_op jit(solution)/shard_map/ppermute | solution.py:32
  60.7 2.7 %collective-permute-start.19 = (bf16[672,512]{1,0:T(8,128)(2,1)S(1)}, bf16[672,512]{1,0:T(8,128)(2,1)S(1)}, u32[]{:S(2)}, u32[]{:S(2)}) collective-permute-start(bf16[672,512]{1,0:T(8,128)(2,1)S(1)} %collective-permute-done.12.refs_1_), channel_id=1, source_target_pairs={{0,6},{1,7},{2,0},{3,1},{4,2},{5,3},{6,4},{7,5},{8,14},{9,15},{10,... | collective-permute-start | bytes 2064392 | tf_op jit(solution)/shard_map/ppermute | solution.py:32
  64.8 6.8 %collective-permute-done.17.refs_2_ = bf16[672,512]{1,0:T(8,128)(2,1)S(1)} collective-permute-done((bf16[672,512]{1,0:T(8,128)(2,1)S(1)}, bf16[672,512]{1,0:T(8,128)(2,1)S(1)}, u32[]{:S(2)}, u32[]{:S(2)}) %collective-permute-start.17) | collective-permute-done | bytes 688160 | tf_op jit(solution)/shard_map/ppermute | solution.py:32
  71.6 7.2 %collective-permute-start.24 = (bf16[672,512]{1,0:T(8,128)(2,1)S(1)}, bf16[672,512]{1,0:T(8,128)(2,1)S(1)}, u32[]{:S(2)}, u32[]{:S(2)}) collective-permute-start(bf16[672,512]{1,0:T(8,128)(2,1)S(1)} %collective-permute-done.4.refs_3_), channel_id=1, source_target_pairs={{0,1},{1,0},{2,3},{3,2},{4,5},{5,4},{6,7},{7,6},{8,9},{9,8},{10,11... | collective-permute-start | bytes 2064392 | tf_op jit(solution)/shard_map/ppermute | solution.py:32
  80.3 2.7 %collective-permute-start.27 = (bf16[672,512]{1,0:T(8,128)(2,1)S(1)}, bf16[672,512]{1,0:T(8,128)(2,1)S(1)}, u32[]{:S(2)}, u32[]{:S(2)}) collective-permute-start(bf16[672,512]{1,0:T(8,128)(2,1)S(1)} %collective-permute-done.20.refs_6_), channel_id=1, source_target_pairs={{0,1},{1,0},{2,3},{3,2},{4,5},{5,4},{6,7},{7,6},{8,9},{9,8},{10,11... | collective-permute-start | bytes 2064392 | tf_op jit(solution)/shard_map/ppermute | solution.py:32
  85.2 4.4 %project_most.2 = (f32[512,512]{1,0:T(8,128)S(1)}, bf16[672,512]{1,0:T(8,128)(2,1)S(1)}) custom-call(bf16[672,512]{1,0:T(8,128)(2,1)S(1)} %bitcast.16, bf16[672,512]{1,0:T(8,128)(2,1)S(1)} %collective-permute-done.2.refs_1_, bf16[672,512]{1,0:T(8,128)(2,1)S(1)} %collective-permute-done.3.refs_2_, bf16[672,512]{1,0:T(8,128)(2,1)S(1)} %collective-permute-done.4.refs_3_, ...), custom_call_target="tpu_custom_call" | custom-call | flops 2466250752 | bytes 15728640 | tf_op jit(solution)/shard_map/project_most/pallas_call | solution.py:171
  90.3 4.2 %project_most.3 = (f32[512,512]{1,0:T(8,128)S(1)}, bf16[672,512]{1,0:T(8,128)(2,1)S(1)}) custom-call(bf16[672,512]{1,0:T(8,128)(2,1)S(1)} %collective-permute-done.9.refs_0_, bf16[672,512]{1,0:T(8,128)(2,1)S(1)} %collective-permute-done.10.refs_1_, bf16[672,512]{1,0:T(8,128)(2,1)S(1)} %collective-permute-done.11.refs_2_, ...), custom_call_target="tpu_custom_call" | custom-call | flops 2466250752 | bytes 15728640 | tf_op jit(solution)/shard_map/project_most/pallas_call | solution.py:171
  103.4 13.1 %collective-permute-done.29.sent_ref = bf16[256,1024]{1,0:T(8,128)(2,1)S(1)} collective-permute-done((bf16[256,1024]{1,0:T(8,128)(2,1)S(1)}, bf16[256,1024]{1,0:T(8,128)(2,1)S(1)}, u32[]{:S(2)}, u32[]{:S(2)}) %collective-permute-start.29) | collective-permute-done | bytes 524320 | tf_op jit(solution)/shard_map/ppermute | solution.py:462
  121.1 2.7 %collective-permute-start.36 = (bf16[672,256]{1,0:T(8,128)(2,1)}, bf16[672,256]{1,0:T(8,128)(2,1)S(1)}, u32[]{:S(2)}, u32[]{:S(2)}) collective-permute-start(bf16[672,256]{1,0:T(8,128)(2,1)} %collective-permute-done.31.refs_12_), channel_id=1, source_target_pairs={{0,6},{1,7},{2,0},{3,1},{4,2},{5,3},{6,4},{7,5},{8,14},{9,15},{10,... | collective-permute-start | bytes 1032200 | tf_op jit(solution)/shard_map/ppermute | solution.py:32
  123.8 6.3 %collective-permute-done.35.refs_11_ = bf16[672,256]{1,0:T(8,128)(2,1)S(1)} collective-permute-done((bf16[672,256]{1,0:T(8,128)(2,1)}, bf16[672,256]{1,0:T(8,128)(2,1)S(1)}, u32[]{:S(2)}, u32[]{:S(2)}) %collective-permute-start.35) | collective-permute-done | bytes 344096 | tf_op jit(solution)/shard_map/ppermute | solution.py:32
  131.7 2.9 %collective-permute-start.37 = (bf16[256,1024]{1,0:T(8,128)(2,1)S(1)}, bf16[256,1024]{1,0:T(8,128)(2,1)S(1)}, u32[]{:S(2)}, u32[]{:S(2)}) collective-permute-start(bf16[256,1024]{1,0:T(8,128)(2,1)S(1)} %collective-permute-done.33.refs_2_), channel_id=1, source_target_pairs={{0,32},{1,33},{2,34},{3,35},{4,36},{5,37},{6,38},{7,39},{8,40},{9,... | collective-permute-start | bytes 1572872 | tf_op jit(solution)/shard_map/ppermute | solution.py:32
  134.5 2.6 %collective-permute-start.38 = (bf16[256,1024]{1,0:T(8,128)(2,1)S(1)}, bf16[256,1024]{1,0:T(8,128)(2,1)S(1)}, u32[]{:S(2)}, u32[]{:S(2)}) collective-permute-start(bf16[256,1024]{1,0:T(8,128)(2,1)S(1)} %collective-permute-done.33.refs_2_), channel_id=1, source_target_pairs={{0,16},{1,17},{2,18},{3,19},{4,20},{5,21},{6,22},{7,23},{8,24},{9,... | collective-permute-start | bytes 1572872 | tf_op jit(solution)/shard_map/ppermute | solution.py:32
  137.5 8.7 %collective-permute-done.37.refs_6_ = bf16[256,1024]{1,0:T(8,128)(2,1)S(1)} collective-permute-done((bf16[256,1024]{1,0:T(8,128)(2,1)S(1)}, bf16[256,1024]{1,0:T(8,128)(2,1)S(1)}, u32[]{:S(2)}, u32[]{:S(2)}) %collective-permute-start.37) | collective-permute-done | bytes 524320 | tf_op jit(solution)/shard_map/ppermute | solution.py:32
  151.0 4.0 %out_most.1 = (f32[2,672,512]{2,1,0:T(8,128)S(1)}, bf16[672,256]{1,0:T(8,128)(2,1)S(1)}) custom-call(bf16[256,1024]{1,0:T(8,128)(2,1)S(1)} %attend_before.1.refs_0_, bf16[256,1024]{1,0:T(8,128)(2,1)S(1)} %collective-permute-done.32.refs_1_, bf16[256,1024]{1,0:T(8,128)(2,1)S(1)} %collective-permute-done.33.refs_2_, ...), custom_call_target="tpu_custom_call" | custom-call | flops 1024 | bytes 1024 | tf_op jit(solution)/shard_map/out_most/pallas_call | solution.py:386
  156.4 4.6 %collective-permute-start.43 = (bf16[672,512]{1,0:T(8,128)(2,1)S(1)}, bf16[672,512]{1,0:T(8,128)(2,1)S(1)}, u32[]{:S(2)}, u32[]{:S(2)}) collective-permute-start(bf16[672,512]{1,0:T(8,128)(2,1)S(1)} %out_rest.3), channel_id=1, source_target_pairs={{0,1},{1,0},{2,3},{3,2},{4,5},{5,4},{6,7},{7,6},{8,9},{9,8},{10,11... | collective-permute-start | bytes 2064392 | tf_op jit(solution)/shard_map/ppermute | solution.py:32
  (100 shorter events, 50.3 us)
Async XLA Ops:
  1.1 22.3 %collective-permute-start.2 = (bf16[672,512]{1,0:T(8,128)(2,1)}, bf16[672,512]{1,0:T(8,128)(2,1)S(1)}, u32[]{:S(2)}, u32[]{:S(2)}) collective-permute-start(bf16[672,512]{1,0:T(8,128)(2,1)} %bitcast.12), channel_id=1, source_target_pairs={{0,16},{1,17},{2,18},{3,19},{4,20},{5,21},{6,22},{7,23},{8,24},{9,... | collective-permute-start | bytes 2064392 | tf_op jit(solution)/shard_map/ppermute | solution.py:32
  3.9 19.5 %collective-permute-start.3 = (bf16[672,512]{1,0:T(8,128)(2,1)}, bf16[672,512]{1,0:T(8,128)(2,1)S(1)}, u32[]{:S(2)}, u32[]{:S(2)}) collective-permute-start(bf16[672,512]{1,0:T(8,128)(2,1)} %bitcast.13), channel_id=1, source_target_pairs={{0,32},{1,33},{2,34},{3,35},{4,36},{5,37},{6,38},{7,39},{8,40},{9,... | collective-permute-start | bytes 2064392 | tf_op jit(solution)/shard_map/ppermute | solution.py:32
  4.1 19.3 %collective-permute-start.4 = (bf16[672,512]{1,0:T(8,128)(2,1)}, bf16[672,512]{1,0:T(8,128)(2,1)S(1)}, u32[]{:S(2)}, u32[]{:S(2)}) collective-permute-start(bf16[672,512]{1,0:T(8,128)(2,1)} %bitcast.14), channel_id=1, source_target_pairs={{0,96},{1,97},{2,98},{3,99},{4,100},{5,101},{6,102},{7,103},{8,104... | collective-permute-start | bytes 2064392 | tf_op jit(solution)/shard_map/ppermute | solution.py:32
  10.0 13.4 %collective-permute-start.1 = (bf16[672,256]{1,0:T(8,128)(2,1)S(1)}, bf16[672,256]{1,0:T(8,128)(2,1)S(1)}, u32[]{:S(2)}, u32[]{:S(2)}) collective-permute-start(bf16[672,256]{1,0:T(8,128)(2,1)S(1)} %bitcast.22), channel_id=1, source_target_pairs={{0,0},{1,1},{2,2},{3,3},{4,4},{5,5},{6,6},{7,7},{8,8},{9,9},{10,10... | collective-permute-start | bytes 1032200 | tf_op jit(solution)/shard_map/ppermute | solution.py:32
  16.1 14.9 %collective-permute-start.9 = (bf16[672,512]{1,0:T(8,128)(2,1)}, bf16[672,512]{1,0:T(8,128)(2,1)S(1)}, u32[]{:S(2)}, u32[]{:S(2)}) collective-permute-start(bf16[672,512]{1,0:T(8,128)(2,1)} %bitcast.15), channel_id=1, source_target_pairs={{0,1},{1,0},{2,3},{3,2},{4,5},{5,4},{6,7},{7,6},{8,9},{9,8},{10,11... | collective-permute-start | bytes 2064392 | tf_op jit(solution)/shard_map/ppermute | solution.py:32
  23.4 18.8 %collective-permute-start.5 = (bf16[672,512]{1,0:T(8,128)(2,1)S(1)}, bf16[672,512]{1,0:T(8,128)(2,1)S(1)}, u32[]{:S(2)}, u32[]{:S(2)}) collective-permute-start(bf16[672,512]{1,0:T(8,128)(2,1)S(1)} %small.6), channel_id=1, source_target_pairs={{0,0},{1,1},{2,34},{3,35},{4,68},{5,69},{6,102},{7,103},{8,16},{9,... | collective-permute-start | bytes 2064392 | tf_op jit(solution)/shard_map/ppermute | solution.py:32
  28.1 14.1 %collective-permute-start.10 = (bf16[672,512]{1,0:T(8,128)(2,1)S(1)}, bf16[672,512]{1,0:T(8,128)(2,1)S(1)}, u32[]{:S(2)}, u32[]{:S(2)}) collective-permute-start(bf16[672,512]{1,0:T(8,128)(2,1)S(1)} %collective-permute-done.2.refs_1_), channel_id=1, source_target_pairs={{0,1},{1,0},{2,3},{3,2},{4,5},{5,4},{6,7},{7,6},{8,9},{9,8},{10,11... | collective-permute-start | bytes 2064392 | tf_op jit(solution)/shard_map/ppermute | solution.py:32
  42.2 13.6 %collective-permute-start.12 = (bf16[672,512]{1,0:T(8,128)(2,1)S(1)}, bf16[672,512]{1,0:T(8,128)(2,1)S(1)}, u32[]{:S(2)}, u32[]{:S(2)}) collective-permute-start(bf16[672,512]{1,0:T(8,128)(2,1)S(1)} %collective-permute-done.5.refs_0_), channel_id=1, source_target_pairs={{0,8},{1,9},{2,10},{3,11},{4,12},{5,13},{6,14},{7,15},{8,0},{9,1},... | collective-permute-start | bytes 2064392 | tf_op jit(solution)/shard_map/ppermute | solution.py:32
  42.2 15.1 %collective-permute-start.13 = (bf16[672,512]{1,0:T(8,128)(2,1)S(1)}, bf16[672,512]{1,0:T(8,128)(2,1)S(1)}, u32[]{:S(2)}, u32[]{:S(2)}) collective-permute-start(bf16[672,512]{1,0:T(8,128)(2,1)S(1)} %collective-permute-done.5.refs_0_), channel_id=1, source_target_pairs={{0,2},{1,3},{2,4},{3,5},{4,6},{5,7},{6,0},{7,1},{8,10},{9,11},{10,... | collective-permute-start | bytes 2064392 | tf_op jit(solution)/shard_map/ppermute | solution.py:32
  42.4 14.9 %collective-permute-start.14 = (bf16[672,512]{1,0:T(8,128)(2,1)S(1)}, bf16[672,512]{1,0:T(8,128)(2,1)S(1)}, u32[]{:S(2)}, u32[]{:S(2)}) collective-permute-start(bf16[672,512]{1,0:T(8,128)(2,1)S(1)} %collective-permute-done.5.refs_0_), channel_id=1, source_target_pairs={{0,6},{1,7},{2,0},{3,1},{4,2},{5,3},{6,4},{7,5},{8,14},{9,15},{10,... | collective-permute-start | bytes 2064392 | tf_op jit(solution)/shard_map/ppermute | solution.py:32
  45.5 12.9 %collective-permute-start.15 = (bf16[672,512]{1,0:T(8,128)(2,1)S(1)}, bf16[672,512]{1,0:T(8,128)(2,1)S(1)}, u32[]{:S(2)}, u32[]{:S(2)}) collective-permute-start(bf16[672,512]{1,0:T(8,128)(2,1)S(1)} %collective-permute-done.2.refs_1_), channel_id=1, source_target_pairs={{0,32},{1,33},{2,34},{3,35},{4,36},{5,37},{6,38},{7,39},{8,40},{9,... | collective-permute-start | bytes 2064392 | tf_op jit(solution)/shard_map/ppermute | solution.py:32
  46.9 12.8 %collective-permute-start.16 = (bf16[672,512]{1,0:T(8,128)(2,1)S(1)}, bf16[672,512]{1,0:T(8,128)(2,1)S(1)}, u32[]{:S(2)}, u32[]{:S(2)}) collective-permute-start(bf16[672,512]{1,0:T(8,128)(2,1)S(1)} %collective-permute-done.2.refs_1_), channel_id=1, source_target_pairs={{0,96},{1,97},{2,98},{3,99},{4,100},{5,101},{6,102},{7,103},{8,104... | collective-permute-start | bytes 2064392 | tf_op jit(solution)/shard_map/ppermute | solution.py:32
  59.7 19.1 %collective-permute-start.18 = (bf16[672,512]{1,0:T(8,128)(2,1)S(1)}, bf16[672,512]{1,0:T(8,128)(2,1)S(1)}, u32[]{:S(2)}, u32[]{:S(2)}) collective-permute-start(bf16[672,512]{1,0:T(8,128)(2,1)S(1)} %collective-permute-done.13.refs_2_), channel_id=1, source_target_pairs={{0,8},{1,9},{2,10},{3,11},{4,12},{5,13},{6,14},{7,15},{8,0},{9,1},... | collective-permute-start | bytes 2064392 | tf_op jit(solution)/shard_map/ppermute | solution.py:32
  60.7 19.0 %collective-permute-start.19 = (bf16[672,512]{1,0:T(8,128)(2,1)S(1)}, bf16[672,512]{1,0:T(8,128)(2,1)S(1)}, u32[]{:S(2)}, u32[]{:S(2)}) collective-permute-start(bf16[672,512]{1,0:T(8,128)(2,1)S(1)} %collective-permute-done.12.refs_1_), channel_id=1, source_target_pairs={{0,6},{1,7},{2,0},{3,1},{4,2},{5,3},{6,4},{7,5},{8,14},{9,15},{10,... | collective-permute-start | bytes 2064392 | tf_op jit(solution)/shard_map/ppermute | solution.py:32
  63.3 16.9 %collective-permute-start.20 = (bf16[672,512]{1,0:T(8,128)(2,1)S(1)}, bf16[672,512]{1,0:T(8,128)(2,1)S(1)}, u32[]{:S(2)}, u32[]{:S(2)}) collective-permute-start(bf16[672,512]{1,0:T(8,128)(2,1)S(1)} %collective-permute-done.3.refs_2_), channel_id=1, source_target_pairs={{0,32},{1,33},{2,34},{3,35},{4,36},{5,37},{6,38},{7,39},{8,40},{9,... | collective-permute-start | bytes 2064392 | tf_op jit(solution)/shard_map/ppermute | solution.py:32
  63.9 16.4 %collective-permute-start.21 = (bf16[672,512]{1,0:T(8,128)(2,1)S(1)}, bf16[672,512]{1,0:T(8,128)(2,1)S(1)}, u32[]{:S(2)}, u32[]{:S(2)}) collective-permute-start(bf16[672,512]{1,0:T(8,128)(2,1)S(1)} %collective-permute-done.16.refs_5_), channel_id=1, source_target_pairs={{0,96},{1,97},{2,98},{3,99},{4,100},{5,101},{6,102},{7,103},{8,104... | collective-permute-start | bytes 2064392 | tf_op jit(solution)/shard_map/ppermute | solution.py:32
  95.3 21.2 %collective-permute-start.29 = (bf16[256,1024]{1,0:T(8,128)(2,1)S(1)}, bf16[256,1024]{1,0:T(8,128)(2,1)S(1)}, u32[]{:S(2)}, u32[]{:S(2)}) collective-permute-start(bf16[256,1024]{1,0:T(8,128)(2,1)S(1)} %project_rest.2.kv.kv_ref), channel_id=1, source_target_pairs={{0,2},{1,3},{2,4},{3,5},{4,6},{5,7},{6,8},{7,9},{8,10},{9,11},{10,... | collective-permute-start | bytes 1572872 | tf_op jit(solution)/shard_map/ppermute | solution.py:462
  98.1 20.7 %collective-permute-start.31 = (bf16[672,256]{1,0:T(8,128)(2,1)}, bf16[672,256]{1,0:T(8,128)(2,1)}, u32[]{:S(2)}, u32[]{:S(2)}) collective-permute-start(bf16[672,256]{1,0:T(8,128)(2,1)} %collective-permute-done.6.refs_8_), channel_id=1, source_target_pairs={{0,6},{1,7},{2,0},{3,1},{4,2},{5,3},{6,4},{7,5},{8,14},{9,15},{10,... | collective-permute-start | bytes 1032200 | tf_op jit(solution)/shard_map/ppermute | solution.py:32
  118.8 12.9 %collective-permute-start.32 = (bf16[256,1024]{1,0:T(8,128)(2,1)S(1)}, bf16[256,1024]{1,0:T(8,128)(2,1)S(1)}, u32[]{:S(2)}, u32[]{:S(2)}) collective-permute-start(bf16[256,1024]{1,0:T(8,128)(2,1)S(1)} %attend_before.1.refs_0_), channel_id=1, source_target_pairs={{0,16},{1,17},{2,18},{3,19},{4,20},{5,21},{6,22},{7,23},{8,24},{9,... | collective-permute-start | bytes 1572872 | tf_op jit(solution)/shard_map/ppermute | solution.py:32
  118.9 12.8 %collective-permute-start.33 = (bf16[256,1024]{1,0:T(8,128)(2,1)S(1)}, bf16[256,1024]{1,0:T(8,128)(2,1)S(1)}, u32[]{:S(2)}, u32[]{:S(2)}) collective-permute-start(bf16[256,1024]{1,0:T(8,128)(2,1)S(1)} %attend_before.1.refs_0_), channel_id=1, source_target_pairs={{0,32},{1,33},{2,34},{3,35},{4,36},{5,37},{6,38},{7,39},{8,40},{9,... | collective-permute-start | bytes 1572872 | tf_op jit(solution)/shard_map/ppermute | solution.py:32
  118.9 12.7 %collective-permute-start.34 = (bf16[256,1024]{1,0:T(8,128)(2,1)S(1)}, bf16[256,1024]{1,0:T(8,128)(2,1)S(1)}, u32[]{:S(2)}, u32[]{:S(2)}) collective-permute-start(bf16[256,1024]{1,0:T(8,128)(2,1)S(1)} %attend_before.1.refs_0_), channel_id=1, source_target_pairs={{0,96},{1,97},{2,98},{3,99},{4,100},{5,101},{6,102},{7,103},{8,104... | collective-permute-start | bytes 1572872 | tf_op jit(solution)/shard_map/ppermute | solution.py:32
  131.7 14.5 %collective-permute-start.37 = (bf16[256,1024]{1,0:T(8,128)(2,1)S(1)}, bf16[256,1024]{1,0:T(8,128)(2,1)S(1)}, u32[]{:S(2)}, u32[]{:S(2)}) collective-permute-start(bf16[256,1024]{1,0:T(8,128)(2,1)S(1)} %collective-permute-done.33.refs_2_), channel_id=1, source_target_pairs={{0,32},{1,33},{2,34},{3,35},{4,36},{5,37},{6,38},{7,39},{8,40},{9,... | collective-permute-start | bytes 1572872 | tf_op jit(solution)/shard_map/ppermute | solution.py:32
  134.5 13.2 %collective-permute-start.38 = (bf16[256,1024]{1,0:T(8,128)(2,1)S(1)}, bf16[256,1024]{1,0:T(8,128)(2,1)S(1)}, u32[]{:S(2)}, u32[]{:S(2)}) collective-permute-start(bf16[256,1024]{1,0:T(8,128)(2,1)S(1)} %collective-permute-done.33.refs_2_), channel_id=1, source_target_pairs={{0,16},{1,17},{2,18},{3,19},{4,20},{5,21},{6,22},{7,23},{8,24},{9,... | collective-permute-start | bytes 1572872 | tf_op jit(solution)/shard_map/ppermute | solution.py:32
  137.1 13.9 %collective-permute-start.40 = (bf16[672,256]{1,0:T(8,128)(2,1)S(1)}, bf16[672,256]{1,0:T(8,128)(2,1)S(1)}, u32[]{:S(2)}, u32[]{:S(2)}) collective-permute-start(bf16[672,256]{1,0:T(8,128)(2,1)S(1)} %copy-done.5), channel_id=1, source_target_pairs={{0,6},{1,7},{2,0},{3,1},{4,2},{5,3},{6,4},{7,5},{8,14},{9,15},{10,... | collective-permute-start | bytes 1032200 | tf_op jit(solution)/shard_map/ppermute | solution.py:32
  (29 other events, 352.0 us)
